TPU v7x, 32 devices: a whole 2x2x4 slice. The times are simulated.
32 devices in a mesh: seq: 4 (over x, core), fsdp: 8 (over z, y).
Axes of the slice: x: 2, y: 2, z: 4, core: 2. Of those that a mesh axis runs over, the one named last changes fastest.
Arguments:
- inputs: bfloat16 [8, 1024, 512], P('fsdp', 'seq'), may hold values from -6 to 6
- block_ids: int32 [8, 1024], P('fsdp'), may hold values from 0 to 7, never falling along the last dimension, each value on 1 to 256 neighbouring positions
- query_weight: bfloat16 [512, 512], P('fsdp'), may hold values from -0.25 to 0.25
- query_bias: bfloat16 [512], P('fsdp'), may hold values from -1.5 to 1.5
- key_weight: bfloat16 [512, 512], P('fsdp'), may hold values from -0.25 to 0.25
- value_weight: bfloat16 [512, 512], P('fsdp'), may hold values from -0.25 to 0.25
- value_bias: bfloat16 [512], P('fsdp'), may hold values from -1.5 to 1.5
- out_weight: bfloat16 [512, 512], P('fsdp'), may hold values from -6 to 6
- out_bias: bfloat16 [512], P('fsdp'), may hold values from -1.5 to 1.5
- gain_one: bfloat16 [512], P('fsdp'), may hold values from 0.5 to 1.5
- shift_one: bfloat16 [512], P('fsdp'), may hold values from -1.5 to 1.5
- up_weight: bfloat16 [512, 2048], P('fsdp'), may hold values from -0.25 to 0.25
- up_bias: bfloat16 [2048], P('fsdp'), may hold values from -1.5 to 1.5
- down_weight: bfloat16 [2048, 512], P('fsdp'), may hold values from -0.125 to 0.125
- down_bias: bfloat16 [512], P('fsdp'), may hold values from -1.5 to 1.5
- gain_two: bfloat16 [512], P('fsdp'), may hold values from 0.5 to 1.5
- shift_two: bfloat16 [512], P('fsdp'), may hold values from -1.5 to 1.5
- cotangent: bfloat16 [8, 1024, 512], P('fsdp', 'seq'), may hold values from -6 to 6
Outputs:
- output: bfloat16 [8, 1024, 512], P('fsdp', 'seq')
- input_grad: float32 [8, 1024, 512], P('fsdp', 'seq')
- query_weight_grad: float32 [512, 512], P('fsdp')
- query_bias_grad: float32 [512], P('fsdp')
- key_weight_grad: float32 [512, 512], P('fsdp')
- value_weight_grad: float32 [512, 512], P('fsdp')
- value_bias_grad: float32 [512], P('fsdp')
- out_weight_grad: float32 [512, 512], P('fsdp')
- out_bias_grad: float32 [512], P('fsdp')
- gain_one_grad: float32 [512], P('fsdp')
- shift_one_grad: float32 [512], P('fsdp')
- up_weight_grad: float32 [512, 2048], P('fsdp')
- up_bias_grad: float32 [2048], P('fsdp')
- down_weight_grad: float32 [2048, 512], P('fsdp')
- down_bias_grad: float32 [512], P('fsdp')
- gain_two_grad: float32 [512], P('fsdp')
- shift_two_grad: float32 [512], P('fsdp')
Inputs may be any that keep to these rules, and one draw needn't show every extreme that they name: `block_ids`: in each sequence the block numbers never fall along the positions, every number from 0 to 7 occurs, each block spans at most 256 positions, and in every draw some block spans exactly 256.
All inputs are finite; a program needn't handle non-finite values.
Results may differ from a plain program's by a relative error of at most 0.019.
Values may be sent and summed in bfloat16 or wider, within the bound.
No kernel may reach another device: no remote copies, remote signals or barrier semaphores. Data moves between devices by JAX's collectives and lax.ppermute only.
A program may use at most 128 MiB of HBM per device.

v0:
```python
import math

import jax
import jax.numpy as jnp
from jax import lax
from jax.sharding import PartitionSpec as P

H = 8


norm_eps = 1e-05
masked_score = -1e30
gelu_root = 0.7978845608028654
gelu_cubic = 0.044715


def product(left, right):
    return jnp.dot(left, right, preferred_element_type=jnp.float32)


def weight_grad(left, right):
    return lax.dot_general(
        left, right, (((0,), (0,)), ((), ())), preferred_element_type=jnp.float32
    )


def back_product(left, right):
    return lax.dot_general(
        left, right, (((1,), (1,)), ((), ())), preferred_element_type=jnp.float32
    )


def column_sum(entries):
    return jnp.sum(entries, axis=0, dtype=jnp.float32)


def gelu_slope(values):
    inner = gelu_root * (values + gelu_cubic * values * values * values)
    tanh_part = jnp.tanh(inner)
    return 0.5 * (1.0 + tanh_part) + 0.5 * values * (1.0 - tanh_part * tanh_part) * gelu_root * (
        1.0 + 3.0 * gelu_cubic * values * values
    )


def normalize(summed):
    centre = summed - jnp.mean(summed, axis=-1, keepdims=True)
    inverse = lax.rsqrt(jnp.mean(centre * centre, axis=-1, keepdims=True) + norm_eps)
    return (centre * inverse, inverse)


def norm_back(grad_normed, normed, inverse):
    first_mean = jnp.mean(grad_normed, axis=-1, keepdims=True)
    cross_mean = jnp.mean(grad_normed * normed, axis=-1, keepdims=True)
    return inverse * (grad_normed - first_mean - normed * cross_mean)


def head_scores(queries, key_rows, blocks, heads):
    length = queries.shape[0]
    width = queries.shape[1] // heads
    query_heads = queries.reshape(length, heads, width)
    key_heads = key_rows.reshape(length, heads, width)
    scores = jnp.einsum("qhd,khd->hqk", query_heads, key_heads, preferred_element_type=jnp.float32)
    scores = scores * (1.0 / math.sqrt(width))
    allowed = blocks[None, :] <= blocks[:, None]
    return jnp.where(allowed[None, :, :], scores, masked_score)


def attend_forward(queries, key_rows, value_rows, blocks, heads):
    length, columns = queries.shape
    scores = head_scores(queries, key_rows, blocks, heads)
    top = jnp.max(scores, axis=-1, keepdims=True)
    raised = jnp.exp(scores - top)
    total = jnp.sum(raised, axis=-1, keepdims=True)
    probs = (raised / total).astype(jnp.bfloat16)
    value_heads = value_rows.reshape(length, heads, columns // heads)
    mixed = jnp.einsum("hqk,khd->qhd", probs, value_heads, preferred_element_type=jnp.float32)
    return (mixed.reshape(length, columns).astype(jnp.bfloat16), (top + jnp.log(total))[:, :, 0])


def attend_backward(grad_mixed, queries, key_rows, value_rows, blocks, log_total, heads):
    length, columns = queries.shape
    width = columns // heads
    scale = 1.0 / math.sqrt(width)
    scores = head_scores(queries, key_rows, blocks, heads)
    probs = jnp.exp(scores - log_total[:, :, None])
    grad_split = grad_mixed.reshape(length, heads, width)
    query_heads = queries.reshape(length, heads, width)
    key_heads = key_rows.reshape(length, heads, width)
    value_heads = value_rows.reshape(length, heads, width)
    grad_probs = jnp.einsum(
        "qhd,khd->hqk", grad_split, value_heads, preferred_element_type=jnp.float32
    )
    row_terms = jnp.sum(probs * grad_probs, axis=-1, keepdims=True)
    grad_scores = (probs * (grad_probs - row_terms)).astype(jnp.bfloat16)
    grad_values = jnp.einsum(
        "hqk,qhd->khd", probs.astype(jnp.bfloat16), grad_split, preferred_element_type=jnp.float32
    )
    grad_queries = (
        jnp.einsum("hqk,khd->qhd", grad_scores, key_heads, preferred_element_type=jnp.float32)
        * scale
    )
    grad_keys = (
        jnp.einsum("hqk,qhd->khd", grad_scores, query_heads, preferred_element_type=jnp.float32)
        * scale
    )
    return (
        grad_queries.reshape(length, columns).astype(jnp.bfloat16),
        grad_keys.reshape(length, columns).astype(jnp.bfloat16),
        grad_values.reshape(length, columns).astype(jnp.bfloat16),
    )


def body(
    inputs,
    block_ids,
    query_weight,
    query_bias,
    key_weight,
    value_weight,
    value_bias,
    out_weight,
    out_bias,
    gain_one,
    shift_one,
    up_weight,
    up_bias,
    down_weight,
    down_bias,
    gain_two,
    shift_two,
    cotangent,
):
    seq_count, part_len, width_all = inputs.shape
    seq_parts = lax.axis_size("seq")
    heads_here = H // seq_parts
    token_rows = inputs.reshape(-1, width_all)
    full_query, full_key, full_value, full_out, full_query_bias, full_value_bias, full_out_bias = (
        lax.all_gather(query_weight, "fsdp", axis=0, tiled=True),
        lax.all_gather(key_weight, "fsdp", axis=0, tiled=True),
        lax.all_gather(value_weight, "fsdp", axis=0, tiled=True),
        lax.all_gather(out_weight, "fsdp", axis=0, tiled=True),
        lax.all_gather(query_bias, "fsdp", axis=0, tiled=True),
        lax.all_gather(value_bias, "fsdp", axis=0, tiled=True),
        lax.all_gather(out_bias, "fsdp", axis=0, tiled=True),
    )
    queries = (product(token_rows, full_query) + full_query_bias).astype(jnp.bfloat16)
    key_rows = product(token_rows, full_key).astype(jnp.bfloat16)
    value_rows = (product(token_rows, full_value) + full_value_bias).astype(jnp.bfloat16)
    head_query, head_key, head_value = (
        lax.all_to_all(
            queries.reshape(seq_count, part_len, width_all),
            "seq",
            split_axis=2,
            concat_axis=1,
            tiled=True,
        ),
        lax.all_to_all(
            key_rows.reshape(seq_count, part_len, width_all),
            "seq",
            split_axis=2,
            concat_axis=1,
            tiled=True,
        ),
        lax.all_to_all(
            value_rows.reshape(seq_count, part_len, width_all),
            "seq",
            split_axis=2,
            concat_axis=1,
            tiled=True,
        ),
    )

    def forward_one(items):
        return attend_forward(items[0], items[1], items[2], items[3], heads_here)

    mixed_heads, log_total = lax.map(forward_one, (head_query, head_key, head_value, block_ids))
    mixed_rows = lax.all_to_all(
        mixed_heads, "seq", split_axis=1, concat_axis=2, tiled=True
    ).reshape(-1, width_all)
    attention = product(mixed_rows, full_out) + full_out_bias
    normed_one, inverse_one = normalize(token_rows.astype(jnp.float32) + attention)
    (
        full_gain_one,
        full_shift_one,
        full_up,
        full_up_bias,
        full_down,
        full_down_bias,
        full_gain_two,
        full_shift_two,
    ) = (
        lax.all_gather(gain_one, "fsdp", axis=0, tiled=True),
        lax.all_gather(shift_one, "fsdp", axis=0, tiled=True),
        lax.all_gather(up_weight, "fsdp", axis=0, tiled=True),
        lax.all_gather(up_bias, "fsdp", axis=0, tiled=True),
        lax.all_gather(down_weight, "fsdp", axis=0, tiled=True),
        lax.all_gather(down_bias, "fsdp", axis=0, tiled=True),
        lax.all_gather(gain_two, "fsdp", axis=0, tiled=True),
        lax.all_gather(shift_two, "fsdp", axis=0, tiled=True),
    )
    first = (normed_one * full_gain_one + full_shift_one).astype(jnp.bfloat16)
    up_out = product(first, full_up) + full_up_bias
    hidden = jax.nn.gelu(up_out, approximate=True).astype(jnp.bfloat16)
    branch = product(hidden, full_down) + full_down_bias
    normed_two, inverse_two = normalize(first.astype(jnp.float32) + branch)
    result = (normed_two * full_gain_two + full_shift_two).astype(jnp.bfloat16)
    grad_out = cotangent.reshape(-1, width_all).astype(jnp.float32)
    held = lax.optimization_barrier((grad_out, gain_one, up_weight, down_weight, gain_two))
    full_gain_one, full_up, full_down, full_gain_two = (
        lax.all_gather(held[1], "fsdp", axis=0, tiled=True),
        lax.all_gather(held[2], "fsdp", axis=0, tiled=True),
        lax.all_gather(held[3], "fsdp", axis=0, tiled=True),
        lax.all_gather(held[4], "fsdp", axis=0, tiled=True),
    )
    grad_out = held[0]
    gain_two_grad = jnp.sum(grad_out * normed_two, axis=0)
    shift_two_grad = jnp.sum(grad_out, axis=0)
    grad_two = norm_back(grad_out * full_gain_two, normed_two, inverse_two)
    grad_branch = grad_two.astype(jnp.bfloat16)
    down_weight_grad = weight_grad(hidden, grad_branch)
    down_bias_grad = column_sum(grad_branch)
    grad_hidden = back_product(grad_branch, full_down).astype(jnp.bfloat16)
    grad_up = (grad_hidden.astype(jnp.float32) * gelu_slope(up_out)).astype(jnp.bfloat16)
    up_weight_grad = weight_grad(first, grad_up)
    up_bias_grad = column_sum(grad_up)
    grad_first = back_product(grad_up, full_up) + grad_two
    gain_one_grad = jnp.sum(grad_first * normed_one, axis=0)
    shift_one_grad = jnp.sum(grad_first, axis=0)
    grad_one = norm_back(grad_first * full_gain_one, normed_one, inverse_one)
    grad_attention = grad_one.astype(jnp.bfloat16)
    held = lax.optimization_barrier(
        (grad_attention, query_weight, key_weight, value_weight, out_weight)
    )
    full_query, full_key, full_value, full_out = (
        lax.all_gather(held[1], "fsdp", axis=0, tiled=True),
        lax.all_gather(held[2], "fsdp", axis=0, tiled=True),
        lax.all_gather(held[3], "fsdp", axis=0, tiled=True),
        lax.all_gather(held[4], "fsdp", axis=0, tiled=True),
    )
    grad_attention = held[0]
    out_weight_grad = weight_grad(mixed_rows, grad_attention)
    out_bias_grad = column_sum(grad_attention)
    grad_mixed = back_product(grad_attention, full_out).astype(jnp.bfloat16)
    grad_split = lax.all_to_all(
        grad_mixed.reshape(seq_count, part_len, width_all),
        "seq",
        split_axis=2,
        concat_axis=1,
        tiled=True,
    )

    def backward_one(items):
        return attend_backward(
            items[0], items[1], items[2], items[3], items[4], items[5], heads_here
        )

    head_grad_query, head_grad_key, head_grad_value = lax.map(
        backward_one, (grad_split, head_query, head_key, head_value, block_ids, log_total)
    )
    grad_query, grad_key, grad_value = (
        lax.all_to_all(head_grad_query, "seq", split_axis=1, concat_axis=2, tiled=True),
        lax.all_to_all(head_grad_key, "seq", split_axis=1, concat_axis=2, tiled=True),
        lax.all_to_all(head_grad_value, "seq", split_axis=1, concat_axis=2, tiled=True),
    )
    grad_query = grad_query.reshape(-1, width_all)
    grad_key = grad_key.reshape(-1, width_all)
    grad_value = grad_value.reshape(-1, width_all)
    query_weight_grad = weight_grad(token_rows, grad_query)
    query_bias_grad = column_sum(grad_query)
    key_weight_grad = weight_grad(token_rows, grad_key)
    value_weight_grad = weight_grad(token_rows, grad_value)
    value_bias_grad = column_sum(grad_value)
    input_grad = (
        grad_one
        + back_product(grad_query, full_query)
        + back_product(grad_key, full_key)
        + back_product(grad_value, full_value)
    )
    shares = (
        lax.psum_scatter(query_weight_grad, "fsdp", scatter_dimension=0, tiled=True),
        lax.psum_scatter(query_bias_grad, "fsdp", scatter_dimension=0, tiled=True),
        lax.psum_scatter(key_weight_grad, "fsdp", scatter_dimension=0, tiled=True),
        lax.psum_scatter(value_weight_grad, "fsdp", scatter_dimension=0, tiled=True),
        lax.psum_scatter(value_bias_grad, "fsdp", scatter_dimension=0, tiled=True),
        lax.psum_scatter(out_weight_grad, "fsdp", scatter_dimension=0, tiled=True),
        lax.psum_scatter(out_bias_grad, "fsdp", scatter_dimension=0, tiled=True),
        lax.psum_scatter(gain_one_grad, "fsdp", scatter_dimension=0, tiled=True),
        lax.psum_scatter(shift_one_grad, "fsdp", scatter_dimension=0, tiled=True),
        lax.psum_scatter(up_weight_grad, "fsdp", scatter_dimension=0, tiled=True),
        lax.psum_scatter(up_bias_grad, "fsdp", scatter_dimension=0, tiled=True),
        lax.psum_scatter(down_weight_grad, "fsdp", scatter_dimension=0, tiled=True),
        lax.psum_scatter(down_bias_grad, "fsdp", scatter_dimension=0, tiled=True),
        lax.psum_scatter(gain_two_grad, "fsdp", scatter_dimension=0, tiled=True),
        lax.psum_scatter(shift_two_grad, "fsdp", scatter_dimension=0, tiled=True),
    )
    totals = (
        lax.psum(shares[0].astype(jnp.bfloat16), "seq").astype(jnp.float32),
        lax.psum(shares[1].astype(jnp.bfloat16), "seq").astype(jnp.float32),
        lax.psum(shares[2].astype(jnp.bfloat16), "seq").astype(jnp.float32),
        lax.psum(shares[3].astype(jnp.bfloat16), "seq").astype(jnp.float32),
        lax.psum(shares[4].astype(jnp.bfloat16), "seq").astype(jnp.float32),
        lax.psum(shares[5].astype(jnp.bfloat16), "seq").astype(jnp.float32),
        lax.psum(shares[6].astype(jnp.bfloat16), "seq").astype(jnp.float32),
        lax.psum(shares[7].astype(jnp.bfloat16), "seq").astype(jnp.float32),
        lax.psum(shares[8].astype(jnp.bfloat16), "seq").astype(jnp.float32),
        lax.psum(shares[9].astype(jnp.bfloat16), "seq").astype(jnp.float32),
        lax.psum(shares[10].astype(jnp.bfloat16), "seq").astype(jnp.float32),
        lax.psum(shares[11].astype(jnp.bfloat16), "seq").astype(jnp.float32),
        lax.psum(shares[12].astype(jnp.bfloat16), "seq").astype(jnp.float32),
        lax.psum(shares[13].astype(jnp.bfloat16), "seq").astype(jnp.float32),
        lax.psum(shares[14].astype(jnp.bfloat16), "seq").astype(jnp.float32),
    )
    return (
        result.reshape(seq_count, part_len, width_all),
        input_grad.reshape(seq_count, part_len, width_all),
    ) + tuple(totals)


def solution(mesh):
    in_specs = (
        P("fsdp", "seq", None),
        P("fsdp", None),
        P("fsdp", None),
        P("fsdp"),
        P("fsdp", None),
        P("fsdp", None),
        P("fsdp"),
        P("fsdp", None),
        P("fsdp"),
        P("fsdp"),
        P("fsdp"),
        P("fsdp", None),
        P("fsdp"),
        P("fsdp", None),
        P("fsdp"),
        P("fsdp"),
        P("fsdp"),
        P("fsdp", "seq", None),
    )
    out_specs = (
        P("fsdp", "seq", None),
        P("fsdp", "seq", None),
        P("fsdp", None),
        P("fsdp"),
        P("fsdp", None),
        P("fsdp", None),
        P("fsdp"),
        P("fsdp", None),
        P("fsdp"),
        P("fsdp"),
        P("fsdp"),
        P("fsdp", None),
        P("fsdp"),
        P("fsdp", None),
        P("fsdp"),
        P("fsdp"),
        P("fsdp"),
    )
    return jax.shard_map(body, mesh=mesh, in_specs=in_specs, out_specs=out_specs, check_vma=False)
```

profile of v0, /device:TPU:0, one launch (start us, length us, event | category | flops | bytes accessed | tf_op | source)
XLA Modules:
  0.0 789.8 jit_solution(9816883894885869864)
XLA Ops:
  20.3 39.3 %all-reduce.20 = (bf16[512]{0:T(512)(128)(2,1)S(1)}, bf16[512]{0:T(512)(128)(2,1)S(1)}, bf16[512]{0:T(512)(128)(2,1)S(1)}, bf16[512]{0:T(512)(128)(2,1)S(1)}, bf...) all-reduce(bf16[512]{0:T(512)(128)(2,1)S(1)} %dynamic-update-slice,, ...), channel_id=1, replica_groups=mesh['seq'=4,'fsdp'=8] {'fsdp'}, use_global_device_ids=true, to_apply=%add | all-reduce | flops 5120 | bytes 20480
  59.6 32.0 %all_gather.71 = bf16[512,512]{1,0:T(8,128)(2,1)S(1)} all-gather(bf16[64,512]{1,0:T(8,128)(2,1)} %param.20), channel_id=1, replica_groups=mesh['seq'=4,'fsdp'=8] {'fsdp'}, dimensions={0}, use_global_device_ids=true | all-gather | bytes 589824 | tf_op jit(solution)/shard_map/all_gather | solution.py:138
  95.8 3.4 all-to-all-start.1
  99.8 32.5 %all_gather.73 = bf16[512,512]{1,0:T(8,128)(2,1)S(1)} all-gather(bf16[64,512]{1,0:T(8,128)(2,1)S(1)} %copy-done.17), channel_id=1, replica_groups=mesh['seq'=4,'fsdp'=8] {'fsdp'}, dimensions={0}, use_global_device_ids=true | all-gather | bytes 589824 | tf_op jit(solution)/shard_map/all_gather | solution.py:139
  136.1 3.5 all-to-all-start.2
  139.6 32.4 %all_gather.69 = bf16[512,512]{1,0:T(8,128)(2,1)S(1)} all-gather(bf16[64,512]{1,0:T(8,128)(2,1)S(1)} %copy-done.18), channel_id=1, replica_groups=mesh['seq'=4,'fsdp'=8] {'fsdp'}, dimensions={0}, use_global_device_ids=true | all-gather | bytes 589824 | tf_op jit(solution)/shard_map/all_gather | solution.py:140
  175.8 16.3 %all-gather = bf16[8,1,256]{2,1,0:T(2,128)(2,1)S(1)} all-gather(bf16[1,1,256]{2,1,0:T(2,128)(2,1)S(1)} %reshape.304), channel_id=1, replica_groups=mesh['seq'=4,'fsdp'=8] {'fsdp'}, dimensions={0}, use_global_device_ids=true | all-gather | bytes 4608 | tf_op jit(solution)/shard_map/all_gather | solution.py:195
  195.6 3.7 all-to-all-start
  201.4 3.9 all-to-all-done
  216.8 3.4 all-to-all-start.3
  220.3 31.6 %all_gather.74 = bf16[512,512]{1,0:T(8,128)(2,1)S(1)} all-gather(bf16[64,512]{1,0:T(8,128)(2,1)S(1)} %copy-done.15), channel_id=1, replica_groups=mesh['seq'=4,'fsdp'=8] {'fsdp'}, dimensions={0}, use_global_device_ids=true | all-gather | bytes 589824 | tf_op jit(solution)/shard_map/all_gather | solution.py:141
  260.8 5.1 convert_reduce_fusion
  266.0 3.6 multiply_reduce_fusion.2
  272.0 32.2 %all_gather.88 = bf16[512,512]{1,0:T(8,128)(2,1)S(1)} all-gather(bf16[64,512]{1,0:T(8,128)(2,1)S(1)} %copy-done.15), channel_id=1, replica_groups=mesh['seq'=4,'fsdp'=8] {'fsdp'}, dimensions={0}, use_global_device_ids=true | all-gather | bytes 589824 | tf_op jit(solution)/shard_map/all_gather | solution.py:238
  309.5 3.4 all-to-all-start.4
  313.0 5.9 all-to-all-done.4
  323.0 5.5 fusion.27
  330.4 3.8 reduce.9
  336.0 10.3 %all_to_all.120 = bf16[4,2,16384]{2,1,0:T(2,128)(2,1)} all-to-all(bf16[4,2,16384]{2,1,0:T(2,128)(2,1)} %reshape.356), channel_id=1, replica_groups=mesh['seq'=4,'fsdp'=8] {'seq'}, dimensions={0} | all-to-all | bytes 524288 | tf_op jit(solution)/shard_map/all_to_all | solution.py:263
  356.5 5.3 multiply_reduce_fusion
  361.8 4.7 multiply_convert_fusion
  373.5 9.4 %all_to_all.121 = bf16[4,2,16384]{2,1,0:T(2,128)(2,1)S(1)} all-to-all(bf16[4,2,16384]{2,1,0:T(2,128)(2,1)} %reshape.354), channel_id=1, replica_groups=mesh['seq'=4,'fsdp'=8] {'seq'}, dimensions={0} | all-to-all | bytes 524288 | tf_op jit(solution)/shard_map/all_to_all | solution.py:262
  398.8 9.4 %all_to_all.122 = bf16[4,2,16384]{2,1,0:T(2,128)(2,1)S(1)} all-to-all(bf16[4,2,16384]{2,1,0:T(2,128)(2,1)} %reshape.352), channel_id=1, replica_groups=mesh['seq'=4,'fsdp'=8] {'seq'}, dimensions={0} | all-to-all | bytes 524288 | tf_op jit(solution)/shard_map/all_to_all | solution.py:261
  415.9 4.0 fusion.54
  425.5 31.9 %all_gather.89 = bf16[512,512]{1,0:T(8,128)(2,1)S(1)} all-gather(bf16[64,512]{1,0:T(8,128)(2,1)S(1)} %copy-done.16), channel_id=1, replica_groups=mesh['seq'=4,'fsdp'=8] {'fsdp'}, dimensions={0}, use_global_device_ids=true | all-gather | bytes 589824 | tf_op jit(solution)/shard_map/all_gather | solution.py:235
  457.4 31.7 %all_gather.90 = bf16[512,512]{1,0:T(8,128)(2,1)S(1)} all-gather(bf16[64,512]{1,0:T(8,128)(2,1)S(1)} %copy-done.17), channel_id=1, replica_groups=mesh['seq'=4,'fsdp'=8] {'fsdp'}, dimensions={0}, use_global_device_ids=true | all-gather | bytes 589824 | tf_op jit(solution)/shard_map/all_gather | solution.py:236
  489.2 31.8 %all_gather.91 = bf16[512,512]{1,0:T(8,128)(2,1)S(1)} all-gather(bf16[64,512]{1,0:T(8,128)(2,1)S(1)} %copy-done.19), channel_id=1, replica_groups=mesh['seq'=4,'fsdp'=8] {'fsdp'}, dimensions={0}, use_global_device_ids=true | all-gather | bytes 589824 | tf_op jit(solution)/shard_map/all_gather | solution.py:237
  521.2 34.9 %all-reduce.19 = (bf16[512]{0:T(512)(128)(2,1)S(1)}, bf16[512]{0:T(512)(128)(2,1)S(1)}, bf16[512]{0:T(512)(128)(2,1)S(1)}, bf16[512]{0:T(512)(128)(2,1)S(1)}, bf...) all-reduce(f32[512]{0:T(512)S(1)} %bitcast.183, ...), channel_id=3, replica_groups=mesh['seq'=4,'fsdp'=8] {'fsdp'}, use_global_device_ids=true, to_apply=%region_14.15.clone | all-reduce | flops 6144 | bytes 36864
  556.7 5.7 all-reduce.21
  575.2 67.4 %reduce-scatter.15.cloned.1.call-done = f32[64,2048]{1,0:T(8,128)} async-done(((f32[512,2048]{1,0:T(8,128)}), f32[64,2048]{1,0:T(8,128)}) %reduce-scatter.15.cloned.1.call-update) | async-done | bytes 524304 | tf_op jit(solution)/shard_map/reduce_scatter | solution.py:289
  644.4 89.8 %reduce-scatter.17.cloned.1.call-done = f32[256,512]{1,0:T(8,128)} async-done(((f32[2048,512]{1,0:T(8,128)}), f32[256,512]{1,0:T(8,128)}) %reduce-scatter.17.cloned.1.call-update) | async-done | bytes 524304 | tf_op jit(solution)/shard_map/reduce_scatter | solution.py:291
  737.5 37.2 %all-reduce.25.cloned.1.call-done = (bf16[64,512]{0,1:T(8,128)(2,1)}, bf16[64,512]{0,1:T(8,128)(2,1)}, bf16[64,512]{0,1:T(8,128)(2,1)}, bf16[64,512]{1,0:T(8,128...) async-done(((bf16[64,512]{0,1:T(8,128)(2,1)}, bf16[64,512]{0,1:T(8,128)(2,1)}, bf16[64,512]{0,1:T(8,128)(2,1)}, bf16[64,512]{1,0:T(8,128)(2,1)}, ...) | async-done | bytes 786448 | tf_op jit(solution)/shard_map/psum | solution.py:297
  (267 shorter events, 137.5 us)
Async XLA Ops:
  7.2 84.4 %copy-start.2 = (bf16[1,256,512]{2,1,0:T(8,128)(2,1)S(1)}, bf16[1,256,512]{2,1,0:T(8,128)(2,1)}, u32[]{:S(2)}) copy-start(bf16[1,256,512]{2,1,0:T(8,128)(2,1)} %param.18) | copy-start | bytes 786436
  7.2 245.9 %all-gather.6.cloned.1.call-start = ((), (), s32[]{:S(2)}) async-start(), calls=%async_computation.14 | async-start | bytes 2359296 | tf_op jit(solution)/shard_map/all_gather | solution.py:194
  7.9 247.6 %all-gather.8.cloned.1.call-start = ((), (), s32[]{:S(2)}) async-start(), calls=%async_computation.15 | async-start | bytes 2359296 | tf_op jit(solution)/shard_map/all_gather | solution.py:196
  8.7 252.1 %all-gather.10.cloned.1.call-start = ((), (), s32[]{:S(2)}) async-start(), calls=%async_computation.16 | async-start | bytes 2359296 | tf_op jit(solution)/shard_map/all_gather | solution.py:212
  95.8 40.3 %all-to-all-start.1 = ((bf16[4,2,16384]{2,1,0:T(2,128)(2,1)}), bf16[4,2,16384]{2,1,0:T(2,128)(2,1)S(1)}, u32[]{:S(2)}, u32[]{:S(2)}) async-start(bf16[4,2,16384]{2,1,0:T(2,128)(2,1)} %reshape.346), calls=%async_computation.1 | async-start | bytes 524288 | tf_op jit(solution)/shard_map/all_to_all | solution.py:150
  99.2 166.7 %all-gather.12.cloned.1.call-start = ((), (), s32[]{:S(2)}) async-start(), calls=%async_computation.17 | async-start | bytes 2359296 | tf_op jit(solution)/shard_map/all_gather | solution.py:211
  99.8 39.8 %copy-start.18 = (bf16[64,512]{1,0:T(8,128)(2,1)S(1)}, bf16[64,512]{1,0:T(8,128)(2,1)}, u32[]{:S(2)}) copy-start(bf16[64,512]{1,0:T(8,128)(2,1)} %param.23) | copy-start | bytes 196612
  136.1 39.7 %copy-start.38 = (bf16[256]{0:T(256)(128)(2,1)S(1)}, bf16[256]{0:T(256)(128)(2,1)}, u32[]{:S(2)}) copy-start(bf16[256]{0:T(256)(128)(2,1)} %param.30) | copy-start | bytes 1540
  136.1 59.5 %all-to-all-start.2 = ((bf16[4,2,16384]{2,1,0:T(2,128)(2,1)}), bf16[4,2,16384]{2,1,0:T(2,128)(2,1)S(1)}, u32[]{:S(2)}, u32[]{:S(2)}) async-start(bf16[4,2,16384]{2,1,0:T(2,128)(2,1)} %reshape.342), calls=%async_computation.2 | async-start | bytes 524288 | tf_op jit(solution)/shard_map/all_to_all | solution.py:157
  139.6 59.7 %copy-start.27 = (s32[1,1024]{1,0:T(1,128)S(1)}, s32[1,1024]{1,0:T(1,128)}, u32[]{:S(2)}) copy-start(s32[1,1024]{1,0:T(1,128)} %param.19) | copy-start | bytes 12292
  195.6 9.7 %all-to-all-start = ((bf16[4,2,16384]{2,1,0:T(2,128)(2,1)}), bf16[4,2,16384]{2,1,0:T(2,128)(2,1)S(1)}, u32[]{:S(2)}, u32[]{:S(2)}) async-start(bf16[4,2,16384]{2,1,0:T(2,128)(2,1)} %reshape.344), calls=%async_computation | async-start | bytes 524288 | tf_op jit(solution)/shard_map/all_to_all | solution.py:164
  216.8 35.1 %all-to-all-start.3 = ((bf16[4,2,16384]{2,1,0:T(2,128)(2,1)}), bf16[4,2,16384]{2,1,0:T(2,128)(2,1)S(1)}, u32[]{:S(2)}, u32[]{:S(2)}) async-start(bf16[4,2,16384]{2,1,0:T(2,128)(2,1)} %reshape.348), calls=%async_computation.3 | async-start | bytes 524288 | tf_op jit(solution)/shard_map/all_to_all | solution.py:177
  220.3 348.3 %reduce-scatter.13.cloned.1.call-start = ((), (), s32[]{:S(2)}) async-start(), calls=%async_computation.18 | async-start | bytes 1179648 | tf_op jit(solution)/shard_map/reduce_scatter | solution.py:285
  304.2 8.8 %copy-start.25 = (f32[2,1024]{1,0:T(2,128)S(1)}, f32[2,1024]{1,0:T(2,128)}, u32[]{:S(2)}) copy-start(f32[2,1024]{1,0:T(2,128)} %copy-done.24) | copy-start | bytes 24580
  309.5 9.4 %all-to-all-start.4 = ((bf16[4,2,16384]{2,1,0:T(2,128)(2,1)}), bf16[4,2,16384]{2,1,0:T(2,128)(2,1)S(1)}, u32[]{:S(2)}, u32[]{:S(2)}) async-start(bf16[4,2,16384]{2,1,0:T(2,128)(2,1)} %reshape.350), calls=%async_computation.4 | async-start | bytes 524288 | tf_op jit(solution)/shard_map/all_to_all | solution.py:244
  312.9 257.3 %reduce-scatter.23.cloned.1.call-start = ((), (), s32[]{:S(2)}) async-start(), calls=%async_computation.23 | async-start | bytes 1179648
  356.5 215.3 %reduce-scatter.21.cloned.1.call-start = ((), (), s32[]{:S(2)}) async-start(), calls=%async_computation.22 | async-start | bytes 1179648
  390.5 183.0 %reduce-scatter.19.cloned.1.call-start = ((), (), s32[]{:S(2)}) async-start(), calls=%async_computation.21 | async-start | bytes 1179648
  415.8 226.7 %reduce-scatter.15.cloned.1.call-start = ((), (), s32[]{:S(2)}) async-start(), calls=%async_computation.19 | async-start | bytes 4718592 | tf_op jit(solution)/shard_map/reduce_scatter | solution.py:289
  419.9 314.3 %reduce-scatter.17.cloned.1.call-start = ((), (), s32[]{:S(2)}) async-start(), calls=%async_computation.20 | async-start | bytes 4718592 | tf_op jit(solution)/shard_map/reduce_scatter | solution.py:291
  423.9 65.3 %copy-start.19 = (bf16[64,512]{1,0:T(8,128)(2,1)S(1)}, bf16[64,512]{1,0:T(8,128)(2,1)}, u32[]{:S(2)}) copy-start(bf16[64,512]{1,0:T(8,128)(2,1)} %param.23) | copy-start | bytes 196612
  423.9 97.1 %copy-start.4 = (bf16[1,1024,128]{2,1,0:T(8,128)(2,1)S(1)}, bf16[1,1024,128]{2,1,0:T(8,128)(2,1)}, u32[]{:S(2)}) copy-start(bf16[1,1024,128]{2,1,0:T(8,128)(2,1)} %copy.139) | copy-start | bytes 786436
  423.9 97.2 %copy-start.28 = (f32[512]{0:T(512)S(1)}, f32[512]{0:T(512)}, u32[]{:S(2)}) copy-start(f32[512]{0:T(512)} %get-tuple-element.173) | copy-start | bytes 6148
  423.9 97.2 %copy-start.29 = (f32[512]{0:T(512)S(1)}, f32[512]{0:T(512)}, u32[]{:S(2)}) copy-start(f32[512]{0:T(512)} %get-tuple-element.179) | copy-start | bytes 6148
  424.0 97.2 %copy-start.30 = (f32[512]{0:T(512)S(1)}, f32[512]{0:T(512)}, u32[]{:S(2)}) copy-start(f32[512]{0:T(512)} %get-tuple-element.215) | copy-start | bytes 6148
  424.0 97.2 %copy-start.33 = (f32[2048]{0:T(1024)S(1)}, f32[2048]{0:T(1024)}, u32[]{:S(2)}) copy-start(f32[2048]{0:T(1024)} %get-tuple-element.231) | copy-start | bytes 24580
  424.0 97.2 %copy-start.36 = (f32[512]{0:T(512)S(1)}, f32[512]{0:T(512)}, u32[]{:S(2)}) copy-start(f32[512]{0:T(512)} %get-tuple-element.175) | copy-start | bytes 6148
  424.0 97.2 %copy-start.37 = (f32[512]{0:T(512)S(1)}, f32[512]{0:T(512)}, u32[]{:S(2)}) copy-start(f32[512]{0:T(512)} %get-tuple-element.180) | copy-start | bytes 6148
  424.0 143.2 %copy-start.8 = (bf16[1,256,4,128]{1,3,2,0:T(8,128)(2,1)S(1)}, bf16[1,256,4,128]{1,3,2,0:T(8,128)(2,1)}, u32[]{:S(2)}) copy-start(bf16[1,256,4,128]{1,3,2,0:T(8,128)(2,1)} %copy.112) | copy-start | bytes 786436
  424.0 350.7 %all-reduce.25.cloned.1.call-start = ((), (), s32[]{:S(2)}) async-start(), calls=%async_computation.24 | async-start | bytes 1966080 | tf_op jit(solution)/shard_map/psum | solution.py:297
  568.5 167.5 %copy-start.7 = (bf16[1,256,4,128]{1,3,2,0:T(8,128)(2,1)S(1)}, bf16[1,256,4,128]{1,3,2,0:T(8,128)(2,1)}, u32[]{:S(2)}) copy-start(bf16[1,256,4,128]{1,3,2,0:T(8,128)(2,1)} %copy-done.6) | copy-start | bytes 786436
  575.2 161.2 %copy-start.5 = (bf16[1,256,4,128]{1,3,2,0:T(8,128)(2,1)S(1)}, bf16[1,256,4,128]{1,3,2,0:T(8,128)(2,1)}, u32[]{:S(2)}) copy-start(bf16[1,256,4,128]{1,3,2,0:T(8,128)(2,1)} %copy.118) | copy-start | bytes 786436
  (23 other events, 97.6 us)
Sparse Core Ops, SparseCore 0:
  10.2 52.9 all-gather.5
  65.3 54.5 all-gather.7
  122.0 52.8 all-gather.9
  176.9 49.8 all-gather.11
  272.1 62.5 reduce-scatter.12
  356.6 61.0 reduce-scatter.22
  421.1 64.0 reduce-scatter.20
  489.0 62.7 reduce-scatter.18
  555.4 87.1 reduce-scatter.14
  646.5 87.6 reduce-scatter.16
  738.2 36.5 all-reduce.24
where the time goes:
time: 800 us; the launch traced here: 790 us
  blocking collectives  381 us (48%)
  waiting for transfers between devices  206 us (26%)
  local copies, waits for them, and re-layouts  63.7 us (8%)
  other arithmetic  52.1 us (7%)
  matrix products  50.9 us (6%)
  starting transfers between devices  18.1 us (2%)
  between operations  17 us (2%)
    reduce_scatter x1, waiting for transfers between devices, body(): lax.psum_scatter(down_weight_grad, 'fsdp', scatter_dimension=0, tiled=True)  89.8 us
    unnamed x2, blocking collectives  74.2 us
    reduce_scatter x1, waiting for transfers between devices, body(): lax.psum_scatter(up_weight_grad, 'fsdp', scatter_dimension=0, tiled=True)  67.4 us
    unnamed x143, local copies, waits for them, and re-layouts  49.8 us
    psum x1, waiting for transfers between devices, body(): lax.psum(shares[0].astype(jnp.bfloat16), 'seq').astype(jnp.float32)  37.2 us
    all_gather x1, blocking collectives, body(): lax.all_gather(key_weight, 'fsdp', axis=0, tiled=True)  32.5 us
    all_gather x1, blocking collectives, body(): lax.all_gather(value_weight, 'fsdp', axis=0, tiled=True)  32.4 us
    all_gather x1, blocking collectives, body(): lax.all_gather(held[4], 'fsdp', axis=0, tiled=True)  32.2 us
  transfers between devices with their start and end apart: 16, of which 5 were waited for; matrix products, arithmetic and copies ran while one was open for 19% of the time, Pallas kernels for 0%

commit v1 on v0

v1 whole, which is shorter than its diff:
```python
import functools
import math

import jax
import jax.numpy as jnp
from jax import lax
from jax.experimental import pallas as pl
from jax.experimental.pallas import tpu as pltpu
from jax.sharding import PartitionSpec as P

HEADS = 8
BLOCKS = 8
PARTS = 8
NORM_EPS = 1e-05
MASKED = -1e30
GELU_ROOT = 0.7978845608028654
GELU_CUBIC = 0.044715
BF = jnp.bfloat16
F32 = jnp.float32
VMEM = pl.BlockSpec(memory_space=pltpu.VMEM)
SMEM = pl.BlockSpec(memory_space=pltpu.SMEM)


def dot_nn(left, right):
    return lax.dot_general(left, right, (((1,), (0,)), ((), ())), preferred_element_type=F32)


def dot_nt(left, right):
    return lax.dot_general(left, right, (((1,), (1,)), ((), ())), preferred_element_type=F32)


def dot_tn(left, right):
    return lax.dot_general(left, right, (((0,), (0,)), ((), ())), preferred_element_type=F32)


def run(kernel, outs, index, args, scratch=(), flops=0, moved=0):
    outs = [jax.ShapeDtypeStruct(*o) for o in outs]
    return pl.pallas_call(
        kernel,
        out_shape=outs,
        in_specs=[SMEM] + [VMEM] * len(args),
        out_specs=[VMEM] * len(outs),
        scratch_shapes=[pltpu.VMEM(*s) for s in scratch],
        compiler_params=pltpu.CompilerParams(vmem_limit_bytes=56 * 1024 * 1024),
        cost_estimate=pl.CostEstimate(flops=flops, bytes_accessed=moved, transcendentals=0),
    )(index, *args)


def lanes_of(shape):
    return lax.broadcasted_iota(jnp.int32, shape, len(shape) - 1)


def rows_of(shape):
    return lax.broadcasted_iota(jnp.int32, shape, len(shape) - 2)


def half_roll(values):
    return pltpu.roll(values, 64, 1)


def pack_kernel(idx, wq, wk, wv, wo, up, down, vec, head_out, up_out, down_out):
    s, c = idx[1], idx[2]
    columns = pl.ds(pl.multiple_of(s * 128, 128), 128)
    for i, ref in enumerate((wq, wk, wv)):
        head_out[:64, i * 128 : (i + 1) * 128] = ref[:, columns]
    head_out[64:80, :] = vec[...]
    rows = pl.ds(pl.multiple_of(c * 32, 32), 32)
    up_out[:, :512] = wo[rows, :]
    up_out[:, 512:] = up[rows, :]
    down_out[...] = down[pl.ds(pl.multiple_of(c * 128, 128), 128), :]


def stack_kernel(idx, a, b, c, d, out):
    for i, ref in enumerate((a, b, c, d)):
        out[i] = ref[...]


def load_vectors(idx, parts, first, second):
    f = idx[0]
    for k, ref in enumerate(parts):
        rows = ref[64:80, :].astype(F32)
        first[pl.ds(f ^ k, 1), :] = rows[0:1]
        second[pl.ds(f ^ k, 1), :] = rows[1:2]


def load_heads(idx, parts, weight):
    f = idx[0]
    for k, ref in enumerate(parts):
        weight[pl.ds(pl.multiple_of((f ^ k) * 64, 64), 64), :] = ref[:64, :]


def key_limit(i, part, count):
    return min((i + 2) * part, count * part)


def attend_kernel(idx, *refs):
    xs, parts, ids = refs[:4], refs[4:12], refs[12]
    ms = refs[13:17]
    qa, ka, v_out, m_out, rinv_out = refs[17:22]
    weight, first, second, q_s, k_s = refs[22:]
    s = idx[1]
    part = xs[0].shape[0]
    count = ids.shape[1] // part
    total = part * count
    load_heads(idx, parts, weight)
    load_vectors(idx, parts, first, second)
    even, odd = first[pl.ds(2 * s, 1), :][:, :128], first[pl.ds(2 * s + 1, 1), :][:, :128]
    low_row = lanes_of((1, 128)) < 64
    query_bias = jnp.where(low_row, even, half_roll(odd))
    value_bias = jnp.where(low_row, half_roll(even), odd)
    for k, ref in enumerate(xs):
        rows = pl.ds(pl.multiple_of((s ^ k) * part, part), part)
        made = dot_nn(ref[...], weight[...])
        q_s[rows, :] = (made[:, :128] + query_bias).astype(BF)
        k_s[rows, :] = made[:, 128:256].astype(BF)
        v_out[rows, :] = (made[:, 256:] + value_bias).astype(BF)
    blocks = jnp.broadcast_to(ids[...], (128, total))
    row = rows_of((128, total))
    row = jnp.where(row >= 64, row - 64, row)
    own = jnp.where((row < BLOCKS) & (blocks == row), 1.0, 0.0).astype(F32).T
    barred = jnp.where(
        row < BLOCKS,
        jnp.where(blocks > row, MASKED, 0.0),
        jnp.where(row < BLOCKS + 3, 1.0, 0.0),
    ).astype(F32).T
    lane = lanes_of((total, 128))
    low = lane < 64
    queries = q_s[...].astype(F32) * (1.0 / math.sqrt(64))
    keys = k_s[...].astype(F32)
    qa[0] = jnp.where(low, queries, own).astype(BF)
    qa[1] = jnp.where(low, own, queries).astype(BF)
    ka[0] = jnp.where(low, keys, barred).astype(BF)
    ka[1] = jnp.where(low, barred, keys).astype(BF)
    lane = lanes_of((part, 128))
    low = lane < 64
    for i in range(count):
        rows = slice(i * part, (i + 1) * part)
        limit = key_limit(i, part, count)
        mixed = []
        sums = []
        for h in range(2):
            scores = dot_nt(qa[h, rows, :], ka[h, :limit, :])
            top = jnp.max(scores, axis=-1, keepdims=True)
            raised = jnp.exp(scores - top).astype(BF)
            values = v_out[:limit, :]
            mine = lanes_of(values.shape) < 64
            values = jnp.where(mine if h == 0 else ~mine, values, jnp.ones_like(values))
            made = dot_nn(raised, values)
            sums.append(1.0 / half_roll(made))
            mixed.append(made * sums[-1])
            high = top.astype(BF).astype(F32)
            middle = (top - high).astype(BF).astype(F32)
            rest = top - high - middle
            at = lane - (64 if h == 0 else 0) - BLOCKS
            tops = jnp.where(at == 0, -high, jnp.where(at == 1, -middle, jnp.where(at == 2, -rest, 0.0)))
            held = qa[h, rows, :].astype(F32)
            qa[h, rows, :] = jnp.where((at >= 0) & (at < 3), tops, held).astype(BF)
        m_out[rows, :] = jnp.where(low, mixed[0], mixed[1]).astype(BF)
        rinv_out[rows, :] = jnp.where(low, sums[0], sums[1])
    for k, ref in enumerate(ms):
        ref[...] = m_out[pl.ds(pl.multiple_of((s ^ k) * part, part), part), :]


def spread(block, upper, width):
    row = rows_of((PARTS, 128))
    match = (row & 1) == (1 if upper else 0)
    block = jnp.where(match, block, half_roll(block))
    tiled = jnp.concatenate([block] * (width // 128), axis=1)
    keep = lanes_of((PARTS, width)) // 64 == rows_of((PARTS, width))
    return jnp.sum(jnp.where(keep, tiled, 0.0), axis=0, keepdims=True)


def gather_up(vector, upper):
    width = vector.shape[1]
    keep = lanes_of((PARTS, width)) // 64 == rows_of((PARTS, width))
    picked = jnp.where(keep, jnp.broadcast_to(vector, (PARTS, width)), 0.0)
    block = sum(picked[:, j * 128 : (j + 1) * 128] for j in range(width // 128))
    match = (rows_of((PARTS, 128)) & 1) == (1 if upper else 0)
    return jnp.where(match, block, half_roll(block))


def normalize(summed):
    centre = summed - jnp.mean(summed, axis=-1, keepdims=True)
    inverse = lax.rsqrt(jnp.mean(centre * centre, axis=-1, keepdims=True) + NORM_EPS)
    return centre * inverse, inverse


def norm_back(grad, normed, inverse):
    first_mean = jnp.mean(grad, axis=-1, keepdims=True)
    cross_mean = jnp.mean(grad * normed, axis=-1, keepdims=True)
    return inverse * (grad - first_mean - normed * cross_mean)


def gelu(values):
    inner = GELU_ROOT * (values + GELU_CUBIC * values * values * values)
    return 0.5 * values * (1.0 + jnp.tanh(inner))


def gelu_slope(values):
    square = values * values
    inner = GELU_ROOT * (values + GELU_CUBIC * values * square)
    tanh_part = jnp.tanh(inner)
    return 0.5 * (1.0 + tanh_part) + 0.5 * values * (1.0 - tanh_part * tanh_part) * GELU_ROOT * (
        1.0 + 3.0 * GELU_CUBIC * square
    )


def column_sum(values):
    return jnp.sum(values.astype(F32), axis=0, keepdims=True)


def middle_kernel(idx, *refs):
    x0, ms, cot, parts = refs[0], refs[1:5], refs[5], refs[6:14]
    up_parts, down_parts = refs[14:18], refs[18:22]
    refs = refs[22:]
    out, ems, e1_out, u_out, eb_out, y_out, ez_out, m_out, ea_out, vg_out = (
        refs[0],
        refs[1:5],
        *refs[5:13],
    )
    wo, up, down, first, second, z_s, em_s, rows0, rows1 = refs[13:]
    f, s, c = idx[0], idx[1], idx[2]
    for which in range(4):
        half = c if which < 2 else 1 - c
        for j in range(4):
            owner = f ^ (2 * j + (which & 1))
            rows = pl.ds(pl.multiple_of(owner * 64 + half * 32, 32), 32)
            wo[rows, :] = up_parts[which][j, :, :512]
            up[rows, :] = up_parts[which][j, :, 512:]
            rows = pl.ds(pl.multiple_of(owner * 256 + half * 128, 128), 128)
            down[rows, :] = down_parts[which][j]
    load_vectors(idx, parts, first, second)
    v0, v1 = first[...], second[...]
    out_bias = spread(v0[:, 128:256], False, 512)
    gain_one = spread(v0[:, 128:256], True, 512)
    shift_one = spread(v0[:, 256:384], False, 512)
    gain_two = spread(v0[:, 256:384], True, 512)
    shift_two = spread(v1[:, 0:128], False, 512)
    down_bias = spread(v1[:, 0:128], True, 512)
    keep = lanes_of((PARTS, 2048)) // 256 == rows_of((PARTS, 2048))
    tiled = jnp.concatenate([v1[:, 128:384]] * 8, axis=1)
    up_bias = jnp.sum(jnp.where(keep, tiled, 0.0), axis=0, keepdims=True)

    for k, ref in enumerate(ms):
        m_out[:, pl.ds(pl.multiple_of((s ^ k) * 128, 128), 128)] = ref[...]
    h1 = x0[...].astype(F32) + (dot_nn(m_out[...], wo[...]) + out_bias)
    n1, r1 = normalize(h1)
    y = (n1 * gain_one + shift_one).astype(BF)
    y_out[...] = y
    branch = jnp.zeros(h1.shape, F32)
    for j in range(4):
        columns = slice(j * 512, (j + 1) * 512)
        z = dot_nn(y, up[:, columns]) + up_bias[:, columns]
        z_s[:, columns] = z
        u = gelu(z).astype(BF)
        u_out[:, columns] = u
        branch = branch + dot_nn(u, down[columns, :])
    n2, r2 = normalize(y.astype(F32) + (branch + down_bias))
    out[...] = (n2 * gain_two + shift_two).astype(BF)
    grad = cot[...].astype(F32)
    gain_two_grad = column_sum(grad * n2)
    shift_two_grad = column_sum(grad)
    e2 = norm_back(grad * gain_two, n2, r2)
    eb = e2.astype(BF)
    eb_out[...] = eb
    down_bias_grad = column_sum(eb)
    ey = e2
    up_bias_grads = []
    for j in range(4):
        columns = slice(j * 512, (j + 1) * 512)
        eu = dot_nt(eb, down[columns, :]).astype(BF).astype(F32)
        ez = (eu * gelu_slope(z_s[:, columns])).astype(BF)
        ez_out[:, columns] = ez
        up_bias_grads.append(column_sum(ez))
        ey = ey + dot_nt(ez, up[:, columns])
    gain_one_grad = column_sum(ey * n1)
    shift_one_grad = column_sum(ey)
    e1 = norm_back(ey * gain_one, n1, r1)
    e1_out[...] = e1
    ea = e1.astype(BF)
    ea_out[...] = ea
    out_bias_grad = column_sum(ea)
    em_s[...] = dot_nt(ea, wo[...]).astype(BF)
    for k, ref in enumerate(ems):
        ref[...] = em_s[:, pl.ds(pl.multiple_of((s ^ k) * 128, 128), 128)]
    rows0[:, :128] = jnp.zeros((PARTS, 128), F32)
    rows0[:, 128:256] = gather_up(out_bias_grad, False) + gather_up(gain_one_grad, True)
    rows0[:, 256:384] = gather_up(shift_one_grad, False) + gather_up(gain_two_grad, True)
    rows1[:, :128] = gather_up(shift_two_grad, False) + gather_up(down_bias_grad, True)
    up_bias_grad = jnp.concatenate(up_bias_grads, axis=1)
    picked = jnp.where(keep, jnp.broadcast_to(up_bias_grad, (PARTS, 2048)), 0.0)
    rows1[:, 128:384] = sum(picked[:, j * 256 : (j + 1) * 256] for j in range(8))
    at = rows_of((16, 384))
    for k in range(PARTS):
        a, b = rows0[pl.ds(f ^ k, 1), :], rows1[pl.ds(f ^ k, 1), :]
        vg_out[k] = jnp.where(at == 1, a, jnp.where(at == 2, b, 0.0)).astype(BF)


def down_grad_kernel(idx, u, eb, keep, send):
    f, c = idx[0], idx[2]
    right = eb[...]
    for owner in range(PARTS):
        made = dot_tn(u[:, owner * 256 : (owner + 1) * 256], right).astype(BF)
        slot = f ^ owner
        keep[slot] = jnp.where(c == 0, made[:128], made[128:])
        send[slot] = jnp.where(c == 0, made[128:], made[:128])


def up_grad_kernel(idx, y, ez, m, ea, keep, send):
    f, c = idx[0], idx[2]
    for pair in range(PARTS // 2):
        columns = slice(pair * 128, (pair + 1) * 128)
        made_up = dot_tn(y[:, columns], ez[...]).astype(BF)
        made_out = dot_tn(m[:, columns], ea[...]).astype(BF)
        for one in range(2):
            slot = f ^ (2 * pair + one)
            at = one * 64
            for made, lanes in ((made_out, slice(0, 512)), (made_up, slice(512, 2560))):
                upper, lower = made[at : at + 32], made[at + 32 : at + 64]
                keep[slot, :, lanes] = jnp.where(c == 0, upper, lower)
                send[slot, :, lanes] = jnp.where(c == 0, lower, upper)


def attend_back_kernel(idx, *refs):
    ems, qa, ka, v, m, rinv = refs[:4], refs[4], refs[5], refs[6], refs[7], refs[8]
    xs, parts, vg = refs[9:13], refs[13:21], refs[21]
    dx_keep, dx_send, w_keep, w_send = refs[22:26]
    weight, em_s, ema, va, eq_s, e_s, wg_s = refs[26:]
    f, s = idx[0], idx[1]
    part = xs[0].shape[0]
    total = v.shape[0]
    count = total // part
    load_heads(idx, parts, weight)
    for k, ref in enumerate(ems):
        em_s[pl.ds(pl.multiple_of((s ^ k) * part, part), part), :] = ref[...]
    lane = lanes_of((total, 128))
    low = lane < 64
    inverse = rinv[...]
    em = em_s[...].astype(F32)
    scaled = em * inverse
    product = scaled * m[...].astype(F32)
    values = v[...]
    for h in range(2):
        mine = low if h == 0 else ~low
        delta = jnp.sum(jnp.where(mine, product, 0.0), axis=-1, keepdims=True)
        high = delta.astype(BF).astype(F32)
        at = lane - (64 if h == 0 else 0)
        extra = jnp.where(at == 0, -high, jnp.where(at == 1, high - delta, 0.0))
        ema[h] = jnp.where(mine, scaled, extra).astype(BF)
        ones = jnp.where((at == 0) | (at == 1), 1.0, 0.0)
        va[h] = jnp.where(mine, values.astype(F32), ones).astype(BF)
    lane = lanes_of((part, 128))
    low = lane < 64
    eq_s[...] = jnp.zeros_like(eq_s)
    for j in range(count):
        rows = slice(j * part, (j + 1) * part)
        start = max(j - 1, 0) * part
        grad_keys, grad_values = [], []
        for h in range(2):
            raised = jnp.exp(dot_nt(ka[h, rows, :], qa[h, start:, :]))
            slopes = dot_nt(va[h, rows, :], ema[h, start:, :])
            grad = (raised * slopes).astype(BF)
            grad_keys.append(dot_nn(grad, qa[h, start:, :]))
            grad_values.append(dot_nn(raised.astype(BF), ema[h, start:, :]))
            eq_s[h, start:, :] += dot_tn(grad, ka[h, rows, :])
        e_s[rows, 128:256] = jnp.where(low, grad_keys[0], grad_keys[1]).astype(BF)
        e_s[rows, 256:384] = jnp.where(low, grad_values[0], grad_values[1]).astype(BF)
    lane = lanes_of((total, 128))
    e_s[:, :128] = (jnp.where(lane < 64, eq_s[0], eq_s[1]) * (1.0 / math.sqrt(64))).astype(BF)
    wg = jnp.zeros(wg_s.shape, F32)
    for k in range(4):
        grads = e_s[pl.ds(pl.multiple_of((s ^ k) * part, part), part), :]
        wg = wg + dot_tn(xs[k][...], grads)
        made = dot_nt(grads, weight[...]).astype(BF)
        if k & 1:
            dx_send[k >> 1] = made
        else:
            dx_keep[k >> 1] = made
    wg_s[...] = wg
    bias = column_sum(e_s[...])
    at = rows_of((16, 384))
    middle = (lanes_of((16, 384)) >= 128) & (lanes_of((16, 384)) < 256)
    bias = jnp.where((at == 0) & ~middle, jnp.broadcast_to(bias, (16, 384)), 0.0)
    for k in range(PARTS):
        to = w_send if k & 1 else w_keep
        rows = pl.ds(pl.multiple_of((f ^ k) * 64, 64), 64)
        to[k >> 1, :64, :] = wg_s[rows, :].astype(BF)
        to[k >> 1, 64:80, :] = (vg[k].astype(F32) + bias).astype(BF)


def core_sum_kernel(idx, keep, got, stay, go):
    for k in range(PARTS):
        to = go if k & 1 else stay
        to[k >> 1] = (keep[k].astype(F32) + got[k].astype(F32)).astype(BF)


def y_sum_kernel(idx, keep, got, *outs):
    for k in range(PARTS // 2):
        outs[k][...] = (keep[k].astype(F32) + got[k].astype(F32)).astype(BF)


def z_sum_kernel(idx, a, b, c, d, out):
    out[...] = (
        (a[...].astype(F32) + b[...].astype(F32)) + (c[...].astype(F32) + d[...].astype(F32))
    ).astype(BF)


def end_up_kernel(idx, a, b, c, d, out_grad, up_grad):
    core = idx[2]
    own = a[...].astype(F32) + c[...].astype(F32)
    other = b[...].astype(F32) + d[...].astype(F32)
    upper, lower = jnp.where(core == 0, own, other), jnp.where(core == 0, other, own)
    out_grad[:32], out_grad[32:] = upper[:, :512], lower[:, :512]
    up_grad[:32], up_grad[32:] = upper[:, 512:], lower[:, 512:]


def end_down_kernel(idx, a, b, c, d, down_grad):
    core = idx[2]
    own = a[...].astype(F32) + c[...].astype(F32)
    other = b[...].astype(F32) + d[...].astype(F32)
    down_grad[:128] = jnp.where(core == 0, own, other)
    down_grad[128:] = jnp.where(core == 0, other, own)


def end_heads_kernel(idx, a, b, c, d, wq, wk, wv, vec):
    f, s = idx[0], idx[1]
    refs = (a, b, c, d)
    for k, ref in enumerate(refs):
        columns = pl.ds(pl.multiple_of((s ^ k) * 128, 128), 128)
        for i, to in enumerate((wq, wk, wv)):
            to[:, columns] = ref[:64, i * 128 : (i + 1) * 128].astype(F32)
    tails = [ref[64:80, :].astype(F32) for ref in refs]
    summed = (tails[0] + tails[2]) + (tails[1] + tails[3])
    bias = jnp.zeros((1, 384), F32)
    for k in range(4):
        bias = bias + jnp.where((s ^ k) == f // 2, tails[k][0:1], 0.0)
    odd = (f & 1) == 1
    query, value = bias[:, :128], bias[:, 256:384]
    query = jnp.where(odd, half_roll(query), query)
    value = jnp.where(odd, half_roll(value), value)
    vec[0:1, 0:128] = query
    vec[1:2, 0:128] = value
    vec[0:1, 128:384] = summed[1:2, 128:384]
    vec[1:2, 128:256] = summed[2:3, 0:128]
    vec[1:2, 256:384] = jnp.zeros((1, 128), F32)
    vec[2:3, 0:256] = summed[2:3, 128:384]


def dx_core_kernel(idx, keep, got, stay, go):
    stay[...] = keep[0].astype(F32) + got[0].astype(F32)
    go[...] = (keep[1].astype(F32) + got[1].astype(F32)).astype(BF)


def dx_end_kernel(idx, e1, stay, got, out):
    out[...] = e1[...] + stay[...] + got[...].astype(F32)


def swap(values, axis, step):
    size = lax.axis_size(axis)
    return lax.ppermute(values, axis, [(i, i ^ step) for i in range(size)])


def body(
    inputs,
    block_ids,
    query_weight,
    query_bias,
    key_weight,
    value_weight,
    value_bias,
    out_weight,
    out_bias,
    gain_one,
    shift_one,
    up_weight,
    up_bias,
    down_weight,
    down_bias,
    gain_two,
    shift_two,
    cotangent,
):
    owners = lax.axis_size("fsdp")
    direct = owners == PARTS
    seq = lax.axis_index("seq").astype(jnp.int32)
    fsdp = lax.axis_index("fsdp").astype(jnp.int32)
    zero = jnp.zeros((), jnp.int32)
    index = jnp.stack([fsdp, seq, seq & 1]) if direct else jnp.stack([zero, seq, zero])
    _, part, width = inputs.shape
    own = inputs.reshape(part, width)
    across = swap(own, "seq", 2)
    xs = [own, swap(own, "seq", 1), across, swap(across, "seq", 1)]
    total = part * lax.axis_size("seq")
    vectors = (query_bias, value_bias, out_bias, gain_one, shift_one, gain_two, shift_two, down_bias)

    if direct:
        vec = jnp.concatenate((*vectors, up_bias)).reshape(2, 384)
        vec = jnp.pad(vec, ((0, 14), (0, 0)))
        head_part, up_part, down_part = run(
            pack_kernel,
            [((80, 384), BF), ((32, 2560), BF), ((128, 512), BF)],
            index,
            (query_weight, key_weight, value_weight, out_weight, up_weight, down_weight, vec),
        )
        evens = [head_part] + [swap(head_part, "fsdp", k) for k in (2, 4, 6)]
        odds = [swap(e, "fsdp", 1) for e in evens]
        heads = [p for pair in zip(evens, odds) for p in pair]

        def gathered(piece):
            mine = [piece] + [swap(piece, "fsdp", k) for k in (2, 4, 6)]
            (even,) = run(stack_kernel, [((4, *piece.shape), BF)], index, mine)
            odd = swap(even, "fsdp", 1)
            return even, odd, swap(even, "seq", 1), swap(odd, "seq", 1)

        ups, downs = gathered(up_part), gathered(down_part)
    else:

        def full(values):
            return lax.all_gather(values, "fsdp", axis=0, tiled=True)

        vec = jnp.concatenate([full(v).reshape(PARTS, 64) for v in vectors] + [full(up_bias).reshape(PARTS, 256)], axis=1)
        vec = jnp.pad(vec.reshape(PARTS, 2, 384), ((0, 0), (0, 14), (0, 0)))
        cut = [
            lax.dynamic_slice_in_dim(full(w), seq * 128, 128, 1)
            for w in (query_weight, key_weight, value_weight)
        ]
        packed = jnp.concatenate([jnp.concatenate(cut, axis=1).reshape(PARTS, 64, 384), vec], axis=1)
        heads = [packed[k] for k in range(PARTS)]
        wide = jnp.concatenate([full(out_weight), full(up_weight)], axis=1).reshape(4, 2, 64, 2560)
        ups = [wide[:, k & 1, (k >> 1) * 32 : (k >> 1) * 32 + 32] for k in range(4)]
        tall = full(down_weight).reshape(4, 2, 256, 512)
        downs = [tall[:, k & 1, (k >> 1) * 128 : (k >> 1) * 128 + 128] for k in range(4)]

    piece = ((part, 128), BF)
    *ms, qa, ka, v, m_heads, rinv = run(
        attend_kernel,
        [piece] * 4
        + [((2, total, 128), BF)] * 2
        + [((total, 128), BF)] * 2
        + [((total, 128), F32)],
        index,
        (*xs, *heads, block_ids),
        scratch=(
            ((512, 384), BF),
            ((PARTS, 384), F32),
            ((PARTS, 384), F32),
            ((total, 128), BF),
            ((total, 128), BF),
        ),
    )
    ms = [ms[0]] + [swap(ms[k], "seq", k) for k in (1, 2, 3)]
    result, *rest = run(
        middle_kernel,
        [((part, width), BF)]
        + [piece] * 4
        + [
            ((part, width), F32),
            ((part, 2048), BF),
            ((part, width), BF),
            ((part, width), BF),
            ((part, 2048), BF),
            ((part, width), BF),
            ((part, width), BF),
            ((PARTS, 16, 384), BF),
        ],
        index,
        (own, *ms, cotangent.reshape(part, width), *heads, *ups, *downs),
        scratch=(
            ((512, 512), BF),
            ((512, 2048), BF),
            ((2048, 512), BF),
            ((PARTS, 384), F32),
            ((PARTS, 384), F32),
            ((part, 2048), F32),
            ((part, width), BF),
            ((PARTS, 384), F32),
            ((PARTS, 384), F32),
        ),
    )
    ems, (e1, u, eb, y, ez, m, ea, vg) = rest[:4], rest[4:]
    ems = [ems[0]] + [swap(ems[k], "seq", k) for k in (1, 2, 3)]
    down_keep, down_send = run(
        down_grad_kernel, [((PARTS, 128, 512), BF)] * 2, index, (u, eb)
    )
    up_keep, up_send = run(
        up_grad_kernel, [((PARTS, 32, 2560), BF)] * 2, index, (y, ez, m, ea)
    )
    dx_keep, dx_send, w_keep, w_send = run(
        attend_back_kernel,
        [((2, part, width), BF)] * 2 + [((PARTS // 2, 80, 384), BF)] * 2,
        index,
        (*ems, qa, ka, v, m_heads, rinv, *xs, *heads, vg),
        scratch=(
            ((512, 384), BF),
            ((total, 128), BF),
            ((2, total, 128), BF),
            ((2, total, 128), BF),
            ((2, total, 128), F32),
            ((total, 384), BF),
            ((512, 384), F32),
        ),
    )

    stay, go = run(
        dx_core_kernel,
        [((part, width), F32), ((part, width), BF)],
        index,
        (dx_keep, swap(dx_send, "seq", 1)),
    )
    (input_grad,) = run(
        dx_end_kernel, [((part, width), F32)], index, (e1, stay, swap(go, "seq", 2))
    )

    if direct:

        def scattered(stay, go):
            rows, columns = stay.shape[1:]
            got = swap(go, "fsdp", 1)
            outs = run(y_sum_kernel, [((rows, columns), BF)] * 4, index, (stay, got))
            got = [swap(outs[k >> 1], "fsdp", k) for k in (2, 4, 6)]
            (mine,) = run(z_sum_kernel, [((rows, columns), BF)], index, (outs[0], *got))
            return (mine, *(swap(mine, "seq", k) for k in (1, 2, 3)))

        def halved(keep, send):
            rows, columns = keep.shape[1:]
            return run(
                core_sum_kernel,
                [((PARTS // 2, rows, columns), BF)] * 2,
                index,
                (keep, swap(send, "seq", 1)),
            )

        (down_grad,) = run(
            end_down_kernel,
            [((256, 512), F32)],
            index,
            scattered(*halved(down_keep, down_send)),
        )
        out_grad, up_grad = run(
            end_up_kernel,
            [((64, 512), F32), ((64, 2048), F32)],
            index,
            scattered(*halved(up_keep, up_send)),
        )
        wq_grad, wk_grad, wv_grad, vec = run(
            end_heads_kernel,
            [((64, 512), F32)] * 3 + [((3, 384), F32)],
            index,
            scattered(w_keep, w_send),
        )
        flat = vec.reshape(-1)
        small = [flat[k * 64 : (k + 1) * 64] for k in range(16)]
        qb_grad, _, ob_grad, g1_grad, s1_grad, g2_grad, vb_grad, _, s2_grad, db_grad = small[:10]
        ub_grad = flat[768:1024]
    else:

        def summed(values):
            values = lax.psum_scatter(values, "fsdp", scatter_dimension=0, tiled=True)
            return lax.psum(values.astype(BF), "seq").astype(F32)

        both = jnp.concatenate([down_keep, down_send], axis=1).reshape(2048, 512)
        down_grad = summed(both.astype(F32))
        both = jnp.concatenate([up_keep, up_send], axis=1).reshape(512, 2560)
        both = summed(both.astype(F32))
        out_grad, up_grad = both[:, :512], both[:, 512:]
        both = jnp.stack([w_keep, w_send], axis=1).reshape(PARTS, 80, 384).astype(F32)
        made = lax.psum_scatter(both[:, :64].reshape(512, 384), "fsdp", scatter_dimension=0, tiled=True)
        made = lax.all_gather(made.astype(BF), "seq", axis=0).astype(F32)
        wq_grad, wk_grad, wv_grad = (
            jnp.concatenate([made[t, :, i * 128 : (i + 1) * 128] for t in range(4)], axis=1)
            for i in range(3)
        )
        biases = lax.all_gather(lax.psum(both[0, 64], "fsdp").astype(BF), "seq", axis=0).astype(F32)
        cut = width // owners

        def mine(values):
            return lax.dynamic_slice_in_dim(values, fsdp * cut, cut, 0)

        qb_grad, vb_grad = mine(biases[:, :128].reshape(-1)), mine(biases[:, 256:].reshape(-1))
        flat = both[:, 65:67].reshape(PARTS, 768)
        ob_grad, g1_grad, s1_grad, g2_grad, s2_grad, db_grad = (
            summed(flat[:, k * 64 : (k + 1) * 64].reshape(-1)) for k in range(2, 8)
        )
        ub_grad = summed(flat[:, 512:].reshape(-1))

    return (
        result.reshape(inputs.shape),
        input_grad.reshape(inputs.shape),
        wq_grad,
        qb_grad,
        wk_grad,
        wv_grad,
        vb_grad,
        out_grad,
        ob_grad,
        g1_grad,
        s1_grad,
        up_grad,
        ub_grad,
        down_grad,
        db_grad,
        g2_grad,
        s2_grad,
    )


def solution(mesh):
    tokens, matrix, vector = P("fsdp", "seq", None), P("fsdp", None), P("fsdp")
    in_specs = (
        tokens,
        matrix,
        matrix,
        vector,
        matrix,
        matrix,
        vector,
        matrix,
        vector,
        vector,
        vector,
        matrix,
        vector,
        matrix,
        vector,
        vector,
        vector,
        tokens,
    )
    out_specs = (
        tokens,
        tokens,
        matrix,
        vector,
        matrix,
        matrix,
        vector,
        matrix,
        vector,
        vector,
        vector,
        matrix,
        vector,
        matrix,
        vector,
        vector,
        vector,
    )
    return jax.shard_map(body, mesh=mesh, in_specs=in_specs, out_specs=out_specs, check_vma=False)
```

time: 800 us -> 221 us (0.28); the launches traced: 790 us -> 220 us
  blocking collectives: 381 us -> 0 us
  waiting for transfers between devices: 206 us -> 84.2 us
  Pallas kernels: 0 us -> 66.9 us
  other arithmetic: 52.1 us -> 0.62 us
  matrix products: 50.9 us -> 0 us
  local copies, waits for them, and re-layouts: 63.7 us -> 22.8 us
  starting transfers between devices: 18.1 us -> 44.2 us
  between operations: 17 us -> 1.08 us
    all_gather x9 -> x0, blocking collectives: 272 us -> none  [the longest x1 32.5 us: body(): lax.all_gather(key_weight, 'fsdp', axis=0, tiled=True)]
    reduce_scatter x3 -> x0, waiting for transfers between devices: 157 us -> none  [the longest x1 89.8 us: body(): lax.psum_scatter(down_weight_grad, 'fsdp', scatter_dimension=0, tiled=True)]
    ppermute x0 -> x53, waiting for transfers between devices: none -> 84.2 us  [swap(): return lax.ppermute(values, axis, [(i, i ^ step) for i in range(size)])]
    unnamed x2 -> x0, blocking collectives: 74.2 us -> none
    pallas_call x0 -> x21, Pallas kernels: none -> 66.9 us  [run(): pl.pallas_call(kernel, out_shape=outs, in_specs=[SMEM] + [VMEM] * len(arg...]
    dot_general x24 -> x0, matrix products: 50.9 us -> none  [the longest x6 14.1 us: weight_grad(): lax.dot_general(left, right, (((0,), (0,)), ((), ())), preferred_element_...]
    ppermute x0 -> x53, starting transfers between devices: none -> 44.2 us  [swap(): return lax.ppermute(values, axis, [(i, i ^ step) for i in range(size)])]
    psum x1 -> x0, waiting for transfers between devices: 37.2 us -> none  [body(): lax.psum(shares[0].astype(jnp.bfloat16), 'seq').astype(jnp.float32)]
  transfers between devices with their start and end apart: 16 -> 53, of which waited for: 5 -> 21; matrix products, arithmetic and copies ran while one was open for 19% -> 1% of each run, Pallas kernels for 0% -> 21%
where the time goes in v1:
time: 221 us; the launch traced here: 220 us
  waiting for transfers between devices  84.2 us (38%)
  Pallas kernels  66.9 us (30%)
  starting transfers between devices  44.2 us (20%)
  local copies, waits for them, and re-layouts  22.8 us (10%)
    ppermute x53, waiting for transfers between devices, swap(): return lax.ppermute(values, axis, [(i, i ^ step) for i in range(size)])  84.2 us
    pallas_call x21, Pallas kernels, run(): pl.pallas_call(kernel, out_shape=outs, in_specs=[SMEM] + [VMEM] * len(arg...  66.9 us
    ppermute x53, starting transfers between devices, swap(): return lax.ppermute(values, axis, [(i, i ^ step) for i in range(size)])  44.2 us
    unnamed x120, local copies, waits for them, and re-layouts  14.2 us
    concatenate x1, local copies, waits for them, and re-layouts, body(): vec = jnp.concatenate((*vectors, up_bias)).reshape(2, 384)  6.08 us
  transfers between devices with their start and end apart: 53, of which 21 were waited for; matrix products, arithmetic and copies ran while one was open for 1% of the time, Pallas kernels for 21%

profile of v1, /device:TPU:0, one launch (start us, length us, event | category | flops | bytes accessed | tf_op | source)
XLA Modules:
  0.0 219.7 jit_solution(16890598680045366224)
XLA Ops:
  0.7 6.1 %concatenate.3 = bf16[768]{0:T(1024)(128)(2,1)S(1)} concatenate(bf16[64]{0:T(256)(128)(2,1)} %param.21, bf16[64]{0:T(256)(128)(2,1)} %param.24, bf16[64]{0:T(256)(128)(2,1)} %param.26, bf16[64]{0:T(256)(128)(2,1)} %param.27, bf16[64]{0:T(256)(128)(2,1)} %param.28, bf16[64]{0:T(256)(128)(2,1)} %param.33, bf16[64]{0:T(256)(128)(2,1)} %param.34, bf16[64]{0:T(256)(128)(2,1)} %param.32, ...), dimensions={0} | concatenate | bytes 3072 | tf_op jit(solution)/shard_map/concatenate | solution.py:497
  9.9 5.1 %collective-permute-start.15 = (bf16[32,2560]{1,0:T(8,128)(2,1)}, bf16[32,2560]{1,0:T(8,128)(2,1)S(1)}, u32[]{:S(2)}, u32[]{:S(2)}) collective-permute-start(bf16[32,2560]{1,0:T(8,128)(2,1)} %get-tuple-element.79.a), channel_id=1, source_target_pairs={{0,6},{1,7},{2,4},{3,5},{4,2},{5,3},{6,0},{7,1},{8,14},{9,15},{10,... | collective-permute-start | bytes 491528 | tf_op jit(solution)/shard_map/ppermute | solution.py:460
  15.7 4.7 %collective-permute-done.15.d = bf16[32,2560]{1,0:T(8,128)(2,1)S(1)} collective-permute-done((bf16[32,2560]{1,0:T(8,128)(2,1)}, bf16[32,2560]{1,0:T(8,128)(2,1)S(1)}, u32[]{:S(2)}, u32[]{:S(2)}) %collective-permute-start.15) | collective-permute-done | bytes 163872 | tf_op jit(solution)/shard_map/ppermute | solution.py:460
  20.4 8.8 %collective-permute-done.14.c = bf16[32,2560]{1,0:T(8,128)(2,1)S(1)} collective-permute-done((bf16[32,2560]{1,0:T(8,128)(2,1)}, bf16[32,2560]{1,0:T(8,128)(2,1)S(1)}, u32[]{:S(2)}, u32[]{:S(2)}) %collective-permute-start.14) | collective-permute-done | bytes 163872 | tf_op jit(solution)/shard_map/ppermute | solution.py:460
  34.1 2.5 %collective-permute-start.21 = (bf16[128,512]{1,0:T(8,128)(2,1)S(1)}, bf16[128,512]{1,0:T(8,128)(2,1)S(1)}, u32[]{:S(2)}, u32[]{:S(2)}) collective-permute-start(bf16[128,512]{1,0:T(8,128)(2,1)S(1)} %copy-done.40), channel_id=1, source_target_pairs={{0,6},{1,7},{2,4},{3,5},{4,2},{5,3},{6,0},{7,1},{8,14},{9,15},{10,... | collective-permute-start | bytes 393224 | tf_op jit(solution)/shard_map/ppermute | solution.py:460
  38.4 3.8 %collective-permute-done.21.d = bf16[128,512]{1,0:T(8,128)(2,1)S(1)} collective-permute-done((bf16[128,512]{1,0:T(8,128)(2,1)S(1)}, bf16[128,512]{1,0:T(8,128)(2,1)S(1)}, u32[]{:S(2)}, u32[]{:S(2)}) %collective-permute-start.21) | collective-permute-done | bytes 131104 | tf_op jit(solution)/shard_map/ppermute | solution.py:460
  42.3 4.4 %collective-permute-done.20.c = bf16[128,512]{1,0:T(8,128)(2,1)S(1)} collective-permute-done((bf16[128,512]{1,0:T(8,128)(2,1)S(1)}, bf16[128,512]{1,0:T(8,128)(2,1)S(1)}, u32[]{:S(2)}, u32[]{:S(2)}) %collective-permute-start.20) | collective-permute-done | bytes 131104 | tf_op jit(solution)/shard_map/ppermute | solution.py:460
  51.9 3.0 %collective-permute-start.4 = (bf16[80,384]{1,0:T(8,128)(2,1)S(1)}, bf16[80,384]{1,0:T(8,128)(2,1)S(1)}, u32[]{:S(2)}, u32[]{:S(2)}) collective-permute-start(bf16[80,384]{1,0:T(8,128)(2,1)S(1)} %copy-done.10), channel_id=1, source_target_pairs={{0,2},{1,3},{2,0},{3,1},{4,6},{5,7},{6,4},{7,5},{8,10},{9,11},{10,... | collective-permute-start | bytes 184328 | tf_op jit(solution)/shard_map/ppermute | solution.py:460
  54.8 2.1 collective-permute-done.8.refs_10_.refs_12_.refs_19_
  60.9 4.3 %collective-permute-done.3.refs_5_.refs_7_.refs_14_ = bf16[80,384]{1,0:T(8,128)(2,1)S(1)} collective-permute-done((bf16[80,384]{1,0:T(8,128)(2,1)S(1)}, bf16[80,384]{1,0:T(8,128)(2,1)S(1)}, u32[]{:S(2)}, u32[]{:S(2)}) %collective-permute-start.3) | collective-permute-done | bytes 61472 | tf_op jit(solution)/shard_map/ppermute | solution.py:460
  66.2 3.7 %collective-permute-done.7.refs_9_.refs_11_.refs_18_ = bf16[80,384]{1,0:T(8,128)(2,1)S(1)} collective-permute-done((bf16[80,384]{1,0:T(8,128)(2,1)S(1)}, bf16[80,384]{1,0:T(8,128)(2,1)S(1)}, u32[]{:S(2)}, u32[]{:S(2)}) %collective-permute-start.7) | collective-permute-done | bytes 61472 | tf_op jit(solution)/shard_map/ppermute | solution.py:460
  70.0 4.0 %collective-permute-done.5.refs_7_.refs_9_.refs_16_ = bf16[80,384]{1,0:T(8,128)(2,1)S(1)} collective-permute-done((bf16[80,384]{1,0:T(8,128)(2,1)S(1)}, bf16[80,384]{1,0:T(8,128)(2,1)S(1)}, u32[]{:S(2)}, u32[]{:S(2)}) %collective-permute-start.5) | collective-permute-done | bytes 61472 | tf_op jit(solution)/shard_map/ppermute | solution.py:460
  75.2 3.8 %collective-permute-done.2.refs_3_.refs_12_ = bf16[256,512]{1,0:T(8,128)(2,1)S(1)} collective-permute-done((bf16[256,512]{1,0:T(8,128)(2,1)S(1)}, bf16[256,512]{1,0:T(8,128)(2,1)S(1)}, u32[]{:S(2)}, u32[]{:S(2)}) %collective-permute-start.2) | collective-permute-done | bytes 262176 | tf_op jit(solution)/shard_map/ppermute | solution.py:460
  79.8 7.1 %shard_map.306 = (bf16[256,128]{1,0:T(8,128)(2,1)}, bf16[256,128]{1,0:T(8,128)(2,1)}, bf16[256,128]{1,0:T(8,128)(2,1)}, bf16[256,128]{1,0:T(8,128)(2,1)}, bf16[2...) custom-call(s32[3]{0:T(128)} %pad_add_fusion.idx, ...), custom_call_target="tpu_custom_call" | custom-call | tf_op jit(solution)/shard_map/pallas_call | solution.py:38
  89.9 3.0 %collective-permute-done.11.refs_3_ = bf16[256,128]{1,0:T(8,128)(2,1)S(1)} collective-permute-done((bf16[256,128]{1,0:T(8,128)(2,1)}, bf16[256,128]{1,0:T(8,128)(2,1)S(1)}, u32[]{:S(2)}, u32[]{:S(2)}) %collective-permute-start.11) | collective-permute-done | bytes 65568 | tf_op jit(solution)/shard_map/ppermute | solution.py:460
  93.0 4.5 %collective-permute-done.12.refs_4_ = bf16[256,128]{1,0:T(8,128)(2,1)S(1)} collective-permute-done((bf16[256,128]{1,0:T(8,128)(2,1)}, bf16[256,128]{1,0:T(8,128)(2,1)S(1)}, u32[]{:S(2)}, u32[]{:S(2)}) %collective-permute-start.12) | collective-permute-done | bytes 65568 | tf_op jit(solution)/shard_map/ppermute | solution.py:460
  98.9 10.2 %shard_map.309 = (bf16[256,512]{1,0:T(8,128)(2,1)}, bf16[256,128]{1,0:T(8,128)(2,1)}, bf16[256,128]{1,0:T(8,128)(2,1)}, bf16[256,128]{1,0:T(8,128)(2,1)}, bf16[2...) custom-call(s32[3]{0:T(128)} %pad_add_fusion.idx, ...), custom_call_target="tpu_custom_call" | custom-call | tf_op jit(solution)/shard_map/pallas_call | solution.py:38
  109.1 3.9 %shard_map.316 = (bf16[8,32,2560]{2,1,0:T(8,128)(2,1)}, bf16[8,32,2560]{2,1,0:T(8,128)(2,1)}) custom-call(s32[3]{0:T(128)} %pad_add_fusion.idx, bf16[256,512]{1,0:T(8,128)(2,1)} %get-tuple-element.107.y, bf16[256,2048]{1,0:T(8,128)(2,1)} %get-tuple-element.108.ez, bf16[256,512]{1,0:T(8,128)(2,1)} %get-tuple-element.109.m, bf16[256,512]{1,0:T(8,128)(2,1)} %get-tuple-element.110.ea), custom_call_target="tpu_custom_call" | custom-call | tf_op jit(solution)/shard_map/pallas_call | solution.py:38
  113.1 3.4 %shard_map.321 = (bf16[8,128,512]{2,1,0:T(8,128)(2,1)}, bf16[8,128,512]{2,1,0:T(8,128)(2,1)}) custom-call(s32[3]{0:T(128)} %pad_add_fusion.idx, bf16[256,2048]{1,0:T(8,128)(2,1)} %get-tuple-element.121.u, bf16[256,512]{1,0:T(8,128)(2,1)} %get-tuple-element.122.eb), custom_call_target="tpu_custom_call" | custom-call | tf_op jit(solution)/shard_map/pallas_call | solution.py:38
  119.8 3.1 %shard_map.317 = (bf16[4,32,2560]{2,1,0:T(8,128)(2,1)}, bf16[4,32,2560]{2,1,0:T(8,128)(2,1)}) custom-call(s32[3]{0:T(128)} %pad_add_fusion.idx, bf16[8,32,2560]{2,1,0:T(8,128)(2,1)} %get-tuple-element.111.keep, bf16[8,32,2560]{2,1,0:T(8,128)(2,1)} %copy-done.1), custom_call_target="tpu_custom_call" | custom-call | tf_op jit(solution)/shard_map/pallas_call | solution.py:38
  124.1 2.7 %shard_map.322 = (bf16[4,128,512]{2,1,0:T(8,128)(2,1)}, bf16[4,128,512]{2,1,0:T(8,128)(2,1)}) custom-call(s32[3]{0:T(128)} %pad_add_fusion.idx, bf16[8,128,512]{2,1,0:T(8,128)(2,1)} %get-tuple-element.123.keep, bf16[8,128,512]{2,1,0:T(8,128)(2,1)} %copy-done.2), custom_call_target="tpu_custom_call" | custom-call | tf_op jit(solution)/shard_map/pallas_call | solution.py:38
  129.3 9.2 %shard_map.310 = (bf16[2,256,512]{2,1,0:T(8,128)(2,1)}, bf16[2,256,512]{2,1,0:T(8,128)(2,1)}, bf16[4,80,384]{2,1,0:T(8,128)(2,1)}, bf16[4,80,384]{2,1,0:T(8,128)(2,1)}) custom-call(s32[3]{0:T(128)} %pad_add_fusion.idx, bf16[256,128]{1,0:T(8,128)(2,1)} %get-tuple-element.83.refs_0_, bf16[256,128]{1,0:T(8,128)(2,1)} %copy-done.45, ...), custom_call_target="tpu_custom_call" | custom-call | tf_op jit(solution)/shard_map/pallas_call | solution.py:38
  138.9 17.8 %collective-permute-done.30.got = bf16[4,80,384]{2,1,0:T(8,128)(2,1)S(1)} collective-permute-done((bf16[4,80,384]{2,1,0:T(8,128)(2,1)}, bf16[4,80,384]{2,1,0:T(8,128)(2,1)S(1)}, u32[]{:S(2)}, u32[]{:S(2)}) %collective-permute-start.30) | collective-permute-done | bytes 245792 | tf_op jit(solution)/shard_map/ppermute | solution.py:460
  159.2 2.3 %collective-permute-start.32 = (bf16[80,384]{1,0:T(8,128)(2,1)}, bf16[80,384]{1,0:T(8,128)(2,1)S(1)}, u32[]{:S(2)}, u32[]{:S(2)}) collective-permute-start(bf16[80,384]{1,0:T(8,128)(2,1)} %get-tuple-element.101), channel_id=1, source_target_pairs={{0,4},{1,5},{2,6},{3,7},{4,0},{5,1},{6,2},{7,3},{8,12},{9,13},{10,... | collective-permute-start | bytes 184328 | tf_op jit(solution)/shard_map/ppermute | solution.py:460
  161.5 2.4 %collective-permute-done.31.b = bf16[80,384]{1,0:T(8,128)(2,1)S(1)} collective-permute-done((bf16[80,384]{1,0:T(8,128)(2,1)}, bf16[80,384]{1,0:T(8,128)(2,1)S(1)}, u32[]{:S(2)}, u32[]{:S(2)}) %collective-permute-start.31) | collective-permute-done | bytes 61472 | tf_op jit(solution)/shard_map/ppermute | solution.py:460
  166.1 4.0 %collective-permute-done.33.d = bf16[80,384]{1,0:T(8,128)(2,1)S(1)} collective-permute-done((bf16[80,384]{1,0:T(8,128)(2,1)}, bf16[80,384]{1,0:T(8,128)(2,1)S(1)}, u32[]{:S(2)}, u32[]{:S(2)}) %collective-permute-start.33) | collective-permute-done | bytes 61472 | tf_op jit(solution)/shard_map/ppermute | solution.py:460
  180.2 2.1 shard_map.311
  184.6 2.2 shard_map.318
  186.9 2.5 %collective-permute-done.48.c = bf16[128,512]{1,0:T(8,128)(2,1)S(1)} collective-permute-done((bf16[128,512]{1,0:T(8,128)(2,1)}, bf16[128,512]{1,0:T(8,128)(2,1)S(1)}, u32[]{:S(2)}, u32[]{:S(2)}) %collective-permute-start.48) | collective-permute-done | bytes 131104 | tf_op jit(solution)/shard_map/ppermute | solution.py:460
  198.0 5.5 %collective-permute-done.40.c = bf16[32,2560]{1,0:T(8,128)(2,1)S(1)} collective-permute-done((bf16[32,2560]{1,0:T(8,128)(2,1)}, bf16[32,2560]{1,0:T(8,128)(2,1)S(1)}, u32[]{:S(2)}, u32[]{:S(2)}) %collective-permute-start.40) | collective-permute-done | bytes 163872 | tf_op jit(solution)/shard_map/ppermute | solution.py:460
  208.8 2.1 shard_map.312
  214.3 2.1 collective-permute-done.43.c
  (222 shorter events, 72.2 us)
Async XLA Ops:
  9.9 10.5 %collective-permute-start.15 = (bf16[32,2560]{1,0:T(8,128)(2,1)}, bf16[32,2560]{1,0:T(8,128)(2,1)S(1)}, u32[]{:S(2)}, u32[]{:S(2)}) collective-permute-start(bf16[32,2560]{1,0:T(8,128)(2,1)} %get-tuple-element.79.a), channel_id=1, source_target_pairs={{0,6},{1,7},{2,4},{3,5},{4,2},{5,3},{6,0},{7,1},{8,14},{9,15},{10,... | collective-permute-start | bytes 491528 | tf_op jit(solution)/shard_map/ppermute | solution.py:460
  15.1 14.1 %collective-permute-start.14 = (bf16[32,2560]{1,0:T(8,128)(2,1)}, bf16[32,2560]{1,0:T(8,128)(2,1)S(1)}, u32[]{:S(2)}, u32[]{:S(2)}) collective-permute-start(bf16[32,2560]{1,0:T(8,128)(2,1)} %get-tuple-element.79.a), channel_id=1, source_target_pairs={{0,4},{1,5},{2,6},{3,7},{4,0},{5,1},{6,2},{7,3},{8,12},{9,13},{10,... | collective-permute-start | bytes 491528 | tf_op jit(solution)/shard_map/ppermute | solution.py:460
  15.1 14.1 %collective-permute-start.13 = (bf16[32,2560]{1,0:T(8,128)(2,1)}, bf16[32,2560]{1,0:T(8,128)(2,1)S(1)}, u32[]{:S(2)}, u32[]{:S(2)}) collective-permute-start(bf16[32,2560]{1,0:T(8,128)(2,1)} %get-tuple-element.79.a), channel_id=1, source_target_pairs={{0,2},{1,3},{2,0},{3,1},{4,6},{5,7},{6,4},{7,5},{8,10},{9,11},{10,... | collective-permute-start | bytes 491528 | tf_op jit(solution)/shard_map/ppermute | solution.py:460
  32.5 41.6 %collective-permute-start.16 = (bf16[4,32,2560]{2,1,0:T(8,128)(2,1)}, bf16[4,32,2560]{2,1,0:T(8,128)(2,1)S(1)}, u32[]{:S(2)}, u32[]{:S(2)}) collective-permute-start(bf16[4,32,2560]{2,1,0:T(8,128)(2,1)} %shard_map.307.refs_14_), channel_id=1, source_target_pairs={{0,1},{1,0},{2,3},{3,2},{4,5},{5,4},{6,7},{7,6},{8,9},{9,8},{10,11... | collective-permute-start | bytes 1966088 | tf_op jit(solution)/shard_map/ppermute | solution.py:460
  36.5 10.1 %collective-permute-start.20 = (bf16[128,512]{1,0:T(8,128)(2,1)S(1)}, bf16[128,512]{1,0:T(8,128)(2,1)S(1)}, u32[]{:S(2)}, u32[]{:S(2)}) collective-permute-start(bf16[128,512]{1,0:T(8,128)(2,1)S(1)} %copy-done.40), channel_id=1, source_target_pairs={{0,4},{1,5},{2,6},{3,7},{4,0},{5,1},{6,2},{7,3},{8,12},{9,13},{10,... | collective-permute-start | bytes 393224 | tf_op jit(solution)/shard_map/ppermute | solution.py:460
  36.5 10.1 %collective-permute-start.19 = (bf16[128,512]{1,0:T(8,128)(2,1)S(1)}, bf16[128,512]{1,0:T(8,128)(2,1)S(1)}, u32[]{:S(2)}, u32[]{:S(2)}) collective-permute-start(bf16[128,512]{1,0:T(8,128)(2,1)S(1)} %copy-done.40), channel_id=1, source_target_pairs={{0,2},{1,3},{2,0},{3,1},{4,6},{5,7},{6,4},{7,5},{8,10},{9,11},{10,... | collective-permute-start | bytes 393224 | tf_op jit(solution)/shard_map/ppermute | solution.py:460
  49.9 24.8 %collective-permute-start.22 = (bf16[4,128,512]{2,1,0:T(8,128)(2,1)}, bf16[4,128,512]{2,1,0:T(8,128)(2,1)S(1)}, u32[]{:S(2)}, u32[]{:S(2)}) collective-permute-start(bf16[4,128,512]{2,1,0:T(8,128)(2,1)} %shard_map.308.refs_18_), channel_id=1, source_target_pairs={{0,1},{1,0},{2,3},{3,2},{4,5},{5,4},{6,7},{7,6},{8,9},{9,8},{10,11... | collective-permute-start | bytes 1572872 | tf_op jit(solution)/shard_map/ppermute | solution.py:460
  58.5 16.1 %collective-permute-start.1 = (bf16[256,512]{1,0:T(8,128)(2,1)S(1)}, bf16[256,512]{1,0:T(8,128)(2,1)S(1)}, u32[]{:S(2)}, u32[]{:S(2)}) collective-permute-start(bf16[256,512]{1,0:T(8,128)(2,1)S(1)} %bitcast.10), channel_id=1, source_target_pairs={{0,16},{8,24},{16,0},{24,8},{1,17},{9,25},{17,1},{25,9},{2,18},{10... | collective-permute-start | bytes 786440 | tf_op jit(solution)/shard_map/ppermute | solution.py:460
  66.2 9.0 %collective-permute-start = (bf16[256,512]{1,0:T(8,128)(2,1)S(1)}, bf16[256,512]{1,0:T(8,128)(2,1)S(1)}, u32[]{:S(2)}, u32[]{:S(2)}) collective-permute-start(bf16[256,512]{1,0:T(8,128)(2,1)S(1)} %bitcast.11), channel_id=1, source_target_pairs={{0,8},{8,0},{16,24},{24,16},{1,9},{9,1},{17,25},{25,17},{2,10},{10... | collective-permute-start | bytes 786440 | tf_op jit(solution)/shard_map/ppermute | solution.py:460
  74.1 23.4 %collective-permute-start.17 = (bf16[4,32,2560]{2,1,0:T(8,128)(2,1)}, bf16[4,32,2560]{2,1,0:T(8,128)(2,1)S(1)}, u32[]{:S(2)}, u32[]{:S(2)}) collective-permute-start(bf16[4,32,2560]{2,1,0:T(8,128)(2,1)} %shard_map.307.refs_14_), channel_id=1, source_target_pairs={{0,8},{8,0},{16,24},{24,16},{1,9},{9,1},{17,25},{25,17},{2,10},{10... | collective-permute-start | bytes 1966088 | tf_op jit(solution)/shard_map/ppermute | solution.py:460
  74.1 23.4 %collective-permute-start.18 = (bf16[4,32,2560]{2,1,0:T(8,128)(2,1)S(1)}, bf16[4,32,2560]{2,1,0:T(8,128)(2,1)S(1)}, u32[]{:S(2)}, u32[]{:S(2)}) collective-permute-start(bf16[4,32,2560]{2,1,0:T(8,128)(2,1)S(1)} %collective-permute-done.16.refs_15_), channel_id=1, source_target_pairs={{0,8},{8,0},{16,24},{24,16},{1,9},{9,1},{17,25},{25,17},{2,10},{10... | collective-permute-start | bytes 1966088 | tf_op jit(solution)/shard_map/ppermute | solution.py:460
  74.6 22.9 %collective-permute-start.23 = (bf16[4,128,512]{2,1,0:T(8,128)(2,1)}, bf16[4,128,512]{2,1,0:T(8,128)(2,1)S(1)}, u32[]{:S(2)}, u32[]{:S(2)}) collective-permute-start(bf16[4,128,512]{2,1,0:T(8,128)(2,1)} %shard_map.308.refs_18_), channel_id=1, source_target_pairs={{0,8},{8,0},{16,24},{24,16},{1,9},{9,1},{17,25},{25,17},{2,10},{10... | collective-permute-start | bytes 1572872 | tf_op jit(solution)/shard_map/ppermute | solution.py:460
  74.7 22.8 %collective-permute-start.24 = (bf16[4,128,512]{2,1,0:T(8,128)(2,1)S(1)}, bf16[4,128,512]{2,1,0:T(8,128)(2,1)S(1)}, u32[]{:S(2)}, u32[]{:S(2)}) collective-permute-start(bf16[4,128,512]{2,1,0:T(8,128)(2,1)S(1)} %collective-permute-done.22.refs_19_), channel_id=1, source_target_pairs={{0,8},{8,0},{16,24},{24,16},{1,9},{9,1},{17,25},{25,17},{2,10},{10... | collective-permute-start | bytes 1572872 | tf_op jit(solution)/shard_map/ppermute | solution.py:460
  116.9 11.8 %collective-permute-start.25 = (bf16[256,128]{1,0:T(8,128)(2,1)S(1)}, bf16[256,128]{1,0:T(8,128)(2,1)S(1)}, u32[]{:S(2)}, u32[]{:S(2)}) collective-permute-start(bf16[256,128]{1,0:T(8,128)(2,1)S(1)} %copy-done.59), channel_id=1, source_target_pairs={{0,8},{8,0},{16,24},{24,16},{1,9},{9,1},{17,25},{25,17},{2,10},{10... | collective-permute-start | bytes 196616 | tf_op jit(solution)/shard_map/ppermute | solution.py:460
  117.0 11.6 %collective-permute-start.26 = (bf16[256,128]{1,0:T(8,128)(2,1)S(1)}, bf16[256,128]{1,0:T(8,128)(2,1)S(1)}, u32[]{:S(2)}, u32[]{:S(2)}) collective-permute-start(bf16[256,128]{1,0:T(8,128)(2,1)S(1)} %copy-done.58), channel_id=1, source_target_pairs={{0,16},{8,24},{16,0},{24,8},{1,17},{9,25},{17,1},{25,9},{2,18},{10... | collective-permute-start | bytes 196616 | tf_op jit(solution)/shard_map/ppermute | solution.py:460
  117.8 10.9 %collective-permute-start.27 = (bf16[256,128]{1,0:T(8,128)(2,1)S(1)}, bf16[256,128]{1,0:T(8,128)(2,1)S(1)}, u32[]{:S(2)}, u32[]{:S(2)}) collective-permute-start(bf16[256,128]{1,0:T(8,128)(2,1)S(1)} %copy-done.57), channel_id=1, source_target_pairs={{0,24},{8,16},{16,8},{24,0},{1,25},{9,17},{17,9},{25,1},{2,26},{10... | collective-permute-start | bytes 196616 | tf_op jit(solution)/shard_map/ppermute | solution.py:460
  122.9 60.9 %collective-permute-start.38 = (bf16[4,32,2560]{2,1,0:T(8,128)(2,1)}, bf16[4,32,2560]{2,1,0:T(8,128)(2,1)S(1)}, u32[]{:S(2)}, u32[]{:S(2)}) collective-permute-start(bf16[4,32,2560]{2,1,0:T(8,128)(2,1)} %get-tuple-element.114), channel_id=1, source_target_pairs={{0,1},{1,0},{2,3},{3,2},{4,5},{5,4},{6,7},{7,6},{8,9},{9,8},{10,11... | collective-permute-start | bytes 1966088 | tf_op jit(solution)/shard_map/ppermute | solution.py:460
  126.8 46.1 %collective-permute-start.46 = (bf16[4,128,512]{2,1,0:T(8,128)(2,1)}, bf16[4,128,512]{2,1,0:T(8,128)(2,1)S(1)}, u32[]{:S(2)}, u32[]{:S(2)}) collective-permute-start(bf16[4,128,512]{2,1,0:T(8,128)(2,1)} %get-tuple-element.126), channel_id=1, source_target_pairs={{0,1},{1,0},{2,3},{3,2},{4,5},{5,4},{6,7},{7,6},{8,9},{9,8},{10,11... | collective-permute-start | bytes 1572872 | tf_op jit(solution)/shard_map/ppermute | solution.py:460
  138.6 39.7 %collective-permute-start.28 = (bf16[2,256,512]{2,1,0:T(8,128)(2,1)}, bf16[2,256,512]{2,1,0:T(8,128)(2,1)S(1)}, u32[]{:S(2)}, u32[]{:S(2)}) collective-permute-start(bf16[2,256,512]{2,1,0:T(8,128)(2,1)} %get-tuple-element.94), channel_id=1, source_target_pairs={{0,8},{8,0},{16,24},{24,16},{1,9},{9,1},{17,25},{25,17},{2,10},{10... | collective-permute-start | bytes 1572872 | tf_op jit(solution)/shard_map/ppermute | solution.py:460
  138.6 18.1 %collective-permute-start.30 = (bf16[4,80,384]{2,1,0:T(8,128)(2,1)}, bf16[4,80,384]{2,1,0:T(8,128)(2,1)S(1)}, u32[]{:S(2)}, u32[]{:S(2)}) collective-permute-start(bf16[4,80,384]{2,1,0:T(8,128)(2,1)} %get-tuple-element.98), channel_id=1, source_target_pairs={{0,1},{1,0},{2,3},{3,2},{4,5},{5,4},{6,7},{7,6},{8,9},{9,8},{10,11... | collective-permute-start | bytes 737288 | tf_op jit(solution)/shard_map/ppermute | solution.py:460
  172.3 10.0 %collective-permute-start.35 = (bf16[80,384]{1,0:T(8,128)(2,1)}, bf16[80,384]{1,0:T(8,128)(2,1)S(1)}, u32[]{:S(2)}, u32[]{:S(2)}) collective-permute-start(bf16[80,384]{1,0:T(8,128)(2,1)} %shard_map.314.a), channel_id=1, source_target_pairs={{0,16},{8,24},{16,0},{24,8},{1,17},{9,25},{17,1},{25,9},{2,18},{10... | collective-permute-start | bytes 184328 | tf_op jit(solution)/shard_map/ppermute | solution.py:460
  175.8 11.0 %collective-permute-start.47 = (bf16[128,512]{1,0:T(8,128)(2,1)}, bf16[128,512]{1,0:T(8,128)(2,1)S(1)}, u32[]{:S(2)}, u32[]{:S(2)}) collective-permute-start(bf16[128,512]{1,0:T(8,128)(2,1)} %get-tuple-element.128), channel_id=1, source_target_pairs={{0,2},{1,3},{2,0},{3,1},{4,6},{5,7},{6,4},{7,5},{8,10},{9,11},{10,... | collective-permute-start | bytes 393224 | tf_op jit(solution)/shard_map/ppermute | solution.py:460
  176.3 13.1 %collective-permute-start.48 = (bf16[128,512]{1,0:T(8,128)(2,1)}, bf16[128,512]{1,0:T(8,128)(2,1)S(1)}, u32[]{:S(2)}, u32[]{:S(2)}) collective-permute-start(bf16[128,512]{1,0:T(8,128)(2,1)} %get-tuple-element.129), channel_id=1, source_target_pairs={{0,4},{1,5},{2,6},{3,7},{4,0},{5,1},{6,2},{7,3},{8,12},{9,13},{10,... | collective-permute-start | bytes 393224 | tf_op jit(solution)/shard_map/ppermute | solution.py:460
  178.2 11.2 %collective-permute-start.49 = (bf16[128,512]{1,0:T(8,128)(2,1)}, bf16[128,512]{1,0:T(8,128)(2,1)S(1)}, u32[]{:S(2)}, u32[]{:S(2)}) collective-permute-start(bf16[128,512]{1,0:T(8,128)(2,1)} %get-tuple-element.130), channel_id=1, source_target_pairs={{0,6},{1,7},{2,4},{3,5},{4,2},{5,3},{6,0},{7,1},{8,14},{9,15},{10,... | collective-permute-start | bytes 393224 | tf_op jit(solution)/shard_map/ppermute | solution.py:460
  182.3 24.9 %collective-permute-start.29 = (bf16[256,512]{1,0:T(8,128)(2,1)}, bf16[256,512]{1,0:T(8,128)(2,1)S(1)}, u32[]{:S(2)}, u32[]{:S(2)}) collective-permute-start(bf16[256,512]{1,0:T(8,128)(2,1)} %get-tuple-element.96), channel_id=1, source_target_pairs={{0,16},{8,24},{16,0},{24,8},{1,17},{9,25},{17,1},{25,9},{2,18},{10... | collective-permute-start | bytes 786440 | tf_op jit(solution)/shard_map/ppermute | solution.py:460
  183.8 9.4 %collective-permute-start.34 = (bf16[80,384]{1,0:T(8,128)(2,1)S(1)}, bf16[80,384]{1,0:T(8,128)(2,1)S(1)}, u32[]{:S(2)}, u32[]{:S(2)}) collective-permute-start(bf16[80,384]{1,0:T(8,128)(2,1)S(1)} %copy-done.25), channel_id=1, source_target_pairs={{0,8},{8,0},{16,24},{24,16},{1,9},{9,1},{17,25},{25,17},{2,10},{10... | collective-permute-start | bytes 184328 | tf_op jit(solution)/shard_map/ppermute | solution.py:460
  186.8 10.0 %collective-permute-start.39 = (bf16[32,2560]{1,0:T(8,128)(2,1)}, bf16[32,2560]{1,0:T(8,128)(2,1)S(1)}, u32[]{:S(2)}, u32[]{:S(2)}) collective-permute-start(bf16[32,2560]{1,0:T(8,128)(2,1)} %get-tuple-element.116), channel_id=1, source_target_pairs={{0,2},{1,3},{2,0},{3,1},{4,6},{5,7},{6,4},{7,5},{8,10},{9,11},{10,... | collective-permute-start | bytes 491528 | tf_op jit(solution)/shard_map/ppermute | solution.py:460
  189.4 14.1 %collective-permute-start.40 = (bf16[32,2560]{1,0:T(8,128)(2,1)}, bf16[32,2560]{1,0:T(8,128)(2,1)S(1)}, u32[]{:S(2)}, u32[]{:S(2)}) collective-permute-start(bf16[32,2560]{1,0:T(8,128)(2,1)} %get-tuple-element.117), channel_id=1, source_target_pairs={{0,4},{1,5},{2,6},{3,7},{4,0},{5,1},{6,2},{7,3},{8,12},{9,13},{10,... | collective-permute-start | bytes 491528 | tf_op jit(solution)/shard_map/ppermute | solution.py:460
  189.4 14.1 %collective-permute-start.41 = (bf16[32,2560]{1,0:T(8,128)(2,1)}, bf16[32,2560]{1,0:T(8,128)(2,1)S(1)}, u32[]{:S(2)}, u32[]{:S(2)}) collective-permute-start(bf16[32,2560]{1,0:T(8,128)(2,1)} %get-tuple-element.118), channel_id=1, source_target_pairs={{0,6},{1,7},{2,4},{3,5},{4,2},{5,3},{6,0},{7,1},{8,14},{9,15},{10,... | collective-permute-start | bytes 491528 | tf_op jit(solution)/shard_map/ppermute | solution.py:460
  193.2 15.1 %collective-permute-start.52 = (bf16[128,512]{1,0:T(8,128)(2,1)}, bf16[128,512]{1,0:T(8,128)(2,1)S(1)}, u32[]{:S(2)}, u32[]{:S(2)}) collective-permute-start(bf16[128,512]{1,0:T(8,128)(2,1)} %shard_map.324.a), channel_id=1, source_target_pairs={{0,24},{8,16},{16,8},{24,0},{1,25},{9,17},{17,9},{25,1},{2,26},{10... | collective-permute-start | bytes 393224 | tf_op jit(solution)/shard_map/ppermute | solution.py:460
  196.8 14.2 %collective-permute-start.51 = (bf16[128,512]{1,0:T(8,128)(2,1)}, bf16[128,512]{1,0:T(8,128)(2,1)S(1)}, u32[]{:S(2)}, u32[]{:S(2)}) collective-permute-start(bf16[128,512]{1,0:T(8,128)(2,1)} %shard_map.324.a), channel_id=1, source_target_pairs={{0,16},{8,24},{16,0},{24,8},{1,17},{9,25},{17,1},{25,9},{2,18},{10... | collective-permute-start | bytes 393224 | tf_op jit(solution)/shard_map/ppermute | solution.py:460
  207.2 9.2 %collective-permute-start.43 = (bf16[32,2560]{1,0:T(8,128)(2,1)}, bf16[32,2560]{1,0:T(8,128)(2,1)S(1)}, u32[]{:S(2)}, u32[]{:S(2)}) collective-permute-start(bf16[32,2560]{1,0:T(8,128)(2,1)} %shard_map.319.a), channel_id=1, source_target_pairs={{0,16},{8,24},{16,0},{24,8},{1,17},{9,25},{17,1},{25,9},{2,18},{10... | collective-permute-start | bytes 491528 | tf_op jit(solution)/shard_map/ppermute | solution.py:460
  (81 other events, 539.6 us)

commit v2 on v1

v2 whole, which is shorter than its diff:
```python
import functools
import math

import jax
import jax.numpy as jnp
from jax import lax
from jax.experimental import pallas as pl
from jax.experimental.pallas import tpu as pltpu
from jax.sharding import PartitionSpec as P

HEADS = 8
BLOCKS = 8
PARTS = 8
NORM_EPS = 1e-05
MASKED = -1e30
GELU_ROOT = 0.7978845608028654
GELU_CUBIC = 0.044715
BF = jnp.bfloat16
F32 = jnp.float32
COSTS = {}
VMEM = pl.BlockSpec(memory_space=pltpu.VMEM)
SMEM = pl.BlockSpec(memory_space=pltpu.SMEM)


def dot_nn(left, right):
    return lax.dot_general(left, right, (((1,), (0,)), ((), ())), preferred_element_type=F32)


def dot_nt(left, right):
    return lax.dot_general(left, right, (((1,), (1,)), ((), ())), preferred_element_type=F32)


def dot_tn(left, right):
    return lax.dot_general(left, right, (((0,), (0,)), ((), ())), preferred_element_type=F32)


def run(kernel, outs, index, args, scratch=()):
    cost = COSTS.get(kernel, 1.7)
    outs = [jax.ShapeDtypeStruct(*o) for o in outs]
    return pl.pallas_call(
        kernel,
        out_shape=outs,
        in_specs=[SMEM] + [VMEM] * len(args),
        out_specs=[VMEM] * len(outs),
        scratch_shapes=[pltpu.VMEM(*s) for s in scratch],
        compiler_params=pltpu.CompilerParams(vmem_limit_bytes=56 * 1024 * 1024),
        cost_estimate=pl.CostEstimate(flops=int(cost * 1e9), bytes_accessed=int(cost * 3e6), transcendentals=0),
    )(index, *args)


def lanes_of(shape):
    return lax.broadcasted_iota(jnp.int32, shape, len(shape) - 1)


def rows_of(shape):
    return lax.broadcasted_iota(jnp.int32, shape, len(shape) - 2)


def half_roll(values):
    return pltpu.roll(values, 64, 1)


def pack_kernel(idx, wq, wk, wv, wo, up, down, *refs):
    vectors, first_out, down_out, tail = refs[:9], *refs[9:]
    s, c, x = idx[1], idx[2], idx[3]
    columns = pl.ds(pl.multiple_of(s * 128, 128), 128)
    for i, ref in enumerate((wq, wk, wv)):
        first_out[:64, i * 128 : (i + 1) * 128] = ref[:, columns]
    tail[...] = jnp.zeros_like(tail)
    for k, ref in enumerate(vectors[:8]):
        tail[k // 6 : k // 6 + 1, (k % 6) * 64 : (k % 6 + 1) * 64] = ref[...].astype(F32).reshape(1, 64)
    tail[1:2, 128:384] = vectors[8][...].astype(F32).reshape(1, 256)
    first_out[64:80, :384] = tail[...].astype(BF)
    rows = pl.ds(pl.multiple_of(c * 32 + x * 16, 16), 16)
    first_out[:16, 384:] = wo[rows, :]
    for j in range(4):
        first_out[(j + 1) * 16 : (j + 2) * 16, 384:] = up[rows, j * 512 : (j + 1) * 512]
    down_out[...] = down[pl.ds(pl.multiple_of(c * 128, 128), 128), :]


def load_vectors(idx, even, odd, first, second):
    for k in range(PARTS):
        rows = (odd if k & 1 else even)[k >> 1, 64:80, :384].astype(F32)
        first[pl.ds(idx[0] ^ k, 1), :] = rows[0:1]
        second[pl.ds(idx[0] ^ k, 1), :] = rows[1:2]


def load_heads(idx, even, odd, weight):
    for k in range(PARTS):
        rows = pl.ds(pl.multiple_of((idx[0] ^ k) * 64, 64), 64)
        weight[rows, :] = (odd if k & 1 else even)[k >> 1, :64, :384]


def key_limit(i, part, count):
    return min((i + 2) * part, count * part)


def attend_kernel(idx, *refs):
    xs, even, odd, ids = refs[:4], *refs[4:7]
    ms = refs[7:11]
    qa, ka, v_out, m_out, rinv_out = refs[11:16]
    weight, first, second, q_s, k_s = refs[16:]
    s = idx[1]
    part = ms[0].shape[0]
    count = ids.shape[1] // part
    total = part * count
    load_heads(idx, even, odd, weight)
    load_vectors(idx, even, odd, first, second)
    left, right = first[pl.ds(2 * s, 1), :][:, :128], first[pl.ds(2 * s + 1, 1), :][:, :128]
    low_row = lanes_of((1, 128)) < 64
    query_bias = jnp.where(low_row, left, half_roll(right))
    value_bias = jnp.where(low_row, half_roll(left), right)
    for k, ref in enumerate(xs):
        rows = pl.ds(pl.multiple_of((s ^ k) * part, part), part)
        made = dot_nn(ref[-part:, :], weight[...])
        q_s[rows, :] = (made[:, :128] + query_bias).astype(BF)
        k_s[rows, :] = made[:, 128:256].astype(BF)
        v_out[rows, :] = (made[:, 256:] + value_bias).astype(BF)
    blocks = jnp.broadcast_to(ids[...], (128, total))
    row = rows_of((128, total))
    row = jnp.where(row >= 64, row - 64, row)
    own = jnp.where((row < BLOCKS) & (blocks == row), 1.0, 0.0).astype(F32).T
    barred = jnp.where(
        row < BLOCKS,
        jnp.where(blocks > row, MASKED, 0.0),
        jnp.where(row < BLOCKS + 3, 1.0, 0.0),
    ).astype(F32).T
    lane = lanes_of((total, 128))
    low = lane < 64
    queries = q_s[...].astype(F32) * (1.0 / math.sqrt(64))
    keys = k_s[...].astype(F32)
    qa[0] = jnp.where(low, queries, own).astype(BF)
    qa[1] = jnp.where(low, own, queries).astype(BF)
    ka[0] = jnp.where(low, keys, barred).astype(BF)
    ka[1] = jnp.where(low, barred, keys).astype(BF)
    lane = lanes_of((part, 128))
    low = lane < 64
    for i in range(count):
        rows = slice(i * part, (i + 1) * part)
        limit = key_limit(i, part, count)
        mixed = []
        sums = []
        for h in range(2):
            scores = dot_nt(qa[h, rows, :], ka[h, :limit, :])
            top = jnp.max(scores, axis=-1, keepdims=True)
            raised = jnp.exp(scores - top).astype(BF)
            values = v_out[:limit, :]
            mine = lanes_of(values.shape) < 64
            values = jnp.where(mine if h == 0 else ~mine, values, jnp.ones_like(values))
            made = dot_nn(raised, values)
            sums.append(1.0 / half_roll(made))
            mixed.append(made * sums[-1])
            high = top.astype(BF).astype(F32)
            middle = (top - high).astype(BF).astype(F32)
            rest = top - high - middle
            at = lane - (64 if h == 0 else 0) - BLOCKS
            tops = jnp.where(at == 0, -high, jnp.where(at == 1, -middle, jnp.where(at == 2, -rest, 0.0)))
            held = qa[h, rows, :].astype(F32)
            qa[h, rows, :] = jnp.where((at >= 0) & (at < 3), tops, held).astype(BF)
        m_out[rows, :] = jnp.where(low, mixed[0], mixed[1]).astype(BF)
        rinv_out[rows, :] = jnp.where(low, sums[0], sums[1])
    for k, ref in enumerate(ms):
        ref[...] = m_out[pl.ds(pl.multiple_of((s ^ k) * part, part), part), :]


def spread(block, upper, width):
    row = rows_of((PARTS, 128))
    match = (row & 1) == (1 if upper else 0)
    block = jnp.where(match, block, half_roll(block))
    tiled = jnp.concatenate([block] * (width // 128), axis=1)
    keep = lanes_of((PARTS, width)) // 64 == rows_of((PARTS, width))
    return jnp.sum(jnp.where(keep, tiled, 0.0), axis=0, keepdims=True)


def gather_up(vector, upper):
    width = vector.shape[1]
    keep = lanes_of((PARTS, width)) // 64 == rows_of((PARTS, width))
    picked = jnp.where(keep, jnp.broadcast_to(vector, (PARTS, width)), 0.0)
    block = sum(picked[:, j * 128 : (j + 1) * 128] for j in range(width // 128))
    match = (rows_of((PARTS, 128)) & 1) == (1 if upper else 0)
    return jnp.where(match, block, half_roll(block))


def normalize(summed):
    centre = summed - jnp.mean(summed, axis=-1, keepdims=True)
    inverse = lax.rsqrt(jnp.mean(centre * centre, axis=-1, keepdims=True) + NORM_EPS)
    return centre * inverse, inverse


def norm_back(grad, normed, inverse):
    first_mean = jnp.mean(grad, axis=-1, keepdims=True)
    cross_mean = jnp.mean(grad * normed, axis=-1, keepdims=True)
    return inverse * (grad - first_mean - normed * cross_mean)


def gelu(values):
    inner = GELU_ROOT * (values + GELU_CUBIC * values * values * values)
    return 0.5 * values * (1.0 + jnp.tanh(inner))


def gelu_slope(values):
    square = values * values
    inner = GELU_ROOT * (values + GELU_CUBIC * values * square)
    tanh_part = jnp.tanh(inner)
    return 0.5 * (1.0 + tanh_part) + 0.5 * values * (1.0 - tanh_part * tanh_part) * GELU_ROOT * (
        1.0 + 3.0 * GELU_CUBIC * square
    )


def column_sum(values):
    return jnp.sum(values.astype(F32), axis=0, keepdims=True)


def middle_kernel(idx, *refs):
    x0, ms, cot, even, odd = refs[0], refs[1:5], *refs[5:8]
    even_parts, odd_parts, down_parts = refs[8:11], refs[11:14], refs[14:18]
    out, ems, e1_out = refs[18], refs[19:23], refs[23]
    keep1, ship1, keep2, ship2, vg_out = refs[24:29]
    wo, up, down, first, second, z_s, em_s, m_s, u_s, ez_s, ea_s, rows0, rows1 = refs[29:]
    f, s, c, x = idx[0], idx[1], idx[2], idx[3]
    for k in range(4):
        row = (c ^ (k & 1)) * 32 + (x ^ (k >> 1)) * 16
        for slot in range(PARTS):
            j = slot >> 1
            if k == 0:
                block = (odd if slot & 1 else even)[j, :, 384:]
            elif slot & 1:
                block = odd_parts[k - 1][j]
            else:
                block = even_parts[k - 1][j * 80 : (j + 1) * 80, :]
            rows = pl.ds(pl.multiple_of((f ^ slot) * 64 + row, 16), 16)
            wo[rows, :] = block[:16]
            for i in range(4):
                up[rows, i * 512 : (i + 1) * 512] = block[(i + 1) * 16 : (i + 2) * 16]
    for which in range(4):
        half = c if which < 2 else 1 - c
        for j in range(4):
            owner = f ^ (2 * j + (which & 1))
            rows = pl.ds(pl.multiple_of(owner * 256 + half * 128, 128), 128)
            down[rows, :] = down_parts[which][j]
    load_vectors(idx, even, odd, first, second)
    v0, v1 = first[...], second[...]
    out_bias = spread(v0[:, 128:256], False, 512)
    gain_one = spread(v0[:, 128:256], True, 512)
    shift_one = spread(v0[:, 256:384], False, 512)
    gain_two = spread(v0[:, 256:384], True, 512)
    shift_two = spread(v1[:, 0:128], False, 512)
    down_bias = spread(v1[:, 0:128], True, 512)
    keep = lanes_of((PARTS, 2048)) // 256 == rows_of((PARTS, 2048))
    tiled = jnp.concatenate([v1[:, 128:384]] * 8, axis=1)
    up_bias = jnp.sum(jnp.where(keep, tiled, 0.0), axis=0, keepdims=True)

    for k, ref in enumerate(ms):
        m_s[:, pl.ds(pl.multiple_of((s ^ k) * 128, 128), 128)] = ref[...]
    h1 = x0[...].astype(F32) + (dot_nn(m_s[...], wo[...]) + out_bias)
    n1, r1 = normalize(h1)
    y = (n1 * gain_one + shift_one).astype(BF)
    branch = jnp.zeros(h1.shape, F32)
    for j in range(4):
        columns = slice(j * 512, (j + 1) * 512)
        z = dot_nn(y, up[:, columns]) + up_bias[:, columns]
        z_s[:, columns] = z
        u = gelu(z).astype(BF)
        for one in range(2):
            owner = 2 * j + one
            for half in range(2):
                at = one * 256 + half * 128
                u_s[half, :, owner * 128 : (owner + 1) * 128] = u[:, at : at + 128]
        branch = branch + dot_nn(u, down[columns, :])
    n2, r2 = normalize(y.astype(F32) + (branch + down_bias))
    out[...] = (n2 * gain_two + shift_two).astype(BF)
    grad = cot[...].astype(F32)
    gain_two_grad = column_sum(grad * n2)
    shift_two_grad = column_sum(grad)
    e2 = norm_back(grad * gain_two, n2, r2)
    eb = e2.astype(BF)
    down_bias_grad = column_sum(eb)
    ey = e2
    up_bias_grads = []
    for j in range(4):
        columns = slice(j * 512, (j + 1) * 512)
        eu = dot_nt(eb, down[columns, :]).astype(BF).astype(F32)
        ez = (eu * gelu_slope(z_s[:, columns])).astype(BF)
        ez_s[j // 2, :, (j % 2) * 512 : (j % 2 + 1) * 512] = ez
        up_bias_grads.append(column_sum(ez))
        ey = ey + dot_nt(ez, up[:, columns])
    gain_one_grad = column_sum(ey * n1)
    shift_one_grad = column_sum(ey)
    e1 = norm_back(ey * gain_one, n1, r1)
    e1_out[...] = e1
    ea = e1.astype(BF)
    ea_s[0], ea_s[1] = ea[:, :256], ea[:, 256:]
    out_bias_grad = column_sum(ea)
    em_s[...] = dot_nt(ea, wo[...]).astype(BF)
    for k, ref in enumerate(ems):
        ref[...] = em_s[:, pl.ds(pl.multiple_of((s ^ k) * 128, 128), 128)]
    for to1, to2, half in ((keep1, keep2, c), (ship1, ship2, 1 - c)):
        to1[:, :1024] = u_s[half]
        to1[:, 1024:] = eb
        to2[:, :1024] = ez_s[half]
        to2[:, 1024:1280] = ea_s[half]
        to2[:, 1280:1792] = y
        to2[:, 1792:] = m_s[...]
    rows0[:, :128] = jnp.zeros((PARTS, 128), F32)
    rows0[:, 128:256] = gather_up(out_bias_grad, False) + gather_up(gain_one_grad, True)
    rows0[:, 256:384] = gather_up(shift_one_grad, False) + gather_up(gain_two_grad, True)
    rows1[:, :128] = gather_up(shift_two_grad, False) + gather_up(down_bias_grad, True)
    up_bias_grad = jnp.concatenate(up_bias_grads, axis=1)
    picked = jnp.where(keep, jnp.broadcast_to(up_bias_grad, (PARTS, 2048)), 0.0)
    rows1[:, 128:384] = sum(picked[:, j * 256 : (j + 1) * 256] for j in range(8))
    at = rows_of((16, 384))
    for k in range(PARTS):
        a, b = rows0[k : k + 1, :], rows1[k : k + 1, :]
        vg_out[k] = jnp.where(at == 1, a, jnp.where(at == 2, b, 0.0)).astype(BF)


def down_grad_kernel(idx, mine, other, even, odd, send):
    f, x = idx[0], idx[3]
    for pair in range(PARTS // 2):
        columns = slice(pair * 256, (pair + 1) * 256)
        made = dot_tn(mine[:, columns], mine[:, 1024:]) + dot_tn(other[:, columns], other[:, 1024:])
        made = made.astype(BF)
        for one in range(2):
            slot = f ^ (2 * pair + one)
            upper, lower = made[one * 128 : one * 128 + 64], made[one * 128 + 64 : one * 128 + 128]
            kept, gone = jnp.where(x == 0, upper, lower), jnp.where(x == 0, lower, upper)
            odd_slot = slot & 1
            send[odd_slot * 4 + (slot >> 1)] = gone

            @pl.when(odd_slot == 0)
            def _():
                even[slot >> 1] = kept

            @pl.when(odd_slot == 1)
            def _():
                odd[slot >> 1] = kept


def up_grad_kernel(idx, mine, other, even, odd):
    f = idx[0]
    for pair in range(PARTS // 2):
        columns = slice(1280 + pair * 128, 1280 + (pair + 1) * 128)
        made_up = dot_tn(mine[:, columns], mine[:, :1024]) + dot_tn(other[:, columns], other[:, :1024])
        columns = slice(1792 + pair * 128, 1792 + (pair + 1) * 128)
        made_out = dot_tn(mine[:, columns], mine[:, 1024:1280]) + dot_tn(
            other[:, columns], other[:, 1024:1280]
        )
        for one in range(2):
            slot = f ^ (2 * pair + one)
            for parity, to in ((0, even), (1, odd)):

                @pl.when((slot & 1) == parity)
                def _():
                    to[slot >> 1, :, :1024] = made_up[one * 64 : (one + 1) * 64].astype(BF)
                    to[slot >> 1, :, 1024:] = made_out[one * 64 : (one + 1) * 64].astype(BF)


def attend_back_kernel(idx, *refs):
    ems, qa, ka, v, m, rinv = refs[:4], refs[4], refs[5], refs[6], refs[7], refs[8]
    xs, even, odd, vg = refs[9:13], *refs[13:16]
    dx_keep, dx_send, w_out = refs[16:19]
    weight, em_s, ema, va, eq_s, e_s = refs[19:]
    f, s = idx[0], idx[1]
    part = ems[0].shape[0]
    total = v.shape[0]
    count = total // part
    load_heads(idx, even, odd, weight)
    for k, ref in enumerate(ems):
        em_s[pl.ds(pl.multiple_of((s ^ k) * part, part), part), :] = ref[...]
    lane = lanes_of((total, 128))
    low = lane < 64
    inverse = rinv[...]
    em = em_s[...].astype(F32)
    scaled = em * inverse
    product = scaled * m[...].astype(F32)
    values = v[...]
    for h in range(2):
        mine = low if h == 0 else ~low
        delta = jnp.sum(jnp.where(mine, product, 0.0), axis=-1, keepdims=True)
        high = delta.astype(BF).astype(F32)
        at = lane - (64 if h == 0 else 0)
        extra = jnp.where(at == 0, -high, jnp.where(at == 1, high - delta, 0.0))
        ema[h] = jnp.where(mine, scaled, extra).astype(BF)
        ones = jnp.where((at == 0) | (at == 1), 1.0, 0.0)
        va[h] = jnp.where(mine, values.astype(F32), ones).astype(BF)
    lane = lanes_of((part, 128))
    low = lane < 64
    eq_s[...] = jnp.zeros_like(eq_s)
    for j in range(count):
        rows = slice(j * part, (j + 1) * part)
        start = max(j - 1, 0) * part
        grad_keys, grad_values = [], []
        for h in range(2):
            raised = jnp.exp(dot_nt(ka[h, rows, :], qa[h, start:, :]))
            slopes = dot_nt(va[h, rows, :], ema[h, start:, :])
            grad = (raised * slopes).astype(BF)
            grad_keys.append(dot_nn(grad, qa[h, start:, :]))
            grad_values.append(dot_nn(raised.astype(BF), ema[h, start:, :]))
            eq_s[h, start:, :] += dot_tn(grad, ka[h, rows, :])
        e_s[rows, 128:256] = jnp.where(low, grad_keys[0], grad_keys[1]).astype(BF)
        e_s[rows, 256:384] = jnp.where(low, grad_values[0], grad_values[1]).astype(BF)
    lane = lanes_of((total, 128))
    e_s[:, :128] = (jnp.where(lane < 64, eq_s[0], eq_s[1]) * (1.0 / math.sqrt(64))).astype(BF)
    wg = jnp.zeros(weight.shape, F32)
    for k in range(4):
        grads = e_s[pl.ds(pl.multiple_of((s ^ k) * part, part), part), :]
        wg = wg + dot_tn(xs[k][-part:, :], grads)
        made = dot_nt(grads, weight[...]).astype(BF)
        if k & 1:
            dx_send[k >> 1] = made
        else:
            dx_keep[k >> 1] = made
    bias = column_sum(e_s[...])
    at = rows_of((16, 384))
    middle = (lanes_of((16, 384)) >= 128) & (lanes_of((16, 384)) < 256)
    bias = jnp.where((at == 0) & ~middle, jnp.broadcast_to(bias, (16, 384)), 0.0)
    for k in range(PARTS):
        w_out[k, :64, :] = wg[k * 64 : (k + 1) * 64].astype(BF)
        w_out[k, 64:80, :] = (vg[k].astype(F32) + bias).astype(BF)


def plus(*terms):
    return functools.reduce(jnp.add, [t.astype(F32) for t in terms]).astype(BF)


def end_wide_kernel(idx, a, b, c, d, out_grad, up_grad, down_grad):
    core, x = idx[2], idx[3]
    wide = slice(0, 1280)
    own = a[:, wide].astype(F32) + c[:, wide].astype(F32)
    other = b[:, wide].astype(F32) + d[:, wide].astype(F32)
    left, right = jnp.where(core == 0, own, other), jnp.where(core == 0, other, own)
    up_grad[:, :1024], up_grad[:, 1024:] = left[:, :1024], right[:, :1024]
    out_grad[:, :256], out_grad[:, 256:] = left[:, 1024:], right[:, 1024:]
    for k, ref in enumerate((a, b, c, d)):
        at = (core ^ (k & 1)) * 128 + (x ^ (k >> 1)) * 64
        down_grad[pl.ds(pl.multiple_of(at, 64), 64), :] = ref[:, 1280:].astype(F32)


def end_heads_kernel(idx, a, b, c, d, wq, wk, wv, qb, vb, ob, g1, s1, g2, s2, db, ub):
    f, s = idx[0], idx[1]
    refs = (a, b, c, d)
    for k, ref in enumerate(refs):
        columns = pl.ds(pl.multiple_of((s ^ k) * 128, 128), 128)
        for i, to in enumerate((wq, wk, wv)):
            to[:, columns] = ref[:64, i * 128 : (i + 1) * 128].astype(F32)
    tails = [ref[64:80, :].astype(F32) for ref in refs]
    summed = (tails[0] + tails[2]) + (tails[1] + tails[3])
    bias = jnp.zeros((1, 384), F32)
    for k in range(4):
        bias = bias + jnp.where((s ^ k) == f // 2, tails[k][0:1], 0.0)
    odd = (f & 1) == 1
    for to, row in ((qb, bias[:, :128]), (vb, bias[:, 256:384])):
        to[...] = jnp.where(odd, half_roll(row), row)[:, :64].reshape(64)
    for k, to in enumerate((ob, g1, s1, g2, s2, db)):
        row, at = (summed[1:2], k + 2) if k < 4 else (summed[2:3], k - 4)
        to[...] = row[:, at * 64 : (at + 1) * 64].reshape(64)
    ub[...] = summed[2:3, 128:384].reshape(256)


COSTS.update(
    {
        attend_kernel: 0.5,
        middle_kernel: 10.2,
        down_grad_kernel: 3.4,
        up_grad_kernel: 4.0,
        attend_back_kernel: 9.3,
    }
)


def after(values, *others):
    return lax.optimization_barrier((values, *others))[0]


def swap(values, axis, step):
    size = lax.axis_size(axis)
    return lax.ppermute(values, axis, [(i, i ^ step) for i in range(size)])


def body(
    inputs,
    block_ids,
    query_weight,
    query_bias,
    key_weight,
    value_weight,
    value_bias,
    out_weight,
    out_bias,
    gain_one,
    shift_one,
    up_weight,
    up_bias,
    down_weight,
    down_bias,
    gain_two,
    shift_two,
    cotangent,
):
    owners = lax.axis_size("fsdp")
    direct = owners == PARTS
    seq = lax.axis_index("seq").astype(jnp.int32)
    fsdp = lax.axis_index("fsdp").astype(jnp.int32)
    zero = jnp.zeros((), jnp.int32)
    index = jnp.stack([fsdp if direct else zero, seq, seq & 1, seq >> 1])
    _, part, width = inputs.shape
    own = inputs.reshape(part, width)
    total = part * lax.axis_size("seq")
    vectors = (query_bias, value_bias, out_bias, gain_one, shift_one, gain_two, shift_two, down_bias)

    if direct:
        first_part, down_part = run(
            pack_kernel,
            [((80, 896), BF), ((128, 512), BF)],
            index,
            (
                query_weight,
                key_weight,
                value_weight,
                out_weight,
                up_weight,
                down_weight,
                *vectors,
                up_bias,
            ),
            scratch=(((16, 384), F32),),
        )
        def along_z(piece):
            return [piece] + [swap(piece, "fsdp", k) for k in (2, 4, 6)]

        mine = along_z(first_part)
        down_part = after(down_part, mine[1])
        even = jnp.stack(mine)
        odd = swap(even, "fsdp", 1)
        shared = jnp.concatenate([even[:, :, 384:].reshape(320, 512), own])
        across = swap(shared, "seq", 2)
        evens = [swap(shared, "seq", 1), across, swap(across, "seq", 1)]
        xs = [own, *evens]
        down_even = jnp.stack(along_z(down_part))
        down_odd = swap(down_even, "fsdp", 1)
        odd_wide = odd[:, :, 384:]
        odd_across = swap(odd_wide, "seq", 2)
        odds = [swap(odd_wide, "seq", 1), odd_across]
    else:

        def full(values):
            return lax.all_gather(values, "fsdp", axis=0, tiled=True)

        vec = jnp.concatenate([full(v).reshape(PARTS, 64) for v in vectors] + [full(up_bias).reshape(PARTS, 256)], axis=1)
        vec = jnp.pad(vec.reshape(PARTS, 2, 384), ((0, 0), (0, 14), (0, 0)))
        cut = [
            lax.dynamic_slice_in_dim(full(w), seq * 128, 128, 1)
            for w in (query_weight, key_weight, value_weight)
        ]
        across = swap(own, "seq", 2)
        xs = [own, swap(own, "seq", 1), across, swap(across, "seq", 1)]
        heads = jnp.concatenate([jnp.concatenate(cut, axis=1).reshape(PARTS, 64, 384), vec], axis=1)
        core, x = seq & 1, seq >> 1
        wide = jnp.concatenate([full(out_weight), full(up_weight)], axis=1).reshape(PARTS, 64, 5, 512)
        blocks = []
        for k in range(4):
            at = (core ^ (k & 1)) * 32 + (x ^ (k >> 1)) * 16
            block = lax.dynamic_slice_in_dim(wide, at, 16, 1)
            blocks.append(block.transpose(0, 2, 1, 3).reshape(4, 2, 80, 512))
        both = jnp.concatenate([heads.reshape(4, 2, 80, 384), blocks[0]], axis=-1)
        even, odd = both[:, 0], both[:, 1]
        evens = [b[:, 0].reshape(320, 512) for b in blocks[1:]]
        odds = [b[:, 1] for b in blocks[1:]]
        tall = full(down_weight).reshape(4, 2, 256, 512)
        downs = []
        for k in range(4):
            downs.append(lax.dynamic_slice_in_dim(tall[:, k & 1], (core ^ (k >> 1)) * 128, 128, 1))

    piece = ((part, 128), BF)
    *ms, qa, ka, v, m_heads, rinv = run(
        attend_kernel,
        [piece] * 4
        + [((2, total, 128), BF)] * 2
        + [((total, 128), BF)] * 2
        + [((total, 128), F32)],
        index,
        (*xs, even, odd, block_ids),
        scratch=(
            ((512, 384), BF),
            ((PARTS, 384), F32),
            ((PARTS, 384), F32),
            ((total, 128), BF),
            ((total, 128), BF),
        ),
    )
    if direct:
        odds.append(swap(after(odd_across, ms[0]), "seq", 1))
        downs = [down_even, down_odd, swap(down_even, "seq", 1)]
        downs.append(swap(after(down_odd, ms[0]), "seq", 1))
    ms = [ms[0]] + [swap(ms[k], "seq", k) for k in (1, 2, 3)]
    result, *rest = run(
        middle_kernel,
        [((part, width), BF)]
        + [piece] * 4
        + [((part, width), F32)]
        + [((part, 1536), BF)] * 2
        + [((part, 2304), BF)] * 2
        + [((PARTS, 16, 384), BF)],
        index,
        (own, *ms, cotangent.reshape(part, width), even, odd, *evens, *odds, *downs),
        scratch=(
            ((512, 512), BF),
            ((512, 2048), BF),
            ((2048, 512), BF),
            ((PARTS, 384), F32),
            ((PARTS, 384), F32),
            ((part, 2048), F32),
            ((part, width), BF),
            ((part, width), BF),
            ((2, part, 1024), BF),
            ((2, part, 1024), BF),
            ((2, part, 256), BF),
            ((PARTS, 384), F32),
            ((PARTS, 384), F32),
        ),
    )
    ems, (e1, keep1, ship1, keep2, ship2, vg) = rest[:4], rest[4:]
    ems = [ems[0]] + [swap(ems[k], "seq", k) for k in (1, 2, 3)]
    up_even_grad, up_odd_grad = run(
        up_grad_kernel, [((4, 64, 1280), BF)] * 2, index, (keep2, swap(ship2, "seq", 1))
    )
    down_even, down_odd, down_send = run(
        down_grad_kernel,
        [((4, 64, 512), BF)] * 2 + [((8, 64, 512), BF)],
        index,
        (after(keep1, up_even_grad), swap(ship1, "seq", 1)),
    )
    dx_keep, dx_send, w_grad = run(
        attend_back_kernel,
        [((2, part, width), BF)] * 2 + [((PARTS, 80, 384), BF)],
        index,
        (*ems, after(qa, down_even), ka, v, m_heads, rinv, *xs, even, odd, vg),
        scratch=(
            ((512, 384), BF),
            ((total, 128), BF),
            ((2, total, 128), BF),
            ((2, total, 128), BF),
            ((2, total, 128), F32),
            ((total, 384), BF),
        ),
    )

    down_got = swap(down_send, "seq", 2)
    dx_send, down_got = lax.optimization_barrier((dx_send, down_got))
    got = swap(dx_send, "seq", 1)
    if direct:
        up_got = swap(up_odd_grad, "fsdp", 1)
        dx_keep, up_got = lax.optimization_barrier((dx_keep, up_got))
    far = swap(plus(dx_keep[1], got[1]), "seq", 2)
    input_grad = e1 + ((dx_keep[0].astype(F32) + got[0].astype(F32)) + far.astype(F32))

    if direct:

        def spread_out(mine):
            return (mine, *(swap(mine, "seq", k) for k in (1, 2, 3)))

        def cross(values):
            return [swap(values[k >> 1], "fsdp", k) for k in (2, 4, 6)]

        up_sums = [plus(up_even_grad[k], up_got[k]) for k in range(4)]
        down_got = after(down_got, dx_send)
        down_far = swap(plus(down_odd, down_got[4:]), "fsdp", 1)
        down_stay = plus(down_even, down_got[:4])
        down_far = after(down_far, *up_sums, far)
        down_sums = [plus(down_stay[k], down_far[k]) for k in range(4)]
        sums = [jnp.concatenate(pair, axis=1) for pair in zip(up_sums, down_sums)]
        sums_far = cross(sums)
        w_made = after(lax.all_to_all(w_grad, "fsdp", 0, 0, tiled=True), *down_sums)
        w_made = jnp.sum(w_made.astype(F32), axis=0).astype(BF)
        w_all = spread_out(w_made)
        all_sums = spread_out(plus(sums[0], *after(tuple(sums_far), w_made)))
        (
            wq_grad,
            wk_grad,
            wv_grad,
            qb_grad,
            vb_grad,
            ob_grad,
            g1_grad,
            s1_grad,
            g2_grad,
            s2_grad,
            db_grad,
            ub_grad,
        ) = run(
            end_heads_kernel,
            [((64, 512), F32)] * 3 + [((64,), F32)] * 8 + [((256,), F32)],
            index,
            w_all,
        )
        out_grad, up_grad, down_grad = run(
            end_wide_kernel,
            [((64, 512), F32), ((64, 2048), F32), ((256, 512), F32)],
            index,
            all_sums,
        )
    else:

        def summed(values):
            values = lax.psum_scatter(values, "fsdp", scatter_dimension=0, tiled=True)
            return lax.psum(values.astype(BF), "seq").astype(F32)

        kept = [plus(down_even, down_got[:4]), plus(down_odd, down_got[4:])]
        kept = lax.all_gather(jnp.stack(kept, axis=1).reshape(PARTS, 64, 512), "seq", axis=0)
        kept = kept.reshape(2, 2, PARTS, 64, 512).transpose(2, 1, 0, 3, 4).reshape(2048, 512)
        down_grad = lax.psum_scatter(kept.astype(F32), "fsdp", scatter_dimension=0, tiled=True)
        kept = lax.all_gather(jnp.stack([up_even_grad, up_odd_grad], axis=1).reshape(512, 1280), "seq", axis=0)
        kept = kept.astype(F32).reshape(2, 2, 512, 1280)
        kept = lax.psum_scatter(kept[0] + kept[1], "fsdp", scatter_dimension=1, tiled=True)
        up_grad = jnp.concatenate([kept[0, :, :1024], kept[1, :, :1024]], axis=1)
        out_grad = jnp.concatenate([kept[0, :, 1024:], kept[1, :, 1024:]], axis=1)
        both = w_grad.astype(F32)
        made = lax.psum_scatter(both[:, :64].reshape(512, 384), "fsdp", scatter_dimension=0, tiled=True)
        made = lax.all_gather(made.astype(BF), "seq", axis=0).astype(F32)
        wq_grad, wk_grad, wv_grad = (
            jnp.concatenate([made[t, :, i * 128 : (i + 1) * 128] for t in range(4)], axis=1)
            for i in range(3)
        )
        biases = lax.all_gather(lax.psum(both[0, 64], "fsdp").astype(BF), "seq", axis=0).astype(F32)
        cut = width // owners

        def mine(values):
            return lax.dynamic_slice_in_dim(values, fsdp * cut, cut, 0)

        qb_grad, vb_grad = mine(biases[:, :128].reshape(-1)), mine(biases[:, 256:].reshape(-1))
        flat = both[:, 65:67].reshape(PARTS, 768)
        ob_grad, g1_grad, s1_grad, g2_grad, s2_grad, db_grad = (
            summed(flat[:, k * 64 : (k + 1) * 64].reshape(-1)) for k in range(2, 8)
        )
        ub_grad = summed(flat[:, 512:].reshape(-1))

    return (
        result.reshape(inputs.shape),
        input_grad.reshape(inputs.shape),
        wq_grad,
        qb_grad,
        wk_grad,
        wv_grad,
        vb_grad,
        out_grad,
        ob_grad,
        g1_grad,
        s1_grad,
        up_grad,
        ub_grad,
        down_grad,
        db_grad,
        g2_grad,
        s2_grad,
    )


def solution(mesh):
    tokens, matrix, vector = P("fsdp", "seq", None), P("fsdp", None), P("fsdp")
    in_specs = (
        tokens,
        matrix,
        matrix,
        vector,
        matrix,
        matrix,
        vector,
        matrix,
        vector,
        vector,
        vector,
        matrix,
        vector,
        matrix,
        vector,
        vector,
        vector,
        tokens,
    )
    out_specs = (
        tokens,
        tokens,
        matrix,
        vector,
        matrix,
        matrix,
        vector,
        matrix,
        vector,
        vector,
        vector,
        matrix,
        vector,
        matrix,
        vector,
        vector,
        vector,
    )
    return jax.shard_map(body, mesh=mesh, in_specs=in_specs, out_specs=out_specs, check_vma=False)
```

time: 221 us -> 157 us (0.71)
  waiting for transfers between devices: 84.2 us -> 59.3 us
  Pallas kernels: 66.9 us -> 42.1 us
  local copies, waits for them, and re-layouts: 22.8 us -> 7.79 us
  other arithmetic: 0.62 us -> 4.4 us
  starting transfers between devices: 44.2 us -> 40.5 us
    ppermute x53 -> x38, waiting for transfers between devices: 84.2 us -> 59.3 us  [swap(): return lax.ppermute(values, axis, [(i, i ^ step) for i in range(size)])]
    pallas_call x21 -> x8, Pallas kernels: 66.9 us -> 42.1 us  [run(): pl.pallas_call(kernel, out_shape=outs, in_specs=[SMEM] + [VMEM] * len(arg...]
    ppermute x53 -> x38, starting transfers between devices: 44.2 us -> 35.5 us  [swap(): return lax.ppermute(values, axis, [(i, i ^ step) for i in range(size)])]
    unnamed x120 -> x70, local copies, waits for them, and re-layouts: 14.2 us -> 7.75 us
    concatenate x1 -> x0, local copies, waits for them, and re-layouts: 6.08 us -> none  [body(): vec = jnp.concatenate((*vectors, up_bias)).reshape(2, 384)]
    all_to_all x0 -> x1, starting transfers between devices: none -> 5 us  [body(): w_made = after(lax.all_to_all(w_grad, 'fsdp', 0, 0, tiled=True), *down_sums)]
  transfers between devices with their start and end apart: 53 -> 39, of which waited for: 21 -> 15; matrix products, arithmetic and copies ran while one was open for 1% -> 2% of each run, Pallas kernels for 21% -> 18%
where the time goes in v2:
time: 157 us; the launch traced here: 155 us
  waiting for transfers between devices  59.3 us (38%)
  Pallas kernels  42.1 us (27%)
  starting transfers between devices  40.5 us (26%)
  local copies, waits for them, and re-layouts  7.79 us (5%)
  other arithmetic  4.4 us (3%)
    ppermute x38, waiting for transfers between devices, swap(): return lax.ppermute(values, axis, [(i, i ^ step) for i in range(size)])  59.3 us
    pallas_call x8, Pallas kernels, run(): pl.pallas_call(kernel, out_shape=outs, in_specs=[SMEM] + [VMEM] * len(arg...  42.1 us
    ppermute x38, starting transfers between devices, swap(): return lax.ppermute(values, axis, [(i, i ^ step) for i in range(size)])  35.5 us
    unnamed x70, local copies, waits for them, and re-layouts  7.75 us
    all_to_all x1, starting transfers between devices, body(): w_made = after(lax.all_to_all(w_grad, 'fsdp', 0, 0, tiled=True), *down_sums)  5 us
  transfers between devices with their start and end apart: 39, of which 15 were waited for; matrix products, arithmetic and copies ran while one was open for 2% of the time, Pallas kernels for 18%

profile of v2, /device:TPU:0, one launch (start us, length us, event | category | flops | bytes accessed | tf_op | source)
XLA Modules:
  0.0 155.2 jit_solution(16405848353474148295)
XLA Ops:
  1.3 2.0 %shard_map.305 = (bf16[80,896]{1,0:T(8,128)(2,1)}, bf16[128,512]{1,0:T(8,128)(2,1)}) custom-call(s32[4]{0:T(128)} %pad_add_fusion.idx, bf16[64,512]{1,0:T(8,128)(2,1)} %wq.1, bf16[64,512]{1,0:T(8,128)(2,1)} %wk.1, bf16[64,512]{1,0:T(8,128)(2,1)} %wv.1, bf16[64,512]{1,0:T(8,128)(2,1)} %wo.1, bf16[64,2048]{1,0:T(8,128)(2,1)} %up.1, bf16[256,512]{1,0:T(8,128)(2,1)} %down.1, ...), custom_call_target="tpu_custom_call" | custom-call | flops 1700000000 | bytes 5100000 | tf_op jit(solution)/shard_map/pallas_call | solution.py:40
  3.3 5.1 %collective-permute-start.2 = (bf16[80,896]{1,0:T(8,128)(2,1)}, bf16[80,896]{1,0:T(8,128)(2,1)S(1)}, u32[]{:S(2)}, u32[]{:S(2)}) collective-permute-start(bf16[80,896]{1,0:T(8,128)(2,1)} %get-tuple-element.77), channel_id=1, source_target_pairs={{0,6},{1,7},{2,4},{3,5},{4,2},{5,3},{6,0},{7,1},{8,14},{9,15},{10,... | collective-permute-start | bytes 430088 | tf_op jit(solution)/shard_map/ppermute | solution.py:477
  9.1 4.3 %collective-permute-done.2 = bf16[80,896]{1,0:T(8,128)(2,1)S(1)} collective-permute-done((bf16[80,896]{1,0:T(8,128)(2,1)}, bf16[80,896]{1,0:T(8,128)(2,1)S(1)}, u32[]{:S(2)}, u32[]{:S(2)}) %collective-permute-start.2) | collective-permute-done | bytes 143392 | tf_op jit(solution)/shard_map/ppermute | solution.py:477
  13.3 7.4 %collective-permute-done.1 = bf16[80,896]{1,0:T(8,128)(2,1)S(1)} collective-permute-done((bf16[80,896]{1,0:T(8,128)(2,1)}, bf16[80,896]{1,0:T(8,128)(2,1)S(1)}, u32[]{:S(2)}, u32[]{:S(2)}) %collective-permute-start.1) | collective-permute-done | bytes 143392 | tf_op jit(solution)/shard_map/ppermute | solution.py:477
  21.9 1.6 %collective-permute-start.4 = (bf16[576,512]{1,0:T(8,128)(2,1)S(1)}, bf16[576,512]{1,0:T(8,128)(2,1)S(1)}, u32[]{:S(2)}, u32[]{:S(2)}) collective-permute-start(bf16[576,512]{1,0:T(8,128)(2,1)S(1)} %pad_maximum_fusion), channel_id=1, source_target_pairs={{0,16},{8,24},{16,0},{24,8},{1,17},{9,25},{17,1},{25,9},{2,18},{10... | collective-permute-start | bytes 1769480 | tf_op jit(solution)/shard_map/ppermute | solution.py:477
  23.5 2.5 %collective-permute-start.15 = (bf16[128,512]{1,0:T(8,128)(2,1)S(1)}, bf16[128,512]{1,0:T(8,128)(2,1)S(1)}, u32[]{:S(2)}, u32[]{:S(2)}) collective-permute-start(bf16[128,512]{1,0:T(8,128)(2,1)S(1)} %copy-done.13), channel_id=1, source_target_pairs={{0,6},{1,7},{2,4},{3,5},{4,2},{5,3},{6,0},{7,1},{8,14},{9,15},{10,... | collective-permute-start | bytes 393224 | tf_op jit(solution)/shard_map/ppermute | solution.py:477
  26.0 1.9 %collective-permute-start.13 = (bf16[128,512]{1,0:T(8,128)(2,1)S(1)}, bf16[128,512]{1,0:T(8,128)(2,1)S(1)}, u32[]{:S(2)}, u32[]{:S(2)}) collective-permute-start(bf16[128,512]{1,0:T(8,128)(2,1)S(1)} %copy-done.13), channel_id=1, source_target_pairs={{0,2},{1,3},{2,0},{3,1},{4,6},{5,7},{6,4},{7,5},{8,10},{9,11},{10,... | collective-permute-start | bytes 393224 | tf_op jit(solution)/shard_map/ppermute | solution.py:477
  27.8 1.5 collective-permute-start.6
  29.4 2.3 %collective-permute-done.15 = bf16[128,512]{1,0:T(8,128)(2,1)S(1)} collective-permute-done((bf16[128,512]{1,0:T(8,128)(2,1)S(1)}, bf16[128,512]{1,0:T(8,128)(2,1)S(1)}, u32[]{:S(2)}, u32[]{:S(2)}) %collective-permute-start.15) | collective-permute-done | bytes 131104 | tf_op jit(solution)/shard_map/ppermute | solution.py:477
  31.7 4.7 %collective-permute-done.4.refs_2_.refs_9_.refs_11_ = bf16[576,512]{1,0:T(8,128)(2,1)S(1)} collective-permute-done((bf16[576,512]{1,0:T(8,128)(2,1)S(1)}, bf16[576,512]{1,0:T(8,128)(2,1)S(1)}, u32[]{:S(2)}, u32[]{:S(2)}) %collective-permute-start.4) | collective-permute-done | bytes 589856 | tf_op jit(solution)/shard_map/ppermute | solution.py:477
  36.5 1.6 %collective-permute-start.16 = (bf16[4,128,512]{2,1,0:T(8,128)(2,1)S(1)}, bf16[4,128,512]{2,1,0:T(8,128)(2,1)S(1)}, u32[]{:S(2)}, u32[]{:S(2)}) collective-permute-start(bf16[4,128,512]{2,1,0:T(8,128)(2,1)S(1)} %pad_maximum_fusion.2.refs_14_), channel_id=1, source_target_pairs={{0,1},{1,0},{2,3},{3,2},{4,5},{5,4},{6,7},{7,6},{8,9},{9,8},{10,11... | collective-permute-start | bytes 1572872 | tf_op jit(solution)/shard_map/ppermute | solution.py:477
  38.1 3.8 %collective-permute-done.6.refs_5_.refs_7_.refs_14_ = bf16[4,80,896]{2,1,0:T(8,128)(2,1)S(1)} collective-permute-done((bf16[4,80,896]{2,1,0:T(8,128)(2,1)S(1)}, bf16[4,80,896]{2,1,0:T(8,128)(2,1)S(1)}, u32[]{:S(2)}, u32[]{:S(2)}) %collective-permute-start.6) | collective-permute-done | bytes 573472 | tf_op jit(solution)/shard_map/ppermute | solution.py:477
  44.4 7.7 %shard_map.306 = (bf16[256,128]{1,0:T(8,128)(2,1)}, bf16[256,128]{1,0:T(8,128)(2,1)}, bf16[256,128]{1,0:T(8,128)(2,1)}, bf16[256,128]{1,0:T(8,128)(2,1)}, bf16[2...) custom-call(s32[4]{0:T(128)} %pad_add_fusion.idx, ...), custom_call_target="tpu_custom_call" | custom-call | flops 500000000 | bytes 1500000 | tf_op jit(solution)/shard_map/pallas_call | solution.py:40
  56.0 2.0 %collective-permute-done.8.refs_3_ = bf16[256,128]{1,0:T(8,128)(2,1)S(1)} collective-permute-done((bf16[256,128]{1,0:T(8,128)(2,1)}, bf16[256,128]{1,0:T(8,128)(2,1)S(1)}, u32[]{:S(2)}, u32[]{:S(2)}) %collective-permute-start.8) | collective-permute-done | bytes 65568 | tf_op jit(solution)/shard_map/ppermute | solution.py:477
  59.9 10.3 %shard_map.307 = (bf16[256,512]{1,0:T(8,128)(2,1)}, bf16[256,128]{1,0:T(8,128)(2,1)}, bf16[256,128]{1,0:T(8,128)(2,1)}, bf16[256,128]{1,0:T(8,128)(2,1)}, bf16[2...) custom-call(s32[4]{0:T(128)} %pad_add_fusion.idx, ...), custom_call_target="tpu_custom_call" | custom-call | flops 10200000512 | bytes 30600000 | tf_op jit(solution)/shard_map/pallas_call | solution.py:40
  74.3 4.5 %shard_map.308 = (bf16[4,64,1280]{2,1,0:T(8,128)(2,1)}, bf16[4,64,1280]{2,1,0:T(8,128)(2,1)}) custom-call(s32[4]{0:T(128)} %pad_add_fusion.idx, bf16[256,2304]{1,0:T(8,128)(2,1)} %get-tuple-element.94.mine, bf16[256,2304]{1,0:T(8,128)(2,1)} %copy-done.15), custom_call_target="tpu_custom_call" | custom-call | flops 4000000000 | bytes 12000000 | tf_op jit(solution)/shard_map/pallas_call | solution.py:40
  79.7 3.7 %shard_map.309 = (bf16[4,64,512]{2,1,0:T(8,128)(2,1)}, bf16[4,64,512]{2,1,0:T(8,128)(2,1)}, bf16[8,64,512]{2,1,0:T(8,128)(2,1)}) custom-call(s32[4]{0:T(128)} %pad_add_fusion.idx, bf16[256,1536]{1,0:T(8,128)(2,1)} %get-tuple-element.97.mine, bf16[256,1536]{1,0:T(8,128)(2,1)} %copy-done.16), custom_call_target="tpu_custom_call" | custom-call | flops 3400000000 | bytes 10200000 | tf_op jit(solution)/shard_map/pallas_call | solution.py:40
  84.6 1.5 collective-permute-start.24
  86.8 9.8 %shard_map.310 = (bf16[2,256,512]{2,1,0:T(8,128)(2,1)}, bf16[2,256,512]{2,1,0:T(8,128)(2,1)}, bf16[8,80,384]{2,1,0:T(8,128)(2,1)}) custom-call(s32[4]{0:T(128)} %pad_add_fusion.idx, bf16[256,128]{1,0:T(8,128)(2,1)} %get-tuple-element.88.refs_0_, bf16[256,128]{1,0:T(8,128)(2,1)} %copy-done.26, bf16[256,128]{1,0:T(8,128)(2,1)} %copy-done.27, ...), custom_call_target="tpu_custom_call" | custom-call | flops 9299999744 | bytes 27900000 | tf_op jit(solution)/shard_map/pallas_call | solution.py:40
  97.8 5.0 %all-to-all-start = ((bf16[8,80,384]{2,1,0:T(8,128)(2,1)}), bf16[8,80,384]{2,1,0:T(8,128)(2,1)S(1)}, u32[]{:S(2)}, u32[]{:S(2)}) async-start(bf16[8,80,384]{2,1,0:T(8,128)(2,1)} %get-tuple-element.112), calls=%async_computation | async-start | bytes 983040 | tf_op jit(solution)/shard_map/all_to_all | solution.py:673
  102.9 2.1 %collective-permute-start.28 = (bf16[4,64,512]{2,1,0:T(8,128)(2,1)S(1)}, bf16[4,64,512]{2,1,0:T(8,128)(2,1)S(1)}, u32[]{:S(2)}, u32[]{:S(2)}) collective-permute-start(bf16[4,64,512]{2,1,0:T(8,128)(2,1)S(1)} %get-tuple-element.145), channel_id=1, source_target_pairs={{0,1},{1,0},{2,3},{3,2},{4,5},{5,4},{6,7},{7,6},{8,9},{9,8},{10,11... | collective-permute-start | bytes 786440 | tf_op jit(solution)/shard_map/ppermute | solution.py:477
  105.1 1.3 collective-permute-start.27
  106.5 10.1 %collective-permute-done.28 = bf16[4,64,512]{2,1,0:T(8,128)(2,1)S(1)} collective-permute-done((bf16[4,64,512]{2,1,0:T(8,128)(2,1)S(1)}, bf16[4,64,512]{2,1,0:T(8,128)(2,1)S(1)}, u32[]{:S(2)}, u32[]{:S(2)}) %collective-permute-start.28) | collective-permute-done | bytes 262176 | tf_op jit(solution)/shard_map/ppermute | solution.py:477
  116.8 1.5 collective-permute-start.32
  118.4 2.4 %collective-permute-start.33 = (bf16[64,1792]{1,0:T(8,128)(2,1)S(1)}, bf16[64,1792]{1,0:T(8,128)(2,1)}, u32[]{:S(2)}, u32[]{:S(2)}) collective-permute-start(bf16[64,1792]{1,0:T(8,128)(2,1)S(1)} %pad_maximum_fusion.4), channel_id=1, source_target_pairs={{0,4},{1,5},{2,6},{3,7},{4,0},{5,1},{6,2},{7,3},{8,12},{9,13},{10,... | collective-permute-start | bytes 688136 | tf_op jit(solution)/shard_map/ppermute | solution.py:477
  122.8 5.1 %collective-permute-done.32 = bf16[64,1792]{1,0:T(8,128)(2,1)S(1)} collective-permute-done((bf16[64,1792]{1,0:T(8,128)(2,1)S(1)}, bf16[64,1792]{1,0:T(8,128)(2,1)S(1)}, u32[]{:S(2)}, u32[]{:S(2)}) %collective-permute-start.32) | collective-permute-done | bytes 229408 | tf_op jit(solution)/shard_map/ppermute | solution.py:477
  127.9 9.9 %collective-permute-done.33 = bf16[64,1792]{1,0:T(8,128)(2,1)} collective-permute-done((bf16[64,1792]{1,0:T(8,128)(2,1)S(1)}, bf16[64,1792]{1,0:T(8,128)(2,1)}, u32[]{:S(2)}, u32[]{:S(2)}) %collective-permute-start.33) | collective-permute-done | bytes 229408 | tf_op jit(solution)/shard_map/ppermute | solution.py:477
  139.1 1.3 collective-permute-start.36
  143.1 1.7 %shard_map.311 = (f32[64,512]{1,0:T(8,128)}, f32[64,512]{1,0:T(8,128)}, f32[64,512]{1,0:T(8,128)}, f32[64]{0:T(128)}, f32[64]{0:T(128)}, /*index=5*/f32[64]{0:T(...) custom-call(s32[4]{0:T(128)} %pad_add_fusion.idx, ...), custom_call_target="tpu_custom_call" | custom-call | flops 1700000000 | bytes 5100000 | tf_op jit(solution)/shard_map/pallas_call | solution.py:40
  144.8 2.1 %collective-permute-done.37.d = bf16[64,1792]{1,0:T(8,128)(2,1)S(1)} collective-permute-done((bf16[64,1792]{1,0:T(8,128)(2,1)S(1)}, bf16[64,1792]{1,0:T(8,128)(2,1)S(1)}, u32[]{:S(2)}, u32[]{:S(2)}) %collective-permute-start.37) | collective-permute-done | bytes 229408 | tf_op jit(solution)/shard_map/ppermute | solution.py:477
  146.9 4.4 %collective-permute-done.36.c = bf16[64,1792]{1,0:T(8,128)(2,1)S(1)} collective-permute-done((bf16[64,1792]{1,0:T(8,128)(2,1)S(1)}, bf16[64,1792]{1,0:T(8,128)(2,1)S(1)}, u32[]{:S(2)}, u32[]{:S(2)}) %collective-permute-start.36) | collective-permute-done | bytes 229408 | tf_op jit(solution)/shard_map/ppermute | solution.py:477
  152.8 2.4 %shard_map.312 = (f32[64,512]{1,0:T(8,128)}, f32[64,2048]{1,0:T(8,128)}, f32[256,512]{1,0:T(8,128)}) custom-call(s32[4]{0:T(128)} %pad_add_fusion.idx, bf16[64,1792]{1,0:T(8,128)(2,1)} %copy-done.12, bf16[64,1792]{1,0:T(8,128)(2,1)} %copy-done.25, bf16[64,1792]{1,0:T(8,128)(2,1)} %copy-done.24, bf16[64,1792]{1,0:T(8,128)(2,1)} %copy-done.23), custom_call_target="tpu_custom_call" | custom-call | flops 1700000000 | bytes 5100000 | tf_op jit(solution)/shard_map/pallas_call | solution.py:40
  (140 shorter events, 26.6 us)
Async XLA Ops:
  3.3 10.0 %collective-permute-start.2 = (bf16[80,896]{1,0:T(8,128)(2,1)}, bf16[80,896]{1,0:T(8,128)(2,1)S(1)}, u32[]{:S(2)}, u32[]{:S(2)}) collective-permute-start(bf16[80,896]{1,0:T(8,128)(2,1)} %get-tuple-element.77), channel_id=1, source_target_pairs={{0,6},{1,7},{2,4},{3,5},{4,2},{5,3},{6,0},{7,1},{8,14},{9,15},{10,... | collective-permute-start | bytes 430088 | tf_op jit(solution)/shard_map/ppermute | solution.py:477
  8.4 12.3 %collective-permute-start.1 = (bf16[80,896]{1,0:T(8,128)(2,1)}, bf16[80,896]{1,0:T(8,128)(2,1)S(1)}, u32[]{:S(2)}, u32[]{:S(2)}) collective-permute-start(bf16[80,896]{1,0:T(8,128)(2,1)} %get-tuple-element.77), channel_id=1, source_target_pairs={{0,4},{1,5},{2,6},{3,7},{4,0},{5,1},{6,2},{7,3},{8,12},{9,13},{10,... | collective-permute-start | bytes 430088 | tf_op jit(solution)/shard_map/ppermute | solution.py:477
  8.5 12.3 %collective-permute-start = (bf16[80,896]{1,0:T(8,128)(2,1)}, bf16[80,896]{1,0:T(8,128)(2,1)S(1)}, u32[]{:S(2)}, u32[]{:S(2)}) collective-permute-start(bf16[80,896]{1,0:T(8,128)(2,1)} %get-tuple-element.77), channel_id=1, source_target_pairs={{0,2},{1,3},{2,0},{3,1},{4,6},{5,7},{6,4},{7,5},{8,10},{9,11},{10,... | collective-permute-start | bytes 430088 | tf_op jit(solution)/shard_map/ppermute | solution.py:477
  21.9 14.4 %collective-permute-start.4 = (bf16[576,512]{1,0:T(8,128)(2,1)S(1)}, bf16[576,512]{1,0:T(8,128)(2,1)S(1)}, u32[]{:S(2)}, u32[]{:S(2)}) collective-permute-start(bf16[576,512]{1,0:T(8,128)(2,1)S(1)} %pad_maximum_fusion), channel_id=1, source_target_pairs={{0,16},{8,24},{16,0},{24,8},{1,17},{9,25},{17,1},{25,9},{2,18},{10... | collective-permute-start | bytes 1769480 | tf_op jit(solution)/shard_map/ppermute | solution.py:477
  23.5 8.2 %collective-permute-start.15 = (bf16[128,512]{1,0:T(8,128)(2,1)S(1)}, bf16[128,512]{1,0:T(8,128)(2,1)S(1)}, u32[]{:S(2)}, u32[]{:S(2)}) collective-permute-start(bf16[128,512]{1,0:T(8,128)(2,1)S(1)} %copy-done.13), channel_id=1, source_target_pairs={{0,6},{1,7},{2,4},{3,5},{4,2},{5,3},{6,0},{7,1},{8,14},{9,15},{10,... | collective-permute-start | bytes 393224 | tf_op jit(solution)/shard_map/ppermute | solution.py:477
  26.0 10.4 %collective-permute-start.14 = (bf16[128,512]{1,0:T(8,128)(2,1)S(1)}, bf16[128,512]{1,0:T(8,128)(2,1)S(1)}, u32[]{:S(2)}, u32[]{:S(2)}) collective-permute-start(bf16[128,512]{1,0:T(8,128)(2,1)S(1)} %copy-done.13), channel_id=1, source_target_pairs={{0,4},{1,5},{2,6},{3,7},{4,0},{5,1},{6,2},{7,3},{8,12},{9,13},{10,... | collective-permute-start | bytes 393224 | tf_op jit(solution)/shard_map/ppermute | solution.py:477
  26.0 10.4 %collective-permute-start.13 = (bf16[128,512]{1,0:T(8,128)(2,1)S(1)}, bf16[128,512]{1,0:T(8,128)(2,1)S(1)}, u32[]{:S(2)}, u32[]{:S(2)}) collective-permute-start(bf16[128,512]{1,0:T(8,128)(2,1)S(1)} %copy-done.13), channel_id=1, source_target_pairs={{0,2},{1,3},{2,0},{3,1},{4,6},{5,7},{6,4},{7,5},{8,10},{9,11},{10,... | collective-permute-start | bytes 393224 | tf_op jit(solution)/shard_map/ppermute | solution.py:477
  27.8 14.0 %collective-permute-start.6 = (bf16[4,80,896]{2,1,0:T(8,128)(2,1)S(1)}, bf16[4,80,896]{2,1,0:T(8,128)(2,1)S(1)}, u32[]{:S(2)}, u32[]{:S(2)}) collective-permute-start(bf16[4,80,896]{2,1,0:T(8,128)(2,1)S(1)} %pad_maximum_fusion.1.refs_4_.refs_6_.refs_13_), channel_id=1, source_target_pairs={{0,1},{1,0},{2,3},{3,2},{4,5},{5,4},{6,7},{7,6},{8,9},{9,8},{10,11... | collective-permute-start | bytes 1720328 | tf_op jit(solution)/shard_map/ppermute | solution.py:477
  31.7 11.1 %collective-permute-start.3 = (bf16[576,512]{1,0:T(8,128)(2,1)S(1)}, bf16[576,512]{1,0:T(8,128)(2,1)S(1)}, u32[]{:S(2)}, u32[]{:S(2)}) collective-permute-start(bf16[576,512]{1,0:T(8,128)(2,1)S(1)} %pad_maximum_fusion), channel_id=1, source_target_pairs={{0,8},{8,0},{16,24},{24,16},{1,9},{9,1},{17,25},{25,17},{2,10},{10... | collective-permute-start | bytes 1769480 | tf_op jit(solution)/shard_map/ppermute | solution.py:477
  36.5 15.6 %collective-permute-start.16 = (bf16[4,128,512]{2,1,0:T(8,128)(2,1)S(1)}, bf16[4,128,512]{2,1,0:T(8,128)(2,1)S(1)}, u32[]{:S(2)}, u32[]{:S(2)}) collective-permute-start(bf16[4,128,512]{2,1,0:T(8,128)(2,1)S(1)} %pad_maximum_fusion.2.refs_14_), channel_id=1, source_target_pairs={{0,1},{1,0},{2,3},{3,2},{4,5},{5,4},{6,7},{7,6},{8,9},{9,8},{10,11... | collective-permute-start | bytes 1572872 | tf_op jit(solution)/shard_map/ppermute | solution.py:477
  41.9 10.9 %collective-permute-start.11 = (bf16[4,80,512]{2,1,0:T(8,128)(2,1)S(1)}, bf16[4,80,512]{2,1,0:T(8,128)(2,1)S(1)}, u32[]{:S(2)}, u32[]{:S(2)}) collective-permute-start(bf16[4,80,512]{2,1,0:T(8,128)(2,1)S(1)} %slice.97), channel_id=1, source_target_pairs={{0,16},{8,24},{16,0},{24,8},{1,17},{9,25},{17,1},{25,9},{2,18},{10... | collective-permute-start | bytes 983048 | tf_op jit(solution)/shard_map/ppermute | solution.py:477
  42.8 10.5 %collective-permute-start.17 = (bf16[4,128,512]{2,1,0:T(8,128)(2,1)S(1)}, bf16[4,128,512]{2,1,0:T(8,128)(2,1)S(1)}, u32[]{:S(2)}, u32[]{:S(2)}) collective-permute-start(bf16[4,128,512]{2,1,0:T(8,128)(2,1)S(1)} %pad_maximum_fusion.2.refs_14_), channel_id=1, source_target_pairs={{0,8},{8,0},{16,24},{24,16},{1,9},{9,1},{17,25},{25,17},{2,10},{10... | collective-permute-start | bytes 1572872 | tf_op jit(solution)/shard_map/ppermute | solution.py:477
  52.1 6.8 %collective-permute-start.18 = (bf16[4,128,512]{2,1,0:T(8,128)(2,1)S(1)}, bf16[4,128,512]{2,1,0:T(8,128)(2,1)S(1)}, u32[]{:S(2)}, u32[]{:S(2)}) collective-permute-start(bf16[4,128,512]{2,1,0:T(8,128)(2,1)S(1)} %collective-permute-done.16.refs_15_), channel_id=1, source_target_pairs={{0,8},{8,0},{16,24},{24,16},{1,9},{9,1},{17,25},{25,17},{2,10},{10... | collective-permute-start | bytes 1572872 | tf_op jit(solution)/shard_map/ppermute | solution.py:477
  70.5 8.3 %collective-permute-start.23 = (bf16[256,1536]{1,0:T(8,128)(2,1)}, bf16[256,1536]{1,0:T(8,128)(2,1)S(1)}, u32[]{:S(2)}, u32[]{:S(2)}) collective-permute-start(bf16[256,1536]{1,0:T(8,128)(2,1)} %get-tuple-element.98), channel_id=1, source_target_pairs={{0,8},{8,0},{16,24},{24,16},{1,9},{9,1},{17,25},{25,17},{2,10},{10... | collective-permute-start | bytes 2359304 | tf_op jit(solution)/shard_map/ppermute | solution.py:477
  70.7 15.4 %collective-permute-start.19 = (bf16[256,128]{1,0:T(8,128)(2,1)}, bf16[256,128]{1,0:T(8,128)(2,1)S(1)}, u32[]{:S(2)}, u32[]{:S(2)}) collective-permute-start(bf16[256,128]{1,0:T(8,128)(2,1)} %get-tuple-element.89), channel_id=1, source_target_pairs={{0,8},{8,0},{16,24},{24,16},{1,9},{9,1},{17,25},{25,17},{2,10},{10... | collective-permute-start | bytes 196616 | tf_op jit(solution)/shard_map/ppermute | solution.py:477
  71.0 15.2 %collective-permute-start.20 = (bf16[256,128]{1,0:T(8,128)(2,1)}, bf16[256,128]{1,0:T(8,128)(2,1)S(1)}, u32[]{:S(2)}, u32[]{:S(2)}) collective-permute-start(bf16[256,128]{1,0:T(8,128)(2,1)} %get-tuple-element.90), channel_id=1, source_target_pairs={{0,16},{8,24},{16,0},{24,8},{1,17},{9,25},{17,1},{25,9},{2,18},{10... | collective-permute-start | bytes 196616 | tf_op jit(solution)/shard_map/ppermute | solution.py:477
  72.2 14.0 %collective-permute-start.21 = (bf16[256,128]{1,0:T(8,128)(2,1)}, bf16[256,128]{1,0:T(8,128)(2,1)S(1)}, u32[]{:S(2)}, u32[]{:S(2)}) collective-permute-start(bf16[256,128]{1,0:T(8,128)(2,1)} %get-tuple-element.91), channel_id=1, source_target_pairs={{0,24},{8,16},{16,8},{24,0},{1,25},{9,17},{17,9},{25,1},{2,26},{10... | collective-permute-start | bytes 196616 | tf_op jit(solution)/shard_map/ppermute | solution.py:477
  83.4 14.3 %collective-permute-start.25 = (bf16[8,64,512]{2,1,0:T(8,128)(2,1)}, bf16[8,64,512]{2,1,0:T(8,128)(2,1)S(1)}, u32[]{:S(2)}, u32[]{:S(2)}) collective-permute-start(bf16[8,64,512]{2,1,0:T(8,128)(2,1)} %get-tuple-element.110), channel_id=1, source_target_pairs={{0,16},{8,24},{16,0},{24,8},{1,17},{9,25},{17,1},{25,9},{2,18},{10... | collective-permute-start | bytes 1572872 | tf_op jit(solution)/shard_map/ppermute | solution.py:477
  84.6 20.4 %collective-permute-start.24 = (bf16[4,64,1280]{2,1,0:T(8,128)(2,1)}, bf16[4,64,1280]{2,1,0:T(8,128)(2,1)S(1)}, u32[]{:S(2)}, u32[]{:S(2)}) collective-permute-start(bf16[4,64,1280]{2,1,0:T(8,128)(2,1)} %get-tuple-element.107), channel_id=1, source_target_pairs={{0,1},{1,0},{2,3},{3,2},{4,5},{5,4},{6,7},{7,6},{8,9},{9,8},{10,11... | collective-permute-start | bytes 1966088 | tf_op jit(solution)/shard_map/ppermute | solution.py:477
  97.8 7.3 %collective-permute-start.26 = (bf16[2,256,512]{2,1,0:T(8,128)(2,1)}, bf16[2,256,512]{2,1,0:T(8,128)(2,1)S(1)}, u32[]{:S(2)}, u32[]{:S(2)}) collective-permute-start(bf16[2,256,512]{2,1,0:T(8,128)(2,1)} %get-tuple-element.111), channel_id=1, source_target_pairs={{0,8},{8,0},{16,24},{24,16},{1,9},{9,1},{17,25},{25,17},{2,10},{10... | collective-permute-start | bytes 1572872 | tf_op jit(solution)/shard_map/ppermute | solution.py:477
  97.8 23.6 %all-to-all-start = ((bf16[8,80,384]{2,1,0:T(8,128)(2,1)}), bf16[8,80,384]{2,1,0:T(8,128)(2,1)S(1)}, u32[]{:S(2)}, u32[]{:S(2)}) async-start(bf16[8,80,384]{2,1,0:T(8,128)(2,1)} %get-tuple-element.112), calls=%async_computation | async-start | bytes 983040 | tf_op jit(solution)/shard_map/all_to_all | solution.py:673
  102.9 13.7 %collective-permute-start.28 = (bf16[4,64,512]{2,1,0:T(8,128)(2,1)S(1)}, bf16[4,64,512]{2,1,0:T(8,128)(2,1)S(1)}, u32[]{:S(2)}, u32[]{:S(2)}) collective-permute-start(bf16[4,64,512]{2,1,0:T(8,128)(2,1)S(1)} %get-tuple-element.145), channel_id=1, source_target_pairs={{0,1},{1,0},{2,3},{3,2},{4,5},{5,4},{6,7},{7,6},{8,9},{9,8},{10,11... | collective-permute-start | bytes 786440 | tf_op jit(solution)/shard_map/ppermute | solution.py:477
  105.1 11.6 %collective-permute-start.27 = (bf16[256,512]{1,0:T(8,128)(2,1)S(1)}, bf16[256,512]{1,0:T(8,128)(2,1)S(1)}, u32[]{:S(2)}, u32[]{:S(2)}) collective-permute-start(bf16[256,512]{1,0:T(8,128)(2,1)S(1)} %fusion.2), channel_id=1, source_target_pairs={{0,16},{8,24},{16,0},{24,8},{1,17},{9,25},{17,1},{25,9},{2,18},{10... | collective-permute-start | bytes 786440 | tf_op jit(solution)/shard_map/ppermute | solution.py:477
  116.8 11.1 %collective-permute-start.32 = (bf16[64,1792]{1,0:T(8,128)(2,1)S(1)}, bf16[64,1792]{1,0:T(8,128)(2,1)S(1)}, u32[]{:S(2)}, u32[]{:S(2)}) collective-permute-start(bf16[64,1792]{1,0:T(8,128)(2,1)S(1)} %pad_maximum_fusion.3), channel_id=1, source_target_pairs={{0,2},{1,3},{2,0},{3,1},{4,6},{5,7},{6,4},{7,5},{8,10},{9,11},{10,... | collective-permute-start | bytes 688136 | tf_op jit(solution)/shard_map/ppermute | solution.py:477
  118.4 19.4 %collective-permute-start.33 = (bf16[64,1792]{1,0:T(8,128)(2,1)S(1)}, bf16[64,1792]{1,0:T(8,128)(2,1)}, u32[]{:S(2)}, u32[]{:S(2)}) collective-permute-start(bf16[64,1792]{1,0:T(8,128)(2,1)S(1)} %pad_maximum_fusion.4), channel_id=1, source_target_pairs={{0,4},{1,5},{2,6},{3,7},{4,0},{5,1},{6,2},{7,3},{8,12},{9,13},{10,... | collective-permute-start | bytes 688136 | tf_op jit(solution)/shard_map/ppermute | solution.py:477
  120.8 17.0 %collective-permute-start.34 = (bf16[64,1792]{1,0:T(8,128)(2,1)S(1)}, bf16[64,1792]{1,0:T(8,128)(2,1)}, u32[]{:S(2)}, u32[]{:S(2)}) collective-permute-start(bf16[64,1792]{1,0:T(8,128)(2,1)S(1)} %pad_maximum_fusion.5), channel_id=1, source_target_pairs={{0,6},{1,7},{2,4},{3,5},{4,2},{5,3},{6,0},{7,1},{8,14},{9,15},{10,... | collective-permute-start | bytes 688136 | tf_op jit(solution)/shard_map/ppermute | solution.py:477
  121.4 18.9 %collective-permute-start.31 = (bf16[80,384]{1,0:T(8,128)(2,1)S(1)}, bf16[80,384]{1,0:T(8,128)(2,1)S(1)}, u32[]{:S(2)}, u32[]{:S(2)}) collective-permute-start(bf16[80,384]{1,0:T(8,128)(2,1)S(1)} %reduce_sum.12.a), channel_id=1, source_target_pairs={{0,24},{8,16},{16,8},{24,0},{1,25},{9,17},{17,9},{25,1},{2,26},{10... | collective-permute-start | bytes 184328 | tf_op jit(solution)/shard_map/ppermute | solution.py:477
  121.5 20.3 %collective-permute-start.30 = (bf16[80,384]{1,0:T(8,128)(2,1)S(1)}, bf16[80,384]{1,0:T(8,128)(2,1)S(1)}, u32[]{:S(2)}, u32[]{:S(2)}) collective-permute-start(bf16[80,384]{1,0:T(8,128)(2,1)S(1)} %reduce_sum.12.a), channel_id=1, source_target_pairs={{0,16},{8,24},{16,0},{24,8},{1,17},{9,25},{17,1},{25,9},{2,18},{10... | collective-permute-start | bytes 184328 | tf_op jit(solution)/shard_map/ppermute | solution.py:477
  127.9 14.0 %collective-permute-start.29 = (bf16[80,384]{1,0:T(8,128)(2,1)S(1)}, bf16[80,384]{1,0:T(8,128)(2,1)S(1)}, u32[]{:S(2)}, u32[]{:S(2)}) collective-permute-start(bf16[80,384]{1,0:T(8,128)(2,1)S(1)} %reduce_sum.12.a), channel_id=1, source_target_pairs={{0,8},{8,0},{16,24},{24,16},{1,9},{9,1},{17,25},{25,17},{2,10},{10... | collective-permute-start | bytes 184328 | tf_op jit(solution)/shard_map/ppermute | solution.py:477
  139.0 8.0 %collective-permute-start.37 = (bf16[64,1792]{1,0:T(8,128)(2,1)S(1)}, bf16[64,1792]{1,0:T(8,128)(2,1)S(1)}, u32[]{:S(2)}, u32[]{:S(2)}) collective-permute-start(bf16[64,1792]{1,0:T(8,128)(2,1)S(1)} %add_convert_fusion.3.a), channel_id=1, source_target_pairs={{0,24},{8,16},{16,8},{24,0},{1,25},{9,17},{17,9},{25,1},{2,26},{10... | collective-permute-start | bytes 688136 | tf_op jit(solution)/shard_map/ppermute | solution.py:477
  139.1 12.3 %collective-permute-start.36 = (bf16[64,1792]{1,0:T(8,128)(2,1)S(1)}, bf16[64,1792]{1,0:T(8,128)(2,1)S(1)}, u32[]{:S(2)}, u32[]{:S(2)}) collective-permute-start(bf16[64,1792]{1,0:T(8,128)(2,1)S(1)} %add_convert_fusion.3.a), channel_id=1, source_target_pairs={{0,16},{8,24},{16,0},{24,8},{1,17},{9,25},{17,1},{25,9},{2,18},{10... | collective-permute-start | bytes 688136 | tf_op jit(solution)/shard_map/ppermute | solution.py:477
  140.3 11.1 %collective-permute-start.35 = (bf16[64,1792]{1,0:T(8,128)(2,1)S(1)}, bf16[64,1792]{1,0:T(8,128)(2,1)S(1)}, u32[]{:S(2)}, u32[]{:S(2)}) collective-permute-start(bf16[64,1792]{1,0:T(8,128)(2,1)S(1)} %add_convert_fusion.3.a), channel_id=1, source_target_pairs={{0,8},{8,0},{16,24},{24,16},{1,9},{9,1},{17,25},{25,17},{2,10},{10... | collective-permute-start | bytes 688136 | tf_op jit(solution)/shard_map/ppermute | solution.py:477
  (42 other events, 229.2 us)

commit v3 on v2

--- a/solution.py
+++ b/solution.py
@@ -34,7 +34,7 @@
     return lax.dot_general(left, right, (((0,), (0,)), ((), ())), preferred_element_type=F32)
 
 
-def run(kernel, outs, index, args, scratch=()):
+def run(kernel, outs, index, args, scratch=(), room=20):
     cost = COSTS.get(kernel, 1.7)
     outs = [jax.ShapeDtypeStruct(*o) for o in outs]
     return pl.pallas_call(
@@ -43,7 +43,7 @@
         in_specs=[SMEM] + [VMEM] * len(args),
         out_specs=[VMEM] * len(outs),
         scratch_shapes=[pltpu.VMEM(*s) for s in scratch],
-        compiler_params=pltpu.CompilerParams(vmem_limit_bytes=56 * 1024 * 1024),
+        compiler_params=pltpu.CompilerParams(vmem_limit_bytes=room * 1024 * 1024),
         cost_estimate=pl.CostEstimate(flops=int(cost * 1e9), bytes_accessed=int(cost * 3e6), transcendentals=0),
     )(index, *args)
 
@@ -423,17 +423,17 @@
     return functools.reduce(jnp.add, [t.astype(F32) for t in terms]).astype(BF)
 
 
-def end_wide_kernel(idx, a, b, c, d, out_grad, up_grad, down_grad):
+def end_wide_kernel(idx, a, b, c, d, *refs):
+    parts, (out_grad, up_grad, down_grad) = refs[:4], refs[4:]
     core, x = idx[2], idx[3]
-    wide = slice(0, 1280)
-    own = a[:, wide].astype(F32) + c[:, wide].astype(F32)
-    other = b[:, wide].astype(F32) + d[:, wide].astype(F32)
+    own = a[...].astype(F32) + c[...].astype(F32)
+    other = b[...].astype(F32) + d[...].astype(F32)
     left, right = jnp.where(core == 0, own, other), jnp.where(core == 0, other, own)
     up_grad[:, :1024], up_grad[:, 1024:] = left[:, :1024], right[:, :1024]
     out_grad[:, :256], out_grad[:, 256:] = left[:, 1024:], right[:, 1024:]
-    for k, ref in enumerate((a, b, c, d)):
+    for k, ref in enumerate(parts):
         at = (core ^ (k & 1)) * 128 + (x ^ (k >> 1)) * 64
-        down_grad[pl.ds(pl.multiple_of(at, 64), 64), :] = ref[:, 1280:].astype(F32)
+        down_grad[pl.ds(pl.multiple_of(at, 64), 64), :] = ref[...].astype(F32)
 
 
 def end_heads_kernel(idx, a, b, c, d, wq, wk, wv, qb, vb, ob, g1, s1, g2, s2, db, ub):
@@ -524,6 +524,7 @@
                 up_bias,
             ),
             scratch=(((16, 384), F32),),
+            room=60,
         )
         def along_z(piece):
             return [piece] + [swap(piece, "fsdp", k) for k in (2, 4, 6)]
@@ -534,7 +535,7 @@
         odd = swap(even, "fsdp", 1)
         shared = jnp.concatenate([even[:, :, 384:].reshape(320, 512), own])
         across = swap(shared, "seq", 2)
-        evens = [swap(shared, "seq", 1), across, swap(across, "seq", 1)]
+        evens = [swap(shared, "seq", 1), across, swap(after(across, odd), "seq", 1)]
         xs = [own, *evens]
         down_even = jnp.stack(along_z(down_part))
         down_odd = swap(down_even, "fsdp", 1)
@@ -588,11 +589,12 @@
             ((total, 128), BF),
         ),
     )
+    made = ms[0]
+    ms = [made] + [swap(ms[k], "seq", k) for k in (1, 2, 3)]
     if direct:
-        odds.append(swap(after(odd_across, ms[0]), "seq", 1))
+        odds.append(swap(after(odd_across, made), "seq", 1))
         downs = [down_even, down_odd, swap(down_even, "seq", 1)]
-        downs.append(swap(after(down_odd, ms[0]), "seq", 1))
-    ms = [ms[0]] + [swap(ms[k], "seq", k) for k in (1, 2, 3)]
+        downs.append(swap(after(down_odd, ms[2], ms[3]), "seq", 1))
     result, *rest = run(
         middle_kernel,
         [((part, width), BF)]
@@ -657,7 +659,8 @@
     if direct:
 
         def spread_out(mine):
-            return (mine, *(swap(mine, "seq", k) for k in (1, 2, 3)))
+            across = swap(mine, "seq", 2)
+            return mine, swap(mine, "seq", 1), across, swap(across, "seq", 1)
 
         def cross(values):
             return [swap(values[k >> 1], "fsdp", k) for k in (2, 4, 6)]
@@ -668,12 +671,13 @@
         down_stay = plus(down_even, down_got[:4])
         down_far = after(down_far, *up_sums, far)
         down_sums = [plus(down_stay[k], down_far[k]) for k in range(4)]
-        sums = [jnp.concatenate(pair, axis=1) for pair in zip(up_sums, down_sums)]
-        sums_far = cross(sums)
+        up_far = cross(up_sums)
+        down_far = cross(down_sums)
         w_made = after(lax.all_to_all(w_grad, "fsdp", 0, 0, tiled=True), *down_sums)
         w_made = jnp.sum(w_made.astype(F32), axis=0).astype(BF)
         w_all = spread_out(w_made)
-        all_sums = spread_out(plus(sums[0], *after(tuple(sums_far), w_made)))
+        up_all = spread_out(plus(up_sums[0], *up_far))
+        down_all = spread_out(plus(down_sums[0], *down_far))
         (
             wq_grad,
             wk_grad,
@@ -697,7 +701,7 @@
             end_wide_kernel,
             [((64, 512), F32), ((64, 2048), F32), ((256, 512), F32)],
             index,
-            all_sums,
+            up_all + down_all,
         )
     else:
 

time: 157 us -> 131 us (0.83); the launches traced: 155 us -> 131 us
  Pallas kernels: 42.1 us -> 29.1 us
  waiting for transfers between devices: 59.3 us -> 49.9 us
  local copies, waits for them, and re-layouts: 7.79 us -> 0.08 us
  other arithmetic: 4.4 us -> 8.22 us
  starting transfers between devices: 40.5 us -> 42.7 us
    pallas_call x8, Pallas kernels: 42.1 us -> 29.1 us  [run(): pl.pallas_call(kernel, out_shape=outs, in_specs=[SMEM] + [VMEM] * len(arg...]
    ppermute x38 -> x44, waiting for transfers between devices: 59.3 us -> 49.9 us  [swap(): return lax.ppermute(values, axis, [(i, i ^ step) for i in range(size)])]
    unnamed x70 -> x12, local copies, waits for them, and re-layouts: 7.75 us -> 0.03 us
    ppermute x38 -> x44, starting transfers between devices: 35.5 us -> 38.5 us  [swap(): return lax.ppermute(values, axis, [(i, i ^ step) for i in range(size)])]
    convert_element_type x5 -> x6, other arithmetic: 1.59 us -> 3.55 us  [plus(): return functools.reduce(jnp.add, [t.astype(F32) for t in terms]).astype(BF)]
  transfers between devices with their start and end apart: 39 -> 45, of which waited for: 15 -> 15; matrix products, arithmetic and copies ran while one was open for 2% -> 5% of each run, Pallas kernels for 18% -> 15%
where the time goes in v3:
time: 131 us
  waiting for transfers between devices  49.9 us (38%)
  starting transfers between devices  42.7 us (33%)
  Pallas kernels  29.1 us (22%)
  other arithmetic  8.22 us (6%)
    ppermute x44, waiting for transfers between devices, swap(): return lax.ppermute(values, axis, [(i, i ^ step) for i in range(size)])  49.9 us
    ppermute x44, starting transfers between devices, swap(): return lax.ppermute(values, axis, [(i, i ^ step) for i in range(size)])  38.5 us
    pallas_call x8, Pallas kernels, run(): pl.pallas_call(kernel, out_shape=outs, in_specs=[SMEM] + [VMEM] * len(arg...  29.1 us
    all_to_all x1, starting transfers between devices, body(): w_made = after(lax.all_to_all(w_grad, 'fsdp', 0, 0, tiled=True), *down_sums)  4.14 us
    convert_element_type x6, other arithmetic, plus(): return functools.reduce(jnp.add, [t.astype(F32) for t in terms]).astype(BF)  3.55 us
  transfers between devices with their start and end apart: 45, of which 15 were waited for; matrix products, arithmetic and copies ran while one was open for 5% of the time, Pallas kernels for 15%

profile of v3, /device:TPU:0, one launch (start us, length us, event | category | flops | bytes accessed | tf_op | source)
XLA Modules:
  0.0 130.9 jit_solution(11359028256175092368)
XLA Ops:
  1.2 2.0 %shard_map.305 = (bf16[80,896]{1,0:T(8,128)(2,1)}, bf16[128,512]{1,0:T(8,128)(2,1)}) custom-call(s32[4]{0:T(128)} %pad_add_fusion.idx, bf16[64,512]{1,0:T(8,128)(2,1)} %wq.1, bf16[64,512]{1,0:T(8,128)(2,1)} %wk.1, bf16[64,512]{1,0:T(8,128)(2,1)} %wv.1, bf16[64,512]{1,0:T(8,128)(2,1)} %wo.1, bf16[64,2048]{1,0:T(8,128)(2,1)} %up.1, bf16[256,512]{1,0:T(8,128)(2,1)} %down.1, ...), custom_call_target="tpu_custom_call" | custom-call | flops 1700000000 | bytes 5100000 | tf_op jit(solution)/shard_map/pallas_call | solution.py:40
  3.3 5.1 %collective-permute-start.2 = (bf16[80,896]{1,0:T(8,128)(2,1)}, bf16[80,896]{1,0:T(8,128)(2,1)S(1)}, u32[]{:S(2)}, u32[]{:S(2)}) collective-permute-start(bf16[80,896]{1,0:T(8,128)(2,1)} %get-tuple-element.75), channel_id=1, source_target_pairs={{0,6},{1,7},{2,4},{3,5},{4,2},{5,3},{6,0},{7,1},{8,14},{9,15},{10,... | collective-permute-start | bytes 430088 | tf_op jit(solution)/shard_map/ppermute | solution.py:477
  9.0 4.3 %collective-permute-done.2 = bf16[80,896]{1,0:T(8,128)(2,1)S(1)} collective-permute-done((bf16[80,896]{1,0:T(8,128)(2,1)}, bf16[80,896]{1,0:T(8,128)(2,1)S(1)}, u32[]{:S(2)}, u32[]{:S(2)}) %collective-permute-start.2) | collective-permute-done | bytes 143392 | tf_op jit(solution)/shard_map/ppermute | solution.py:477
  13.3 7.4 %collective-permute-done.1 = bf16[80,896]{1,0:T(8,128)(2,1)S(1)} collective-permute-done((bf16[80,896]{1,0:T(8,128)(2,1)}, bf16[80,896]{1,0:T(8,128)(2,1)S(1)}, u32[]{:S(2)}, u32[]{:S(2)}) %collective-permute-start.1) | collective-permute-done | bytes 143392 | tf_op jit(solution)/shard_map/ppermute | solution.py:477
  21.8 1.6 %collective-permute-start.4 = (bf16[576,512]{1,0:T(8,128)(2,1)S(1)}, bf16[576,512]{1,0:T(8,128)(2,1)S(1)}, u32[]{:S(2)}, u32[]{:S(2)}) collective-permute-start(bf16[576,512]{1,0:T(8,128)(2,1)S(1)} %pad_maximum_fusion), channel_id=1, source_target_pairs={{0,16},{8,24},{16,0},{24,8},{1,17},{9,25},{17,1},{25,9},{2,18},{10... | collective-permute-start | bytes 1769480 | tf_op jit(solution)/shard_map/ppermute | solution.py:477
  23.4 1.5 %collective-permute-start.5 = (bf16[4,80,896]{2,1,0:T(8,128)(2,1)S(1)}, bf16[4,80,896]{2,1,0:T(8,128)(2,1)S(1)}, u32[]{:S(2)}, u32[]{:S(2)}) collective-permute-start(bf16[4,80,896]{2,1,0:T(8,128)(2,1)S(1)} %pad_maximum_fusion.1.refs_4_.refs_6_.refs_13_), channel_id=1, source_target_pairs={{0,1},{1,0},{2,3},{3,2},{4,5},{5,4},{6,7},{7,6},{8,9},{9,8},{10,11... | collective-permute-start | bytes 1720328 | tf_op jit(solution)/shard_map/ppermute | solution.py:477
  24.9 2.5 %collective-permute-start.15 = (bf16[128,512]{1,0:T(8,128)(2,1)S(1)}, bf16[128,512]{1,0:T(8,128)(2,1)S(1)}, u32[]{:S(2)}, u32[]{:S(2)}) collective-permute-start(bf16[128,512]{1,0:T(8,128)(2,1)S(1)} %copy-done.5), channel_id=1, source_target_pairs={{0,6},{1,7},{2,4},{3,5},{4,2},{5,3},{6,0},{7,1},{8,14},{9,15},{10,... | collective-permute-start | bytes 393224 | tf_op jit(solution)/shard_map/ppermute | solution.py:477
  27.4 1.9 %collective-permute-start.13 = (bf16[128,512]{1,0:T(8,128)(2,1)S(1)}, bf16[128,512]{1,0:T(8,128)(2,1)S(1)}, u32[]{:S(2)}, u32[]{:S(2)}) collective-permute-start(bf16[128,512]{1,0:T(8,128)(2,1)S(1)} %copy-done.5), channel_id=1, source_target_pairs={{0,2},{1,3},{2,0},{3,1},{4,6},{5,7},{6,4},{7,5},{8,10},{9,11},{10,... | collective-permute-start | bytes 393224 | tf_op jit(solution)/shard_map/ppermute | solution.py:477
  29.3 7.8 %collective-permute-done.5.refs_5_.refs_7_.refs_14_ = bf16[4,80,896]{2,1,0:T(8,128)(2,1)S(1)} collective-permute-done((bf16[4,80,896]{2,1,0:T(8,128)(2,1)S(1)}, bf16[4,80,896]{2,1,0:T(8,128)(2,1)S(1)}, u32[]{:S(2)}, u32[]{:S(2)}) %collective-permute-start.5) | collective-permute-done | bytes 573472 | tf_op jit(solution)/shard_map/ppermute | solution.py:477
  37.7 1.6 %collective-permute-start.16 = (bf16[4,128,512]{2,1,0:T(8,128)(2,1)S(1)}, bf16[4,128,512]{2,1,0:T(8,128)(2,1)S(1)}, u32[]{:S(2)}, u32[]{:S(2)}) collective-permute-start(bf16[4,128,512]{2,1,0:T(8,128)(2,1)S(1)} %pad_maximum_fusion.2.refs_14_), channel_id=1, source_target_pairs={{0,1},{1,0},{2,3},{3,2},{4,5},{5,4},{6,7},{7,6},{8,9},{9,8},{10,11... | collective-permute-start | bytes 1572872 | tf_op jit(solution)/shard_map/ppermute | solution.py:477
  40.0 5.3 %shard_map.306 = (bf16[256,128]{1,0:T(8,128)(2,1)S(1)}, bf16[256,128]{1,0:T(8,128)(2,1)S(1)}, bf16[256,128]{1,0:T(8,128)(2,1)S(1)}, bf16[256,128]{1,0:T(8,128)(2...) custom-call(s32[4]{0:T(128)S(1)} %copy-done.2, ...), custom_call_target="tpu_custom_call" | custom-call | flops 500000000 | bytes 1500000 | tf_op jit(solution)/shard_map/pallas_call | solution.py:40
  45.3 1.6 %collective-permute-start.8 = (bf16[256,128]{1,0:T(8,128)(2,1)S(1)}, bf16[256,128]{1,0:T(8,128)(2,1)S(1)}, u32[]{:S(2)}, u32[]{:S(2)}) collective-permute-start(bf16[256,128]{1,0:T(8,128)(2,1)S(1)} %get-tuple-element.79), channel_id=1, source_target_pairs={{0,16},{8,24},{16,0},{24,8},{1,17},{9,25},{17,1},{25,9},{2,18},{10... | collective-permute-start | bytes 196616 | tf_op jit(solution)/shard_map/ppermute | solution.py:477
  47.5 4.1 %collective-permute-done.16.refs_15_ = bf16[4,128,512]{2,1,0:T(8,128)(2,1)S(1)} collective-permute-done((bf16[4,128,512]{2,1,0:T(8,128)(2,1)S(1)}, bf16[4,128,512]{2,1,0:T(8,128)(2,1)S(1)}, u32[]{:S(2)}, u32[]{:S(2)}) %collective-permute-start.16) | collective-permute-done | bytes 524320 | tf_op jit(solution)/shard_map/ppermute | solution.py:477
  54.6 6.3 %shard_map.307 = (bf16[256,512]{1,0:T(8,128)(2,1)}, bf16[256,128]{1,0:T(8,128)(2,1)S(1)}, bf16[256,128]{1,0:T(8,128)(2,1)S(1)}, bf16[256,128]{1,0:T(8,128)(2,1)S...) custom-call(s32[4]{0:T(128)S(1)} %copy-done.2, ...), custom_call_target="tpu_custom_call" | custom-call | flops 10200000512 | bytes 30600000 | tf_op jit(solution)/shard_map/pallas_call | solution.py:40
  63.9 2.3 %shard_map.308 = (bf16[4,64,1280]{2,1,0:T(8,128)(2,1)S(1)}, bf16[4,64,1280]{2,1,0:T(8,128)(2,1)S(1)}) custom-call(s32[4]{0:T(128)S(1)} %copy-done.2, bf16[256,2304]{1,0:T(8,128)(2,1)S(1)} %get-tuple-element.93.mine, bf16[256,2304]{1,0:T(8,128)(2,1)S(1)} %collective-permute-done.22.other), custom_call_target="tpu_custom_call" | custom-call | flops 4000000000 | bytes 12000000 | tf_op jit(solution)/shard_map/pallas_call | solution.py:40
  66.2 2.7 %shard_map.309 = (bf16[4,64,512]{2,1,0:T(8,128)(2,1)S(1)}, bf16[4,64,512]{2,1,0:T(8,128)(2,1)S(1)}, bf16[8,64,512]{2,1,0:T(8,128)(2,1)}) custom-call(s32[4]{0:T(128)S(1)} %copy-done.2, bf16[256,1536]{1,0:T(8,128)(2,1)S(1)} %get-tuple-element.96.mine, bf16[256,1536]{1,0:T(8,128)(2,1)S(1)} %collective-permute-done.23.other), custom_call_target="tpu_custom_call" | custom-call | flops 3400000000 | bytes 10200000 | tf_op jit(solution)/shard_map/pallas_call | solution.py:40
  69.5 1.5 %collective-permute-start.24 = (bf16[4,64,1280]{2,1,0:T(8,128)(2,1)S(1)}, bf16[4,64,1280]{2,1,0:T(8,128)(2,1)}, u32[]{:S(2)}, u32[]{:S(2)}) collective-permute-start(bf16[4,64,1280]{2,1,0:T(8,128)(2,1)S(1)} %get-tuple-element.106), channel_id=1, source_target_pairs={{0,1},{1,0},{2,3},{3,2},{4,5},{5,4},{6,7},{7,6},{8,9},{9,8},{10,11... | collective-permute-start | bytes 1966088 | tf_op jit(solution)/shard_map/ppermute | solution.py:477
  71.1 7.4 %shard_map.310 = (bf16[2,256,512]{2,1,0:T(8,128)(2,1)S(1)}, bf16[2,256,512]{2,1,0:T(8,128)(2,1)S(1)}, bf16[8,80,384]{2,1,0:T(8,128)(2,1)}) custom-call(s32[4]{0:T(128)S(1)} %copy-done.2, bf16[256,128]{1,0:T(8,128)(2,1)S(1)} %get-tuple-element.87.refs_0_, bf16[256,128]{1,0:T(8,128)(2,1)S(1)} %collective-permute-done.19.refs_1_, ...), custom_call_target="tpu_custom_call" | custom-call | flops 9299999744 | bytes 27900000 | tf_op jit(solution)/shard_map/pallas_call | solution.py:40
  78.5 4.1 %all-to-all-start = ((bf16[8,80,384]{2,1,0:T(8,128)(2,1)}), bf16[8,80,384]{2,1,0:T(8,128)(2,1)}, u32[]{:S(2)}, u32[]{:S(2)}) async-start(bf16[8,80,384]{2,1,0:T(8,128)(2,1)} %get-tuple-element.111), calls=%async_computation | async-start | bytes 983040 | tf_op jit(solution)/shard_map/all_to_all | solution.py:676
  84.3 1.6 %collective-permute-start.28 = (bf16[4,64,512]{2,1,0:T(8,128)(2,1)S(1)}, bf16[4,64,512]{2,1,0:T(8,128)(2,1)S(1)}, u32[]{:S(2)}, u32[]{:S(2)}) collective-permute-start(bf16[4,64,512]{2,1,0:T(8,128)(2,1)S(1)} %get-tuple-element.143), channel_id=1, source_target_pairs={{0,1},{1,0},{2,3},{3,2},{4,5},{5,4},{6,7},{7,6},{8,9},{9,8},{10,11... | collective-permute-start | bytes 786440 | tf_op jit(solution)/shard_map/ppermute | solution.py:477
  85.9 2.7 %collective-permute-done.24 = bf16[4,64,1280]{2,1,0:T(8,128)(2,1)} collective-permute-done((bf16[4,64,1280]{2,1,0:T(8,128)(2,1)S(1)}, bf16[4,64,1280]{2,1,0:T(8,128)(2,1)}, u32[]{:S(2)}, u32[]{:S(2)}) %collective-permute-start.24) | collective-permute-done | bytes 655392 | tf_op jit(solution)/shard_map/ppermute | solution.py:477
  89.9 2.6 %collective-permute-start.34 = (bf16[64,1280]{1,0:T(8,128)(2,1)S(1)}, bf16[64,1280]{1,0:T(8,128)(2,1)S(1)}, u32[]{:S(2)}, u32[]{:S(2)}) collective-permute-start(bf16[64,1280]{1,0:T(8,128)(2,1)S(1)} %get-tuple-element.138), channel_id=1, source_target_pairs={{0,6},{1,7},{2,4},{3,5},{4,2},{5,3},{6,0},{7,1},{8,14},{9,15},{10,... | collective-permute-start | bytes 491528 | tf_op jit(solution)/shard_map/ppermute | solution.py:477
  93.5 1.5 %collective-permute-start.27 = (bf16[256,512]{1,0:T(8,128)(2,1)S(1)}, bf16[256,512]{1,0:T(8,128)(2,1)S(1)}, u32[]{:S(2)}, u32[]{:S(2)}) collective-permute-start(bf16[256,512]{1,0:T(8,128)(2,1)S(1)} %fusion.2), channel_id=1, source_target_pairs={{0,16},{8,24},{16,0},{24,8},{1,17},{9,25},{17,1},{25,9},{2,18},{10... | collective-permute-start | bytes 786440 | tf_op jit(solution)/shard_map/ppermute | solution.py:477
  95.7 7.5 %collective-permute-done.34 = bf16[64,1280]{1,0:T(8,128)(2,1)S(1)} collective-permute-done((bf16[64,1280]{1,0:T(8,128)(2,1)S(1)}, bf16[64,1280]{1,0:T(8,128)(2,1)S(1)}, u32[]{:S(2)}, u32[]{:S(2)}) %collective-permute-start.34) | collective-permute-done | bytes 163872 | tf_op jit(solution)/shard_map/ppermute | solution.py:477
  103.2 7.1 %collective-permute-done.33 = bf16[64,1280]{1,0:T(8,128)(2,1)S(1)} collective-permute-done((bf16[64,1280]{1,0:T(8,128)(2,1)S(1)}, bf16[64,1280]{1,0:T(8,128)(2,1)S(1)}, u32[]{:S(2)}, u32[]{:S(2)}) %collective-permute-start.33) | collective-permute-done | bytes 163872 | tf_op jit(solution)/shard_map/ppermute | solution.py:477
  112.9 2.2 %collective-permute-start.39 = (bf16[64,512]{1,0:T(8,128)(2,1)S(1)}, bf16[64,512]{1,0:T(8,128)(2,1)S(1)}, u32[]{:S(2)}, u32[]{:S(2)}) collective-permute-start(bf16[64,512]{1,0:T(8,128)(2,1)S(1)} %get-tuple-element.142), channel_id=1, source_target_pairs={{0,4},{1,5},{2,6},{3,7},{4,0},{5,1},{6,2},{7,3},{8,12},{9,13},{10,... | collective-permute-start | bytes 196616 | tf_op jit(solution)/shard_map/ppermute | solution.py:477
  115.0 1.4 %collective-permute-start.36 = (bf16[64,1280]{1,0:T(8,128)(2,1)S(1)}, bf16[64,1280]{1,0:T(8,128)(2,1)S(1)}, u32[]{:S(2)}, u32[]{:S(2)}) collective-permute-start(bf16[64,1280]{1,0:T(8,128)(2,1)S(1)} %add_convert_fusion.3), channel_id=1, source_target_pairs={{0,16},{8,24},{16,0},{24,8},{1,17},{9,25},{17,1},{25,9},{2,18},{10... | collective-permute-start | bytes 491528 | tf_op jit(solution)/shard_map/ppermute | solution.py:477
  117.8 2.1 %collective-permute-done.39 = bf16[64,512]{1,0:T(8,128)(2,1)S(1)} collective-permute-done((bf16[64,512]{1,0:T(8,128)(2,1)S(1)}, bf16[64,512]{1,0:T(8,128)(2,1)S(1)}, u32[]{:S(2)}, u32[]{:S(2)}) %collective-permute-start.39) | collective-permute-done | bytes 65568 | tf_op jit(solution)/shard_map/ppermute | solution.py:477
  121.1 1.5 %collective-permute-start.30 = (bf16[80,384]{1,0:T(8,128)(2,1)S(1)}, bf16[80,384]{1,0:T(8,128)(2,1)S(1)}, u32[]{:S(2)}, u32[]{:S(2)}) collective-permute-start(bf16[80,384]{1,0:T(8,128)(2,1)S(1)} %reduce_sum.12.a), channel_id=1, source_target_pairs={{0,16},{8,24},{16,0},{24,8},{1,17},{9,25},{17,1},{25,9},{2,18},{10... | collective-permute-start | bytes 184328 | tf_op jit(solution)/shard_map/ppermute | solution.py:477
  123.7 1.7 %collective-permute-done.30.c = bf16[80,384]{1,0:T(8,128)(2,1)S(1)} collective-permute-done((bf16[80,384]{1,0:T(8,128)(2,1)S(1)}, bf16[80,384]{1,0:T(8,128)(2,1)S(1)}, u32[]{:S(2)}, u32[]{:S(2)}) %collective-permute-start.30) | collective-permute-done | bytes 61472 | tf_op jit(solution)/shard_map/ppermute | solution.py:477
  125.4 1.9 %fusion.1 = f32[1,256,512]{2,1,0:T(8,128)} fusion(f32[256,512]{1,0:T(8,128)S(1)} %get-tuple-element.86, bf16[256,512]{1,0:T(8,128)(2,1)S(1)} %collective-permute-done.27, bf16[2,256,512]{2,1,0:T(8,128)(2,1)} %copy-done.4, bf16[2,256,512]{2,1,0:T(8,128)(2,1)S(1)} %get-tuple-element.107), kind=kLoop, calls=%fused_computation.5 | loop fusion | flops 786432 | bytes 1835008 | tf_op jit(solution)/shard_map/reshape | solution.py:743
  129.3 1.6 %shard_map.312 = (f32[64,512]{1,0:T(8,128)}, f32[64,2048]{1,0:T(8,128)}, f32[256,512]{1,0:T(8,128)}) custom-call(s32[4]{0:T(128)S(1)} %copy-done.2, bf16[64,1280]{1,0:T(8,128)(2,1)S(1)} %add_convert_fusion.3, bf16[64,1280]{1,0:T(8,128)(2,1)S(1)} %collective-permute-done.35.b, bf16[64,1280]{1,0:T(8,128)(2,1)S(1)} %collective-permute-done.36.c, ...), custom_call_target="tpu_custom_call" | custom-call | flops 1700000000 | bytes 5100000 | tf_op jit(solution)/shard_map/pallas_call | solution.py:40
  (92 shorter events, 23.3 us)
Async XLA Ops:
  3.3 10.0 %collective-permute-start.2 = (bf16[80,896]{1,0:T(8,128)(2,1)}, bf16[80,896]{1,0:T(8,128)(2,1)S(1)}, u32[]{:S(2)}, u32[]{:S(2)}) collective-permute-start(bf16[80,896]{1,0:T(8,128)(2,1)} %get-tuple-element.75), channel_id=1, source_target_pairs={{0,6},{1,7},{2,4},{3,5},{4,2},{5,3},{6,0},{7,1},{8,14},{9,15},{10,... | collective-permute-start | bytes 430088 | tf_op jit(solution)/shard_map/ppermute | solution.py:477
  8.4 12.3 %collective-permute-start.1 = (bf16[80,896]{1,0:T(8,128)(2,1)}, bf16[80,896]{1,0:T(8,128)(2,1)S(1)}, u32[]{:S(2)}, u32[]{:S(2)}) collective-permute-start(bf16[80,896]{1,0:T(8,128)(2,1)} %get-tuple-element.75), channel_id=1, source_target_pairs={{0,4},{1,5},{2,6},{3,7},{4,0},{5,1},{6,2},{7,3},{8,12},{9,13},{10,... | collective-permute-start | bytes 430088 | tf_op jit(solution)/shard_map/ppermute | solution.py:477
  8.4 12.3 %collective-permute-start = (bf16[80,896]{1,0:T(8,128)(2,1)}, bf16[80,896]{1,0:T(8,128)(2,1)S(1)}, u32[]{:S(2)}, u32[]{:S(2)}) collective-permute-start(bf16[80,896]{1,0:T(8,128)(2,1)} %get-tuple-element.75), channel_id=1, source_target_pairs={{0,2},{1,3},{2,0},{3,1},{4,6},{5,7},{6,4},{7,5},{8,10},{9,11},{10,... | collective-permute-start | bytes 430088 | tf_op jit(solution)/shard_map/ppermute | solution.py:477
  21.8 15.3 %collective-permute-start.4 = (bf16[576,512]{1,0:T(8,128)(2,1)S(1)}, bf16[576,512]{1,0:T(8,128)(2,1)S(1)}, u32[]{:S(2)}, u32[]{:S(2)}) collective-permute-start(bf16[576,512]{1,0:T(8,128)(2,1)S(1)} %pad_maximum_fusion), channel_id=1, source_target_pairs={{0,16},{8,24},{16,0},{24,8},{1,17},{9,25},{17,1},{25,9},{2,18},{10... | collective-permute-start | bytes 1769480 | tf_op jit(solution)/shard_map/ppermute | solution.py:477
  23.4 13.8 %collective-permute-start.5 = (bf16[4,80,896]{2,1,0:T(8,128)(2,1)S(1)}, bf16[4,80,896]{2,1,0:T(8,128)(2,1)S(1)}, u32[]{:S(2)}, u32[]{:S(2)}) collective-permute-start(bf16[4,80,896]{2,1,0:T(8,128)(2,1)S(1)} %pad_maximum_fusion.1.refs_4_.refs_6_.refs_13_), channel_id=1, source_target_pairs={{0,1},{1,0},{2,3},{3,2},{4,5},{5,4},{6,7},{7,6},{8,9},{9,8},{10,11... | collective-permute-start | bytes 1720328 | tf_op jit(solution)/shard_map/ppermute | solution.py:477
  24.9 12.7 %collective-permute-start.15 = (bf16[128,512]{1,0:T(8,128)(2,1)S(1)}, bf16[128,512]{1,0:T(8,128)(2,1)S(1)}, u32[]{:S(2)}, u32[]{:S(2)}) collective-permute-start(bf16[128,512]{1,0:T(8,128)(2,1)S(1)} %copy-done.5), channel_id=1, source_target_pairs={{0,6},{1,7},{2,4},{3,5},{4,2},{5,3},{6,0},{7,1},{8,14},{9,15},{10,... | collective-permute-start | bytes 393224 | tf_op jit(solution)/shard_map/ppermute | solution.py:477
  27.4 10.2 %collective-permute-start.14 = (bf16[128,512]{1,0:T(8,128)(2,1)S(1)}, bf16[128,512]{1,0:T(8,128)(2,1)S(1)}, u32[]{:S(2)}, u32[]{:S(2)}) collective-permute-start(bf16[128,512]{1,0:T(8,128)(2,1)S(1)} %copy-done.5), channel_id=1, source_target_pairs={{0,4},{1,5},{2,6},{3,7},{4,0},{5,1},{6,2},{7,3},{8,12},{9,13},{10,... | collective-permute-start | bytes 393224 | tf_op jit(solution)/shard_map/ppermute | solution.py:477
  27.4 10.2 %collective-permute-start.13 = (bf16[128,512]{1,0:T(8,128)(2,1)S(1)}, bf16[128,512]{1,0:T(8,128)(2,1)S(1)}, u32[]{:S(2)}, u32[]{:S(2)}) collective-permute-start(bf16[128,512]{1,0:T(8,128)(2,1)S(1)} %copy-done.5), channel_id=1, source_target_pairs={{0,2},{1,3},{2,0},{3,1},{4,6},{5,7},{6,4},{7,5},{8,10},{9,11},{10,... | collective-permute-start | bytes 393224 | tf_op jit(solution)/shard_map/ppermute | solution.py:477
  37.7 13.9 %collective-permute-start.16 = (bf16[4,128,512]{2,1,0:T(8,128)(2,1)S(1)}, bf16[4,128,512]{2,1,0:T(8,128)(2,1)S(1)}, u32[]{:S(2)}, u32[]{:S(2)}) collective-permute-start(bf16[4,128,512]{2,1,0:T(8,128)(2,1)S(1)} %pad_maximum_fusion.2.refs_14_), channel_id=1, source_target_pairs={{0,1},{1,0},{2,3},{3,2},{4,5},{5,4},{6,7},{7,6},{8,9},{9,8},{10,11... | collective-permute-start | bytes 1572872 | tf_op jit(solution)/shard_map/ppermute | solution.py:477
  39.4 12.8 %collective-permute-start.11 = (bf16[4,80,512]{2,1,0:T(8,128)(2,1)S(1)}, bf16[4,80,512]{2,1,0:T(8,128)(2,1)S(1)}, u32[]{:S(2)}, u32[]{:S(2)}) collective-permute-start(bf16[4,80,512]{2,1,0:T(8,128)(2,1)S(1)} %slice.97), channel_id=1, source_target_pairs={{0,16},{8,24},{16,0},{24,8},{1,17},{9,25},{17,1},{25,9},{2,18},{10... | collective-permute-start | bytes 983048 | tf_op jit(solution)/shard_map/ppermute | solution.py:477
  45.3 6.3 %collective-permute-start.8 = (bf16[256,128]{1,0:T(8,128)(2,1)S(1)}, bf16[256,128]{1,0:T(8,128)(2,1)S(1)}, u32[]{:S(2)}, u32[]{:S(2)}) collective-permute-start(bf16[256,128]{1,0:T(8,128)(2,1)S(1)} %get-tuple-element.79), channel_id=1, source_target_pairs={{0,16},{8,24},{16,0},{24,8},{1,17},{9,25},{17,1},{25,9},{2,18},{10... | collective-permute-start | bytes 196616 | tf_op jit(solution)/shard_map/ppermute | solution.py:477
  46.9 4.8 %collective-permute-start.9 = (bf16[256,128]{1,0:T(8,128)(2,1)S(1)}, bf16[256,128]{1,0:T(8,128)(2,1)S(1)}, u32[]{:S(2)}, u32[]{:S(2)}) collective-permute-start(bf16[256,128]{1,0:T(8,128)(2,1)S(1)} %get-tuple-element.80), channel_id=1, source_target_pairs={{0,24},{8,16},{16,8},{24,0},{1,25},{9,17},{17,9},{25,1},{2,26},{10... | collective-permute-start | bytes 196616 | tf_op jit(solution)/shard_map/ppermute | solution.py:477
  46.9 5.8 %collective-permute-start.17 = (bf16[4,128,512]{2,1,0:T(8,128)(2,1)S(1)}, bf16[4,128,512]{2,1,0:T(8,128)(2,1)S(1)}, u32[]{:S(2)}, u32[]{:S(2)}) collective-permute-start(bf16[4,128,512]{2,1,0:T(8,128)(2,1)S(1)} %pad_maximum_fusion.2.refs_14_), channel_id=1, source_target_pairs={{0,8},{8,0},{16,24},{24,16},{1,9},{9,1},{17,25},{25,17},{2,10},{10... | collective-permute-start | bytes 1572872 | tf_op jit(solution)/shard_map/ppermute | solution.py:477
  61.2 5.0 %collective-permute-start.23 = (bf16[256,1536]{1,0:T(8,128)(2,1)S(1)}, bf16[256,1536]{1,0:T(8,128)(2,1)S(1)}, u32[]{:S(2)}, u32[]{:S(2)}) collective-permute-start(bf16[256,1536]{1,0:T(8,128)(2,1)S(1)} %get-tuple-element.97), channel_id=1, source_target_pairs={{0,8},{8,0},{16,24},{24,16},{1,9},{9,1},{17,25},{25,17},{2,10},{10... | collective-permute-start | bytes 2359304 | tf_op jit(solution)/shard_map/ppermute | solution.py:477
  61.6 9.5 %collective-permute-start.19 = (bf16[256,128]{1,0:T(8,128)(2,1)S(1)}, bf16[256,128]{1,0:T(8,128)(2,1)S(1)}, u32[]{:S(2)}, u32[]{:S(2)}) collective-permute-start(bf16[256,128]{1,0:T(8,128)(2,1)S(1)} %get-tuple-element.88), channel_id=1, source_target_pairs={{0,8},{8,0},{16,24},{24,16},{1,9},{9,1},{17,25},{25,17},{2,10},{10... | collective-permute-start | bytes 196616 | tf_op jit(solution)/shard_map/ppermute | solution.py:477
  61.7 9.3 %collective-permute-start.20 = (bf16[256,128]{1,0:T(8,128)(2,1)S(1)}, bf16[256,128]{1,0:T(8,128)(2,1)S(1)}, u32[]{:S(2)}, u32[]{:S(2)}) collective-permute-start(bf16[256,128]{1,0:T(8,128)(2,1)S(1)} %get-tuple-element.89), channel_id=1, source_target_pairs={{0,16},{8,24},{16,0},{24,8},{1,17},{9,25},{17,1},{25,9},{2,18},{10... | collective-permute-start | bytes 196616 | tf_op jit(solution)/shard_map/ppermute | solution.py:477
  62.3 8.7 %collective-permute-start.21 = (bf16[256,128]{1,0:T(8,128)(2,1)S(1)}, bf16[256,128]{1,0:T(8,128)(2,1)S(1)}, u32[]{:S(2)}, u32[]{:S(2)}) collective-permute-start(bf16[256,128]{1,0:T(8,128)(2,1)S(1)} %get-tuple-element.90), channel_id=1, source_target_pairs={{0,24},{8,16},{16,8},{24,0},{1,25},{9,17},{17,9},{25,1},{2,26},{10... | collective-permute-start | bytes 196616 | tf_op jit(solution)/shard_map/ppermute | solution.py:477
  68.9 14.3 %collective-permute-start.25 = (bf16[8,64,512]{2,1,0:T(8,128)(2,1)}, bf16[8,64,512]{2,1,0:T(8,128)(2,1)}, u32[]{:S(2)}, u32[]{:S(2)}) collective-permute-start(bf16[8,64,512]{2,1,0:T(8,128)(2,1)} %get-tuple-element.109), channel_id=1, source_target_pairs={{0,16},{8,24},{16,0},{24,8},{1,17},{9,25},{17,1},{25,9},{2,18},{10... | collective-permute-start | bytes 1572872 | tf_op jit(solution)/shard_map/ppermute | solution.py:477
  69.5 19.2 %collective-permute-start.24 = (bf16[4,64,1280]{2,1,0:T(8,128)(2,1)S(1)}, bf16[4,64,1280]{2,1,0:T(8,128)(2,1)}, u32[]{:S(2)}, u32[]{:S(2)}) collective-permute-start(bf16[4,64,1280]{2,1,0:T(8,128)(2,1)S(1)} %get-tuple-element.106), channel_id=1, source_target_pairs={{0,1},{1,0},{2,3},{3,2},{4,5},{5,4},{6,7},{7,6},{8,9},{9,8},{10,11... | collective-permute-start | bytes 1966088 | tf_op jit(solution)/shard_map/ppermute | solution.py:477
  78.5 41.5 %all-to-all-start = ((bf16[8,80,384]{2,1,0:T(8,128)(2,1)}), bf16[8,80,384]{2,1,0:T(8,128)(2,1)}, u32[]{:S(2)}, u32[]{:S(2)}) async-start(bf16[8,80,384]{2,1,0:T(8,128)(2,1)} %get-tuple-element.111), calls=%async_computation | async-start | bytes 983040 | tf_op jit(solution)/shard_map/all_to_all | solution.py:676
  83.2 10.3 %collective-permute-start.26 = (bf16[2,256,512]{2,1,0:T(8,128)(2,1)S(1)}, bf16[2,256,512]{2,1,0:T(8,128)(2,1)S(1)}, u32[]{:S(2)}, u32[]{:S(2)}) collective-permute-start(bf16[2,256,512]{2,1,0:T(8,128)(2,1)S(1)} %get-tuple-element.110), channel_id=1, source_target_pairs={{0,8},{8,0},{16,24},{24,16},{1,9},{9,1},{17,25},{25,17},{2,10},{10... | collective-permute-start | bytes 1572872 | tf_op jit(solution)/shard_map/ppermute | solution.py:477
  84.3 27.1 %collective-permute-start.28 = (bf16[4,64,512]{2,1,0:T(8,128)(2,1)S(1)}, bf16[4,64,512]{2,1,0:T(8,128)(2,1)S(1)}, u32[]{:S(2)}, u32[]{:S(2)}) collective-permute-start(bf16[4,64,512]{2,1,0:T(8,128)(2,1)S(1)} %get-tuple-element.143), channel_id=1, source_target_pairs={{0,1},{1,0},{2,3},{3,2},{4,5},{5,4},{6,7},{7,6},{8,9},{9,8},{10,11... | collective-permute-start | bytes 786440 | tf_op jit(solution)/shard_map/ppermute | solution.py:477
  89.9 5.9 %collective-permute-start.32 = (bf16[64,1280]{1,0:T(8,128)(2,1)S(1)}, bf16[64,1280]{1,0:T(8,128)(2,1)S(1)}, u32[]{:S(2)}, u32[]{:S(2)}) collective-permute-start(bf16[64,1280]{1,0:T(8,128)(2,1)S(1)} %get-tuple-element.137), channel_id=1, source_target_pairs={{0,2},{1,3},{2,0},{3,1},{4,6},{5,7},{6,4},{7,5},{8,10},{9,11},{10,... | collective-permute-start | bytes 491528 | tf_op jit(solution)/shard_map/ppermute | solution.py:477
  89.9 13.3 %collective-permute-start.34 = (bf16[64,1280]{1,0:T(8,128)(2,1)S(1)}, bf16[64,1280]{1,0:T(8,128)(2,1)S(1)}, u32[]{:S(2)}, u32[]{:S(2)}) collective-permute-start(bf16[64,1280]{1,0:T(8,128)(2,1)S(1)} %get-tuple-element.138), channel_id=1, source_target_pairs={{0,6},{1,7},{2,4},{3,5},{4,2},{5,3},{6,0},{7,1},{8,14},{9,15},{10,... | collective-permute-start | bytes 491528 | tf_op jit(solution)/shard_map/ppermute | solution.py:477
  92.5 17.8 %collective-permute-start.33 = (bf16[64,1280]{1,0:T(8,128)(2,1)S(1)}, bf16[64,1280]{1,0:T(8,128)(2,1)S(1)}, u32[]{:S(2)}, u32[]{:S(2)}) collective-permute-start(bf16[64,1280]{1,0:T(8,128)(2,1)S(1)} %get-tuple-element.139), channel_id=1, source_target_pairs={{0,4},{1,5},{2,6},{3,7},{4,0},{5,1},{6,2},{7,3},{8,12},{9,13},{10,... | collective-permute-start | bytes 491528 | tf_op jit(solution)/shard_map/ppermute | solution.py:477
  93.5 17.9 %collective-permute-start.27 = (bf16[256,512]{1,0:T(8,128)(2,1)S(1)}, bf16[256,512]{1,0:T(8,128)(2,1)S(1)}, u32[]{:S(2)}, u32[]{:S(2)}) collective-permute-start(bf16[256,512]{1,0:T(8,128)(2,1)S(1)} %fusion.2), channel_id=1, source_target_pairs={{0,16},{8,24},{16,0},{24,8},{1,17},{9,25},{17,1},{25,9},{2,18},{10... | collective-permute-start | bytes 786440 | tf_op jit(solution)/shard_map/ppermute | solution.py:477
  111.5 5.0 %collective-permute-start.38 = (bf16[64,512]{1,0:T(8,128)(2,1)S(1)}, bf16[64,512]{1,0:T(8,128)(2,1)S(1)}, u32[]{:S(2)}, u32[]{:S(2)}) collective-permute-start(bf16[64,512]{1,0:T(8,128)(2,1)S(1)} %get-tuple-element.140), channel_id=1, source_target_pairs={{0,2},{1,3},{2,0},{3,1},{4,6},{5,7},{6,4},{7,5},{8,10},{9,11},{10,... | collective-permute-start | bytes 196616 | tf_op jit(solution)/shard_map/ppermute | solution.py:477
  111.6 6.2 %collective-permute-start.40 = (bf16[64,512]{1,0:T(8,128)(2,1)S(1)}, bf16[64,512]{1,0:T(8,128)(2,1)S(1)}, u32[]{:S(2)}, u32[]{:S(2)}) collective-permute-start(bf16[64,512]{1,0:T(8,128)(2,1)S(1)} %get-tuple-element.141), channel_id=1, source_target_pairs={{0,6},{1,7},{2,4},{3,5},{4,2},{5,3},{6,0},{7,1},{8,14},{9,15},{10,... | collective-permute-start | bytes 196616 | tf_op jit(solution)/shard_map/ppermute | solution.py:477
  112.9 7.1 %collective-permute-start.39 = (bf16[64,512]{1,0:T(8,128)(2,1)S(1)}, bf16[64,512]{1,0:T(8,128)(2,1)S(1)}, u32[]{:S(2)}, u32[]{:S(2)}) collective-permute-start(bf16[64,512]{1,0:T(8,128)(2,1)S(1)} %get-tuple-element.142), channel_id=1, source_target_pairs={{0,4},{1,5},{2,6},{3,7},{4,0},{5,1},{6,2},{7,3},{8,12},{9,13},{10,... | collective-permute-start | bytes 196616 | tf_op jit(solution)/shard_map/ppermute | solution.py:477
  115.0 7.5 %collective-permute-start.36 = (bf16[64,1280]{1,0:T(8,128)(2,1)S(1)}, bf16[64,1280]{1,0:T(8,128)(2,1)S(1)}, u32[]{:S(2)}, u32[]{:S(2)}) collective-permute-start(bf16[64,1280]{1,0:T(8,128)(2,1)S(1)} %add_convert_fusion.3), channel_id=1, source_target_pairs={{0,16},{8,24},{16,0},{24,8},{1,17},{9,25},{17,1},{25,9},{2,18},{10... | collective-permute-start | bytes 491528 | tf_op jit(solution)/shard_map/ppermute | solution.py:477
  122.6 6.6 %collective-permute-start.35 = (bf16[64,1280]{1,0:T(8,128)(2,1)S(1)}, bf16[64,1280]{1,0:T(8,128)(2,1)S(1)}, u32[]{:S(2)}, u32[]{:S(2)}) collective-permute-start(bf16[64,1280]{1,0:T(8,128)(2,1)S(1)} %add_convert_fusion.3), channel_id=1, source_target_pairs={{0,8},{8,0},{16,24},{24,16},{1,9},{9,1},{17,25},{25,17},{2,10},{10... | collective-permute-start | bytes 491528 | tf_op jit(solution)/shard_map/ppermute | solution.py:477
  122.6 6.6 %collective-permute-start.37 = (bf16[64,1280]{1,0:T(8,128)(2,1)S(1)}, bf16[64,1280]{1,0:T(8,128)(2,1)S(1)}, u32[]{:S(2)}, u32[]{:S(2)}) collective-permute-start(bf16[64,1280]{1,0:T(8,128)(2,1)S(1)} %collective-permute-done.36.c), channel_id=1, source_target_pairs={{0,8},{8,0},{16,24},{24,16},{1,9},{9,1},{17,25},{25,17},{2,10},{10... | collective-permute-start | bytes 491528 | tf_op jit(solution)/shard_map/ppermute | solution.py:477
  (19 other events, 135.5 us)

commit v4 on v3

--- a/solution.py
+++ b/solution.py
@@ -193,18 +193,12 @@
     return inverse * (grad - first_mean - normed * cross_mean)
 
 
-def gelu(values):
-    inner = GELU_ROOT * (values + GELU_CUBIC * values * values * values)
-    return 0.5 * values * (1.0 + jnp.tanh(inner))
-
-
-def gelu_slope(values):
+def gelu_and_slope(values):
     square = values * values
-    inner = GELU_ROOT * (values + GELU_CUBIC * values * square)
-    tanh_part = jnp.tanh(inner)
-    return 0.5 * (1.0 + tanh_part) + 0.5 * values * (1.0 - tanh_part * tanh_part) * GELU_ROOT * (
-        1.0 + 3.0 * GELU_CUBIC * square
-    )
+    tanh_part = jnp.tanh(values * (GELU_ROOT + (GELU_ROOT * GELU_CUBIC) * square))
+    half = 0.5 + 0.5 * tanh_part
+    bend = values * (0.5 * GELU_ROOT + (1.5 * GELU_ROOT * GELU_CUBIC) * square)
+    return (values * half).astype(BF), half + bend * (1.0 - tanh_part * tanh_part)
 
 
 def column_sum(values):
@@ -216,7 +210,7 @@
     even_parts, odd_parts, down_parts = refs[8:11], refs[11:14], refs[14:18]
     out, ems, e1_out = refs[18], refs[19:23], refs[23]
     keep1, ship1, keep2, ship2, vg_out = refs[24:29]
-    wo, up, down, first, second, z_s, em_s, m_s, u_s, ez_s, ea_s, rows0, rows1 = refs[29:]
+    wo, up, down, first, second, slopes, em_s, m_s, u_s, ez_s, ea_s, rows0, rows1 = refs[29:]
     f, s, c, x = idx[0], idx[1], idx[2], idx[3]
     for k in range(4):
         row = (c ^ (k & 1)) * 32 + (x ^ (k >> 1)) * 16
@@ -259,8 +253,7 @@
     for j in range(4):
         columns = slice(j * 512, (j + 1) * 512)
         z = dot_nn(y, up[:, columns]) + up_bias[:, columns]
-        z_s[:, columns] = z
-        u = gelu(z).astype(BF)
+        u, slopes[:, columns] = gelu_and_slope(z)
         for one in range(2):
             owner = 2 * j + one
             for half in range(2):
@@ -280,7 +273,7 @@
     for j in range(4):
         columns = slice(j * 512, (j + 1) * 512)
         eu = dot_nt(eb, down[columns, :]).astype(BF).astype(F32)
-        ez = (eu * gelu_slope(z_s[:, columns])).astype(BF)
+        ez = (eu * slopes[:, columns]).astype(BF)
         ez_s[j // 2, :, (j % 2) * 512 : (j % 2 + 1) * 512] = ez
         up_bias_grads.append(column_sum(ez))
         ey = ey + dot_nt(ez, up[:, columns])
@@ -316,43 +309,38 @@
 
 def down_grad_kernel(idx, mine, other, even, odd, send):
     f, x = idx[0], idx[3]
-    for pair in range(PARTS // 2):
-        columns = slice(pair * 256, (pair + 1) * 256)
-        made = dot_tn(mine[:, columns], mine[:, 1024:]) + dot_tn(other[:, columns], other[:, 1024:])
-        made = made.astype(BF)
-        for one in range(2):
-            slot = f ^ (2 * pair + one)
-            upper, lower = made[one * 128 : one * 128 + 64], made[one * 128 + 64 : one * 128 + 128]
-            kept, gone = jnp.where(x == 0, upper, lower), jnp.where(x == 0, lower, upper)
-            odd_slot = slot & 1
-            send[odd_slot * 4 + (slot >> 1)] = gone
-
-            @pl.when(odd_slot == 0)
-            def _():
-                even[slot >> 1] = kept
-
-            @pl.when(odd_slot == 1)
-            def _():
-                odd[slot >> 1] = kept
+    made = dot_tn(mine[:, :1024], mine[:, 1024:]) + dot_tn(other[:, :1024], other[:, 1024:])
+    made = made.astype(BF)
+    for owner in range(PARTS):
+        slot = f ^ owner
+        upper, lower = made[owner * 128 : owner * 128 + 64], made[owner * 128 + 64 : owner * 128 + 128]
+        kept, gone = jnp.where(x == 0, upper, lower), jnp.where(x == 0, lower, upper)
+        odd_slot = slot & 1
+        send[odd_slot * 4 + (slot >> 1)] = gone
+
+        @pl.when(odd_slot == 0)
+        def _():
+            even[slot >> 1] = kept
+
+        @pl.when(odd_slot == 1)
+        def _():
+            odd[slot >> 1] = kept
 
 
 def up_grad_kernel(idx, mine, other, even, odd):
     f = idx[0]
-    for pair in range(PARTS // 2):
-        columns = slice(1280 + pair * 128, 1280 + (pair + 1) * 128)
-        made_up = dot_tn(mine[:, columns], mine[:, :1024]) + dot_tn(other[:, columns], other[:, :1024])
-        columns = slice(1792 + pair * 128, 1792 + (pair + 1) * 128)
-        made_out = dot_tn(mine[:, columns], mine[:, 1024:1280]) + dot_tn(
-            other[:, columns], other[:, 1024:1280]
-        )
-        for one in range(2):
-            slot = f ^ (2 * pair + one)
-            for parity, to in ((0, even), (1, odd)):
-
-                @pl.when((slot & 1) == parity)
-                def _():
-                    to[slot >> 1, :, :1024] = made_up[one * 64 : (one + 1) * 64].astype(BF)
-                    to[slot >> 1, :, 1024:] = made_out[one * 64 : (one + 1) * 64].astype(BF)
+    made_up = dot_tn(mine[:, 1280:1792], mine[:, :1024]) + dot_tn(other[:, 1280:1792], other[:, :1024])
+    made_out = dot_tn(mine[:, 1792:], mine[:, 1024:1280]) + dot_tn(other[:, 1792:], other[:, 1024:1280])
+    made_up, made_out = made_up.astype(BF), made_out.astype(BF)
+    for owner in range(PARTS):
+        slot = f ^ owner
+        rows = slice(owner * 64, (owner + 1) * 64)
+        for parity, to in ((0, even), (1, odd)):
+
+            @pl.when((slot & 1) == parity)
+            def _():
+                to[slot >> 1, :, :1024] = made_up[rows]
+                to[slot >> 1, :, 1024:] = made_out[rows]
 
 
 def attend_back_kernel(idx, *refs):
@@ -461,8 +449,8 @@
     {
         attend_kernel: 0.5,
         middle_kernel: 10.2,
-        down_grad_kernel: 3.4,
-        up_grad_kernel: 4.0,
+        down_grad_kernel: 1.0,
+        up_grad_kernel: 1.0,
         attend_back_kernel: 9.3,
     }
 )
@@ -530,7 +518,6 @@
             return [piece] + [swap(piece, "fsdp", k) for k in (2, 4, 6)]
 
         mine = along_z(first_part)
-        down_part = after(down_part, mine[1])
         even = jnp.stack(mine)
         odd = swap(even, "fsdp", 1)
         shared = jnp.concatenate([even[:, :, 384:].reshape(320, 512), own])
@@ -636,7 +623,7 @@
         attend_back_kernel,
         [((2, part, width), BF)] * 2 + [((PARTS, 80, 384), BF)],
         index,
-        (*ems, after(qa, down_even), ka, v, m_heads, rinv, *xs, even, odd, vg),
+        (*ems, qa, ka, v, m_heads, rinv, *xs, even, odd, vg),
         scratch=(
             ((512, 384), BF),
             ((total, 128), BF),
@@ -648,7 +635,6 @@
     )
 
     down_got = swap(down_send, "seq", 2)
-    dx_send, down_got = lax.optimization_barrier((dx_send, down_got))
     got = swap(dx_send, "seq", 1)
     if direct:
         up_got = swap(up_odd_grad, "fsdp", 1)
@@ -662,22 +648,20 @@
             across = swap(mine, "seq", 2)
             return mine, swap(mine, "seq", 1), across, swap(across, "seq", 1)
 
-        def cross(values):
-            return [swap(values[k >> 1], "fsdp", k) for k in (2, 4, 6)]
-
-        up_sums = [plus(up_even_grad[k], up_got[k]) for k in range(4)]
-        down_got = after(down_got, dx_send)
+        def near(stay, got):
+            came = swap(plus(stay[1::2], got[1::2]), "fsdp", 2)
+            return plus(stay[2], got[2], came[1]), (stay[0], got[0], came[0])
+
         down_far = swap(plus(down_odd, down_got[4:]), "fsdp", 1)
         down_stay = plus(down_even, down_got[:4])
-        down_far = after(down_far, *up_sums, far)
-        down_sums = [plus(down_stay[k], down_far[k]) for k in range(4)]
-        up_far = cross(up_sums)
-        down_far = cross(down_sums)
-        w_made = after(lax.all_to_all(w_grad, "fsdp", 0, 0, tiled=True), *down_sums)
+        up_away, up_here = near(up_even_grad, after(up_got, got))
+        down_far = after(down_far, far)
+        down_away, down_here = near(down_stay, down_far)
+        up_far = swap(up_away, "fsdp", 4)
+        down_far = swap(down_away, "fsdp", 4)
+        w_made = after(lax.all_to_all(w_grad, "fsdp", 0, 0, tiled=True), up_away)
         w_made = jnp.sum(w_made.astype(F32), axis=0).astype(BF)
         w_all = spread_out(w_made)
-        up_all = spread_out(plus(up_sums[0], *up_far))
-        down_all = spread_out(plus(down_sums[0], *down_far))
         (
             wq_grad,
             wk_grad,
@@ -697,6 +681,8 @@
             index,
             w_all,
         )
+        up_all = spread_out(plus(*up_here, after(up_far, input_grad, w_made)))
+        down_all = spread_out(plus(*down_here, down_far))
         out_grad, up_grad, down_grad = run(
             end_wide_kernel,
             [((64, 512), F32), ((64, 2048), F32), ((256, 512), F32)],

time: 131 us -> 123 us (0.939)
  waiting for transfers between devices: 49.9 us -> 42.5 us
  other arithmetic: 8.22 us -> 11.7 us
  starting transfers between devices: 42.7 us -> 40 us
  Pallas kernels: 29.1 us -> 27 us
    ppermute x44 -> x42, waiting for transfers between devices: 49.9 us -> 42.5 us  [swap(): return lax.ppermute(values, axis, [(i, i ^ step) for i in range(size)])]
    convert_element_type x6 -> x8, other arithmetic: 3.55 us -> 6.99 us  [plus(): return functools.reduce(jnp.add, [t.astype(F32) for t in terms]).astype(BF)]
    ppermute x44 -> x42, starting transfers between devices: 38.5 us -> 35.9 us  [swap(): return lax.ppermute(values, axis, [(i, i ^ step) for i in range(size)])]
    pallas_call x8, Pallas kernels: 29.1 us -> 27 us  [run(): pl.pallas_call(kernel, out_shape=outs, in_specs=[SMEM] + [VMEM] * len(arg...]
    reshape x1 -> x0, other arithmetic: 1.88 us -> none  [body(): input_grad.reshape(inputs.shape)]
    add x0 -> x1, other arithmetic: none -> 1.88 us  [body(): e1 + (dx_keep[0].astype(F32) + got[0].astype(F32) + far.astype(F32))]
  transfers between devices with their start and end apart: 45 -> 43, of which waited for: 15 -> 14; matrix products, arithmetic and copies ran while one was open for 5% -> 8% of each run, Pallas kernels for 15% -> 14%
where the time goes in v4:
time: 123 us; the launch traced here: 122 us
  waiting for transfers between devices  42.5 us (35%)
  starting transfers between devices  40 us (33%)
  Pallas kernels  27 us (22%)
  other arithmetic  11.7 us (10%)
    ppermute x42, waiting for transfers between devices, swap(): return lax.ppermute(values, axis, [(i, i ^ step) for i in range(size)])  42.5 us
    ppermute x42, starting transfers between devices, swap(): return lax.ppermute(values, axis, [(i, i ^ step) for i in range(size)])  35.9 us
    pallas_call x8, Pallas kernels, run(): pl.pallas_call(kernel, out_shape=outs, in_specs=[SMEM] + [VMEM] * len(arg...  27 us
    convert_element_type x8, other arithmetic, plus(): return functools.reduce(jnp.add, [t.astype(F32) for t in terms]).astype(BF)  6.99 us
    all_to_all x1, starting transfers between devices, body(): w_made = after(lax.all_to_all(w_grad, 'fsdp', 0, 0, tiled=True), up_away)  4.12 us
  transfers between devices with their start and end apart: 43, of which 14 were waited for; matrix products, arithmetic and copies ran while one was open for 8% of the time, Pallas kernels for 14%

profile of v4, /device:TPU:0, one launch (start us, length us, event | category | flops | bytes accessed | tf_op | source)
XLA Modules:
  0.0 122.2 jit_solution(3690660719875923862)
XLA Ops:
  1.2 2.0 %shard_map.305 = (bf16[80,896]{1,0:T(8,128)(2,1)}, bf16[128,512]{1,0:T(8,128)(2,1)}) custom-call(s32[4]{0:T(128)} %pad_add_fusion.idx, bf16[64,512]{1,0:T(8,128)(2,1)} %wq.1, bf16[64,512]{1,0:T(8,128)(2,1)} %wk.1, bf16[64,512]{1,0:T(8,128)(2,1)} %wv.1, bf16[64,512]{1,0:T(8,128)(2,1)} %wo.1, bf16[64,2048]{1,0:T(8,128)(2,1)} %up.1, bf16[256,512]{1,0:T(8,128)(2,1)} %down.1, ...), custom_call_target="tpu_custom_call" | custom-call | flops 1700000000 | bytes 5100000 | tf_op jit(solution)/shard_map/pallas_call | solution.py:40
  3.3 5.1 %collective-permute-start.2 = (bf16[80,896]{1,0:T(8,128)(2,1)}, bf16[80,896]{1,0:T(8,128)(2,1)S(1)}, u32[]{:S(2)}, u32[]{:S(2)}) collective-permute-start(bf16[80,896]{1,0:T(8,128)(2,1)} %get-tuple-element.72), channel_id=1, source_target_pairs={{0,6},{1,7},{2,4},{3,5},{4,2},{5,3},{6,0},{7,1},{8,14},{9,15},{10,... | collective-permute-start | bytes 430088 | tf_op jit(solution)/shard_map/ppermute | solution.py:465
  9.0 4.3 %collective-permute-done.2 = bf16[80,896]{1,0:T(8,128)(2,1)S(1)} collective-permute-done((bf16[80,896]{1,0:T(8,128)(2,1)}, bf16[80,896]{1,0:T(8,128)(2,1)S(1)}, u32[]{:S(2)}, u32[]{:S(2)}) %collective-permute-start.2) | collective-permute-done | bytes 143392 | tf_op jit(solution)/shard_map/ppermute | solution.py:465
  13.3 7.4 %collective-permute-done.1 = bf16[80,896]{1,0:T(8,128)(2,1)S(1)} collective-permute-done((bf16[80,896]{1,0:T(8,128)(2,1)}, bf16[80,896]{1,0:T(8,128)(2,1)S(1)}, u32[]{:S(2)}, u32[]{:S(2)}) %collective-permute-start.1) | collective-permute-done | bytes 143392 | tf_op jit(solution)/shard_map/ppermute | solution.py:465
  21.8 1.6 %collective-permute-start.4 = (bf16[576,512]{1,0:T(8,128)(2,1)S(1)}, bf16[576,512]{1,0:T(8,128)(2,1)S(1)}, u32[]{:S(2)}, u32[]{:S(2)}) collective-permute-start(bf16[576,512]{1,0:T(8,128)(2,1)S(1)} %pad_maximum_fusion), channel_id=1, source_target_pairs={{0,16},{8,24},{16,0},{24,8},{1,17},{9,25},{17,1},{25,9},{2,18},{10... | collective-permute-start | bytes 1769480 | tf_op jit(solution)/shard_map/ppermute | solution.py:465
  23.4 1.5 %collective-permute-start.5 = (bf16[4,80,896]{2,1,0:T(8,128)(2,1)S(1)}, bf16[4,80,896]{2,1,0:T(8,128)(2,1)S(1)}, u32[]{:S(2)}, u32[]{:S(2)}) collective-permute-start(bf16[4,80,896]{2,1,0:T(8,128)(2,1)S(1)} %pad_maximum_fusion.1.refs_4_.refs_6_.refs_13_), channel_id=1, source_target_pairs={{0,1},{1,0},{2,3},{3,2},{4,5},{5,4},{6,7},{7,6},{8,9},{9,8},{10,11... | collective-permute-start | bytes 1720328 | tf_op jit(solution)/shard_map/ppermute | solution.py:465
  24.9 2.5 %collective-permute-start.15 = (bf16[128,512]{1,0:T(8,128)(2,1)S(1)}, bf16[128,512]{1,0:T(8,128)(2,1)S(1)}, u32[]{:S(2)}, u32[]{:S(2)}) collective-permute-start(bf16[128,512]{1,0:T(8,128)(2,1)S(1)} %copy-done.4), channel_id=1, source_target_pairs={{0,6},{1,7},{2,4},{3,5},{4,2},{5,3},{6,0},{7,1},{8,14},{9,15},{10,... | collective-permute-start | bytes 393224 | tf_op jit(solution)/shard_map/ppermute | solution.py:465
  27.4 1.9 %collective-permute-start.13 = (bf16[128,512]{1,0:T(8,128)(2,1)S(1)}, bf16[128,512]{1,0:T(8,128)(2,1)S(1)}, u32[]{:S(2)}, u32[]{:S(2)}) collective-permute-start(bf16[128,512]{1,0:T(8,128)(2,1)S(1)} %copy-done.4), channel_id=1, source_target_pairs={{0,2},{1,3},{2,0},{3,1},{4,6},{5,7},{6,4},{7,5},{8,10},{9,11},{10,... | collective-permute-start | bytes 393224 | tf_op jit(solution)/shard_map/ppermute | solution.py:465
  29.3 7.8 %collective-permute-done.5.refs_5_.refs_7_.refs_14_ = bf16[4,80,896]{2,1,0:T(8,128)(2,1)S(1)} collective-permute-done((bf16[4,80,896]{2,1,0:T(8,128)(2,1)S(1)}, bf16[4,80,896]{2,1,0:T(8,128)(2,1)S(1)}, u32[]{:S(2)}, u32[]{:S(2)}) %collective-permute-start.5) | collective-permute-done | bytes 573472 | tf_op jit(solution)/shard_map/ppermute | solution.py:465
  37.7 1.6 %collective-permute-start.16 = (bf16[4,128,512]{2,1,0:T(8,128)(2,1)S(1)}, bf16[4,128,512]{2,1,0:T(8,128)(2,1)S(1)}, u32[]{:S(2)}, u32[]{:S(2)}) collective-permute-start(bf16[4,128,512]{2,1,0:T(8,128)(2,1)S(1)} %pad_maximum_fusion.2.refs_14_), channel_id=1, source_target_pairs={{0,1},{1,0},{2,3},{3,2},{4,5},{5,4},{6,7},{7,6},{8,9},{9,8},{10,11... | collective-permute-start | bytes 1572872 | tf_op jit(solution)/shard_map/ppermute | solution.py:465
  40.0 5.3 %shard_map.306 = (bf16[256,128]{1,0:T(8,128)(2,1)S(1)}, bf16[256,128]{1,0:T(8,128)(2,1)S(1)}, bf16[256,128]{1,0:T(8,128)(2,1)S(1)}, bf16[256,128]{1,0:T(8,128)(2...) custom-call(s32[4]{0:T(128)S(1)} %copy-done.2, ...), custom_call_target="tpu_custom_call" | custom-call | flops 500000000 | bytes 1500000 | tf_op jit(solution)/shard_map/pallas_call | solution.py:40
  45.3 1.6 %collective-permute-start.8 = (bf16[256,128]{1,0:T(8,128)(2,1)S(1)}, bf16[256,128]{1,0:T(8,128)(2,1)S(1)}, u32[]{:S(2)}, u32[]{:S(2)}) collective-permute-start(bf16[256,128]{1,0:T(8,128)(2,1)S(1)} %get-tuple-element.76), channel_id=1, source_target_pairs={{0,16},{8,24},{16,0},{24,8},{1,17},{9,25},{17,1},{25,9},{2,18},{10... | collective-permute-start | bytes 196616 | tf_op jit(solution)/shard_map/ppermute | solution.py:465
  47.5 4.1 %collective-permute-done.16.refs_15_ = bf16[4,128,512]{2,1,0:T(8,128)(2,1)S(1)} collective-permute-done((bf16[4,128,512]{2,1,0:T(8,128)(2,1)S(1)}, bf16[4,128,512]{2,1,0:T(8,128)(2,1)S(1)}, u32[]{:S(2)}, u32[]{:S(2)}) %collective-permute-start.16) | collective-permute-done | bytes 524320 | tf_op jit(solution)/shard_map/ppermute | solution.py:465
  54.6 5.9 %shard_map.307 = (bf16[256,512]{1,0:T(8,128)(2,1)}, bf16[256,128]{1,0:T(8,128)(2,1)S(1)}, bf16[256,128]{1,0:T(8,128)(2,1)S(1)}, bf16[256,128]{1,0:T(8,128)(2,1)S...) custom-call(s32[4]{0:T(128)S(1)} %copy-done.2, ...), custom_call_target="tpu_custom_call" | custom-call | flops 10200000512 | bytes 30600000 | tf_op jit(solution)/shard_map/pallas_call | solution.py:40
  63.4 1.8 %shard_map.309 = (bf16[4,64,1280]{2,1,0:T(8,128)(2,1)S(1)}, bf16[4,64,1280]{2,1,0:T(8,128)(2,1)S(1)}) custom-call(s32[4]{0:T(128)S(1)} %copy-done.2, bf16[256,2304]{1,0:T(8,128)(2,1)S(1)} %get-tuple-element.94.mine, bf16[256,2304]{1,0:T(8,128)(2,1)S(1)} %collective-permute-done.22.other), custom_call_target="tpu_custom_call" | custom-call | flops 1000000000 | bytes 3000000 | tf_op jit(solution)/shard_map/pallas_call | solution.py:40
  65.2 1.4 %shard_map.311 = (bf16[4,64,512]{2,1,0:T(8,128)(2,1)S(1)}, bf16[4,64,512]{2,1,0:T(8,128)(2,1)S(1)}, bf16[8,64,512]{2,1,0:T(8,128)(2,1)S(1)}) custom-call(s32[4]{0:T(128)S(1)} %copy-done.2, bf16[256,1536]{1,0:T(8,128)(2,1)S(1)} %get-tuple-element.111.mine, bf16[256,1536]{1,0:T(8,128)(2,1)S(1)} %collective-permute-done.34.other), custom_call_target="tpu_custom_call" | custom-call | flops 1000000000 | bytes 3000000 | tf_op jit(solution)/shard_map/pallas_call | solution.py:40
  67.3 1.5 %collective-permute-start.23 = (bf16[4,64,1280]{2,1,0:T(8,128)(2,1)S(1)}, bf16[4,64,1280]{2,1,0:T(8,128)(2,1)}, u32[]{:S(2)}, u32[]{:S(2)}) collective-permute-start(bf16[4,64,1280]{2,1,0:T(8,128)(2,1)S(1)} %get-tuple-element.96), channel_id=1, source_target_pairs={{0,1},{1,0},{2,3},{3,2},{4,5},{5,4},{6,7},{7,6},{8,9},{9,8},{10,11... | collective-permute-start | bytes 1966088 | tf_op jit(solution)/shard_map/ppermute | solution.py:465
  68.9 7.6 %shard_map.308 = (bf16[2,256,512]{2,1,0:T(8,128)(2,1)S(1)}, bf16[2,256,512]{2,1,0:T(8,128)(2,1)}, bf16[8,80,384]{2,1,0:T(8,128)(2,1)}) custom-call(s32[4]{0:T(128)S(1)} %copy-done.2, bf16[256,128]{1,0:T(8,128)(2,1)S(1)} %get-tuple-element.83.refs_0_, bf16[256,128]{1,0:T(8,128)(2,1)S(1)} %collective-permute-done.19.refs_1_, ...), custom_call_target="tpu_custom_call" | custom-call | flops 9299999744 | bytes 27900000 | tf_op jit(solution)/shard_map/pallas_call | solution.py:40
  76.5 4.1 %all-to-all-start = ((bf16[8,80,384]{2,1,0:T(8,128)(2,1)}), bf16[8,80,384]{2,1,0:T(8,128)(2,1)}, u32[]{:S(2)}, u32[]{:S(2)}) async-start(bf16[8,80,384]{2,1,0:T(8,128)(2,1)} %get-tuple-element.99), calls=%async_computation | async-start | bytes 983040 | tf_op jit(solution)/shard_map/all_to_all | solution.py:662
  82.0 1.8 %collective-permute-start.36 = (bf16[4,64,512]{2,1,0:T(8,128)(2,1)S(1)}, bf16[4,64,512]{2,1,0:T(8,128)(2,1)S(1)}, u32[]{:S(2)}, u32[]{:S(2)}) collective-permute-start(bf16[4,64,512]{2,1,0:T(8,128)(2,1)S(1)} %get-tuple-element.128), channel_id=1, source_target_pairs={{0,1},{1,0},{2,3},{3,2},{4,5},{5,4},{6,7},{7,6},{8,9},{9,8},{10,11... | collective-permute-start | bytes 786440 | tf_op jit(solution)/shard_map/ppermute | solution.py:465
  83.7 1.6 %collective-permute-done.23 = bf16[4,64,1280]{2,1,0:T(8,128)(2,1)} collective-permute-done((bf16[4,64,1280]{2,1,0:T(8,128)(2,1)S(1)}, bf16[4,64,1280]{2,1,0:T(8,128)(2,1)}, u32[]{:S(2)}, u32[]{:S(2)}) %collective-permute-start.23) | collective-permute-done | bytes 655392 | tf_op jit(solution)/shard_map/ppermute | solution.py:465
  86.3 1.5 %collective-permute-start.25 = (bf16[256,512]{1,0:T(8,128)(2,1)S(1)}, bf16[256,512]{1,0:T(8,128)(2,1)S(1)}, u32[]{:S(2)}, u32[]{:S(2)}) collective-permute-start(bf16[256,512]{1,0:T(8,128)(2,1)S(1)} %fusion.2), channel_id=1, source_target_pairs={{0,16},{8,24},{16,0},{24,8},{1,17},{9,25},{17,1},{25,9},{2,18},{10... | collective-permute-start | bytes 786440 | tf_op jit(solution)/shard_map/ppermute | solution.py:465
  88.9 5.8 %collective-permute-done.36 = bf16[4,64,512]{2,1,0:T(8,128)(2,1)S(1)} collective-permute-done((bf16[4,64,512]{2,1,0:T(8,128)(2,1)S(1)}, bf16[4,64,512]{2,1,0:T(8,128)(2,1)S(1)}, u32[]{:S(2)}, u32[]{:S(2)}) %collective-permute-start.36) | collective-permute-done | bytes 262176 | tf_op jit(solution)/shard_map/ppermute | solution.py:465
  94.7 1.5 %collective-permute-start.37 = (bf16[2,64,512]{2,1,0:T(8,128)(2,1)S(1)}, bf16[2,64,512]{2,1,0:T(8,128)(2,1)}, u32[]{:S(2)}, u32[]{:S(2)}) collective-permute-start(bf16[2,64,512]{2,1,0:T(8,128)(2,1)S(1)} %add_convert_fusion.5), channel_id=1, source_target_pairs={{0,2},{1,3},{2,0},{3,1},{4,6},{5,7},{6,4},{7,5},{8,10},{9,11},{10,... | collective-permute-start | bytes 393224 | tf_op jit(solution)/shard_map/ppermute | solution.py:465
  96.2 1.9 %fusion = f32[256,512]{1,0:T(8,128)} fusion(f32[256,512]{1,0:T(8,128)S(1)} %get-tuple-element.82, bf16[256,512]{1,0:T(8,128)(2,1)S(1)} %collective-permute-done.25, bf16[2,256,512]{2,1,0:T(8,128)(2,1)} %collective-permute-done.24, bf16[2,256,512]{2,1,0:T(8,128)(2,1)S(1)} %get-tuple-element.97), kind=kLoop, calls=%fused_computation.5 | loop fusion | flops 786432 | bytes 1835008 | tf_op jit(solution)/shard_map/add | solution.py:643
  98.1 2.9 %collective-permute-done.26 = bf16[2,64,1280]{2,1,0:T(8,128)(2,1)S(1)} collective-permute-done((bf16[2,64,1280]{2,1,0:T(8,128)(2,1)S(1)}, bf16[2,64,1280]{2,1,0:T(8,128)(2,1)S(1)}, u32[]{:S(2)}, u32[]{:S(2)}) %collective-permute-start.26) | collective-permute-done | bytes 327712 | tf_op jit(solution)/shard_map/ppermute | solution.py:465
  106.1 1.8 %collective-permute-start.38 = (bf16[64,512]{1,0:T(8,128)(2,1)S(1)}, bf16[64,512]{1,0:T(8,128)(2,1)S(1)}, u32[]{:S(2)}, u32[]{:S(2)}) collective-permute-start(bf16[64,512]{1,0:T(8,128)(2,1)S(1)} %fusion.5), channel_id=1, source_target_pairs={{0,4},{1,5},{2,6},{3,7},{4,0},{5,1},{6,2},{7,3},{8,12},{9,13},{10,... | collective-permute-start | bytes 196616 | tf_op jit(solution)/shard_map/ppermute | solution.py:465
  107.9 3.3 %collective-permute-done.30 = bf16[64,1280]{1,0:T(8,128)(2,1)S(1)} collective-permute-done((bf16[64,1280]{1,0:T(8,128)(2,1)S(1)}, bf16[64,1280]{1,0:T(8,128)(2,1)S(1)}, u32[]{:S(2)}, u32[]{:S(2)}) %collective-permute-start.30) | collective-permute-done | bytes 163872 | tf_op jit(solution)/shard_map/ppermute | solution.py:465
  112.2 1.6 %collective-permute-start.32 = (bf16[64,1280]{1,0:T(8,128)(2,1)S(1)}, bf16[64,1280]{1,0:T(8,128)(2,1)S(1)}, u32[]{:S(2)}, u32[]{:S(2)}) collective-permute-start(bf16[64,1280]{1,0:T(8,128)(2,1)S(1)} %fusion.1.a), channel_id=1, source_target_pairs={{0,16},{8,24},{16,0},{24,8},{1,17},{9,25},{17,1},{25,9},{2,18},{10... | collective-permute-start | bytes 491528 | tf_op jit(solution)/shard_map/ppermute | solution.py:465
  116.0 2.4 %collective-permute-done.32.c = bf16[64,1280]{1,0:T(8,128)(2,1)S(1)} collective-permute-done((bf16[64,1280]{1,0:T(8,128)(2,1)S(1)}, bf16[64,1280]{1,0:T(8,128)(2,1)S(1)}, u32[]{:S(2)}, u32[]{:S(2)}) %collective-permute-start.32) | collective-permute-done | bytes 163872 | tf_op jit(solution)/shard_map/ppermute | solution.py:465
  119.1 1.4 %shard_map.310 = (f32[64,512]{1,0:T(8,128)}, f32[64,512]{1,0:T(8,128)}, f32[64,512]{1,0:T(8,128)}, f32[64]{0:T(128)}, f32[64]{0:T(128)}, /*index=5*/f32[64]{0:T(...) custom-call(s32[4]{0:T(128)S(1)} %copy-done.2, ...), custom_call_target="tpu_custom_call" | custom-call | flops 1700000000 | bytes 5100000 | tf_op jit(solution)/shard_map/pallas_call | solution.py:40
  120.5 1.6 %shard_map.312 = (f32[64,512]{1,0:T(8,128)}, f32[64,2048]{1,0:T(8,128)}, f32[256,512]{1,0:T(8,128)}) custom-call(s32[4]{0:T(128)S(1)} %copy-done.2, bf16[64,1280]{1,0:T(8,128)(2,1)S(1)} %fusion.1.a, bf16[64,1280]{1,0:T(8,128)(2,1)S(1)} %collective-permute-done.31.b, bf16[64,1280]{1,0:T(8,128)(2,1)S(1)} %collective-permute-done.32.c, ...), custom_call_target="tpu_custom_call" | custom-call | flops 1700000000 | bytes 5100000 | tf_op jit(solution)/shard_map/pallas_call | solution.py:40
  (88 shorter events, 23.2 us)
Async XLA Ops:
  3.3 10.0 %collective-permute-start.2 = (bf16[80,896]{1,0:T(8,128)(2,1)}, bf16[80,896]{1,0:T(8,128)(2,1)S(1)}, u32[]{:S(2)}, u32[]{:S(2)}) collective-permute-start(bf16[80,896]{1,0:T(8,128)(2,1)} %get-tuple-element.72), channel_id=1, source_target_pairs={{0,6},{1,7},{2,4},{3,5},{4,2},{5,3},{6,0},{7,1},{8,14},{9,15},{10,... | collective-permute-start | bytes 430088 | tf_op jit(solution)/shard_map/ppermute | solution.py:465
  8.4 12.3 %collective-permute-start.1 = (bf16[80,896]{1,0:T(8,128)(2,1)}, bf16[80,896]{1,0:T(8,128)(2,1)S(1)}, u32[]{:S(2)}, u32[]{:S(2)}) collective-permute-start(bf16[80,896]{1,0:T(8,128)(2,1)} %get-tuple-element.72), channel_id=1, source_target_pairs={{0,4},{1,5},{2,6},{3,7},{4,0},{5,1},{6,2},{7,3},{8,12},{9,13},{10,... | collective-permute-start | bytes 430088 | tf_op jit(solution)/shard_map/ppermute | solution.py:465
  8.4 12.3 %collective-permute-start = (bf16[80,896]{1,0:T(8,128)(2,1)}, bf16[80,896]{1,0:T(8,128)(2,1)S(1)}, u32[]{:S(2)}, u32[]{:S(2)}) collective-permute-start(bf16[80,896]{1,0:T(8,128)(2,1)} %get-tuple-element.72), channel_id=1, source_target_pairs={{0,2},{1,3},{2,0},{3,1},{4,6},{5,7},{6,4},{7,5},{8,10},{9,11},{10,... | collective-permute-start | bytes 430088 | tf_op jit(solution)/shard_map/ppermute | solution.py:465
  21.8 15.3 %collective-permute-start.4 = (bf16[576,512]{1,0:T(8,128)(2,1)S(1)}, bf16[576,512]{1,0:T(8,128)(2,1)S(1)}, u32[]{:S(2)}, u32[]{:S(2)}) collective-permute-start(bf16[576,512]{1,0:T(8,128)(2,1)S(1)} %pad_maximum_fusion), channel_id=1, source_target_pairs={{0,16},{8,24},{16,0},{24,8},{1,17},{9,25},{17,1},{25,9},{2,18},{10... | collective-permute-start | bytes 1769480 | tf_op jit(solution)/shard_map/ppermute | solution.py:465
  23.4 13.8 %collective-permute-start.5 = (bf16[4,80,896]{2,1,0:T(8,128)(2,1)S(1)}, bf16[4,80,896]{2,1,0:T(8,128)(2,1)S(1)}, u32[]{:S(2)}, u32[]{:S(2)}) collective-permute-start(bf16[4,80,896]{2,1,0:T(8,128)(2,1)S(1)} %pad_maximum_fusion.1.refs_4_.refs_6_.refs_13_), channel_id=1, source_target_pairs={{0,1},{1,0},{2,3},{3,2},{4,5},{5,4},{6,7},{7,6},{8,9},{9,8},{10,11... | collective-permute-start | bytes 1720328 | tf_op jit(solution)/shard_map/ppermute | solution.py:465
  24.9 12.7 %collective-permute-start.15 = (bf16[128,512]{1,0:T(8,128)(2,1)S(1)}, bf16[128,512]{1,0:T(8,128)(2,1)S(1)}, u32[]{:S(2)}, u32[]{:S(2)}) collective-permute-start(bf16[128,512]{1,0:T(8,128)(2,1)S(1)} %copy-done.4), channel_id=1, source_target_pairs={{0,6},{1,7},{2,4},{3,5},{4,2},{5,3},{6,0},{7,1},{8,14},{9,15},{10,... | collective-permute-start | bytes 393224 | tf_op jit(solution)/shard_map/ppermute | solution.py:465
  27.4 10.2 %collective-permute-start.14 = (bf16[128,512]{1,0:T(8,128)(2,1)S(1)}, bf16[128,512]{1,0:T(8,128)(2,1)S(1)}, u32[]{:S(2)}, u32[]{:S(2)}) collective-permute-start(bf16[128,512]{1,0:T(8,128)(2,1)S(1)} %copy-done.4), channel_id=1, source_target_pairs={{0,4},{1,5},{2,6},{3,7},{4,0},{5,1},{6,2},{7,3},{8,12},{9,13},{10,... | collective-permute-start | bytes 393224 | tf_op jit(solution)/shard_map/ppermute | solution.py:465
  27.4 10.2 %collective-permute-start.13 = (bf16[128,512]{1,0:T(8,128)(2,1)S(1)}, bf16[128,512]{1,0:T(8,128)(2,1)S(1)}, u32[]{:S(2)}, u32[]{:S(2)}) collective-permute-start(bf16[128,512]{1,0:T(8,128)(2,1)S(1)} %copy-done.4), channel_id=1, source_target_pairs={{0,2},{1,3},{2,0},{3,1},{4,6},{5,7},{6,4},{7,5},{8,10},{9,11},{10,... | collective-permute-start | bytes 393224 | tf_op jit(solution)/shard_map/ppermute | solution.py:465
  37.7 13.9 %collective-permute-start.16 = (bf16[4,128,512]{2,1,0:T(8,128)(2,1)S(1)}, bf16[4,128,512]{2,1,0:T(8,128)(2,1)S(1)}, u32[]{:S(2)}, u32[]{:S(2)}) collective-permute-start(bf16[4,128,512]{2,1,0:T(8,128)(2,1)S(1)} %pad_maximum_fusion.2.refs_14_), channel_id=1, source_target_pairs={{0,1},{1,0},{2,3},{3,2},{4,5},{5,4},{6,7},{7,6},{8,9},{9,8},{10,11... | collective-permute-start | bytes 1572872 | tf_op jit(solution)/shard_map/ppermute | solution.py:465
  39.4 12.8 %collective-permute-start.11 = (bf16[4,80,512]{2,1,0:T(8,128)(2,1)S(1)}, bf16[4,80,512]{2,1,0:T(8,128)(2,1)S(1)}, u32[]{:S(2)}, u32[]{:S(2)}) collective-permute-start(bf16[4,80,512]{2,1,0:T(8,128)(2,1)S(1)} %slice.97), channel_id=1, source_target_pairs={{0,16},{8,24},{16,0},{24,8},{1,17},{9,25},{17,1},{25,9},{2,18},{10... | collective-permute-start | bytes 983048 | tf_op jit(solution)/shard_map/ppermute | solution.py:465
  45.3 6.3 %collective-permute-start.8 = (bf16[256,128]{1,0:T(8,128)(2,1)S(1)}, bf16[256,128]{1,0:T(8,128)(2,1)S(1)}, u32[]{:S(2)}, u32[]{:S(2)}) collective-permute-start(bf16[256,128]{1,0:T(8,128)(2,1)S(1)} %get-tuple-element.76), channel_id=1, source_target_pairs={{0,16},{8,24},{16,0},{24,8},{1,17},{9,25},{17,1},{25,9},{2,18},{10... | collective-permute-start | bytes 196616 | tf_op jit(solution)/shard_map/ppermute | solution.py:465
  46.9 4.8 %collective-permute-start.9 = (bf16[256,128]{1,0:T(8,128)(2,1)S(1)}, bf16[256,128]{1,0:T(8,128)(2,1)S(1)}, u32[]{:S(2)}, u32[]{:S(2)}) collective-permute-start(bf16[256,128]{1,0:T(8,128)(2,1)S(1)} %get-tuple-element.77), channel_id=1, source_target_pairs={{0,24},{8,16},{16,8},{24,0},{1,25},{9,17},{17,9},{25,1},{2,26},{10... | collective-permute-start | bytes 196616 | tf_op jit(solution)/shard_map/ppermute | solution.py:465
  46.9 5.8 %collective-permute-start.17 = (bf16[4,128,512]{2,1,0:T(8,128)(2,1)S(1)}, bf16[4,128,512]{2,1,0:T(8,128)(2,1)S(1)}, u32[]{:S(2)}, u32[]{:S(2)}) collective-permute-start(bf16[4,128,512]{2,1,0:T(8,128)(2,1)S(1)} %pad_maximum_fusion.2.refs_14_), channel_id=1, source_target_pairs={{0,8},{8,0},{16,24},{24,16},{1,9},{9,1},{17,25},{25,17},{2,10},{10... | collective-permute-start | bytes 1572872 | tf_op jit(solution)/shard_map/ppermute | solution.py:465
  60.7 4.5 %collective-permute-start.34 = (bf16[256,1536]{1,0:T(8,128)(2,1)S(1)}, bf16[256,1536]{1,0:T(8,128)(2,1)S(1)}, u32[]{:S(2)}, u32[]{:S(2)}) collective-permute-start(bf16[256,1536]{1,0:T(8,128)(2,1)S(1)} %get-tuple-element.112), channel_id=1, source_target_pairs={{0,8},{8,0},{16,24},{24,16},{1,9},{9,1},{17,25},{25,17},{2,10},{10... | collective-permute-start | bytes 2359304 | tf_op jit(solution)/shard_map/ppermute | solution.py:465
  61.1 7.8 %collective-permute-start.19 = (bf16[256,128]{1,0:T(8,128)(2,1)S(1)}, bf16[256,128]{1,0:T(8,128)(2,1)S(1)}, u32[]{:S(2)}, u32[]{:S(2)}) collective-permute-start(bf16[256,128]{1,0:T(8,128)(2,1)S(1)} %get-tuple-element.84), channel_id=1, source_target_pairs={{0,8},{8,0},{16,24},{24,16},{1,9},{9,1},{17,25},{25,17},{2,10},{10... | collective-permute-start | bytes 196616 | tf_op jit(solution)/shard_map/ppermute | solution.py:465
  61.2 7.6 %collective-permute-start.20 = (bf16[256,128]{1,0:T(8,128)(2,1)S(1)}, bf16[256,128]{1,0:T(8,128)(2,1)S(1)}, u32[]{:S(2)}, u32[]{:S(2)}) collective-permute-start(bf16[256,128]{1,0:T(8,128)(2,1)S(1)} %get-tuple-element.85), channel_id=1, source_target_pairs={{0,16},{8,24},{16,0},{24,8},{1,17},{9,25},{17,1},{25,9},{2,18},{10... | collective-permute-start | bytes 196616 | tf_op jit(solution)/shard_map/ppermute | solution.py:465
  61.8 7.0 %collective-permute-start.21 = (bf16[256,128]{1,0:T(8,128)(2,1)S(1)}, bf16[256,128]{1,0:T(8,128)(2,1)S(1)}, u32[]{:S(2)}, u32[]{:S(2)}) collective-permute-start(bf16[256,128]{1,0:T(8,128)(2,1)S(1)} %get-tuple-element.86), channel_id=1, source_target_pairs={{0,24},{8,16},{16,8},{24,0},{1,25},{9,17},{17,9},{25,1},{2,26},{10... | collective-permute-start | bytes 196616 | tf_op jit(solution)/shard_map/ppermute | solution.py:465
  66.6 14.1 %collective-permute-start.35 = (bf16[8,64,512]{2,1,0:T(8,128)(2,1)S(1)}, bf16[8,64,512]{2,1,0:T(8,128)(2,1)}, u32[]{:S(2)}, u32[]{:S(2)}) collective-permute-start(bf16[8,64,512]{2,1,0:T(8,128)(2,1)S(1)} %get-tuple-element.114), channel_id=1, source_target_pairs={{0,16},{8,24},{16,0},{24,8},{1,17},{9,25},{17,1},{25,9},{2,18},{10... | collective-permute-start | bytes 1572872 | tf_op jit(solution)/shard_map/ppermute | solution.py:465
  67.3 18.0 %collective-permute-start.23 = (bf16[4,64,1280]{2,1,0:T(8,128)(2,1)S(1)}, bf16[4,64,1280]{2,1,0:T(8,128)(2,1)}, u32[]{:S(2)}, u32[]{:S(2)}) collective-permute-start(bf16[4,64,1280]{2,1,0:T(8,128)(2,1)S(1)} %get-tuple-element.96), channel_id=1, source_target_pairs={{0,1},{1,0},{2,3},{3,2},{4,5},{5,4},{6,7},{7,6},{8,9},{9,8},{10,11... | collective-permute-start | bytes 1966088 | tf_op jit(solution)/shard_map/ppermute | solution.py:465
  76.5 8.8 %collective-permute-start.24 = (bf16[2,256,512]{2,1,0:T(8,128)(2,1)}, bf16[2,256,512]{2,1,0:T(8,128)(2,1)}, u32[]{:S(2)}, u32[]{:S(2)}) collective-permute-start(bf16[2,256,512]{2,1,0:T(8,128)(2,1)} %get-tuple-element.98), channel_id=1, source_target_pairs={{0,8},{8,0},{16,24},{24,16},{1,9},{9,1},{17,25},{25,17},{2,10},{10... | collective-permute-start | bytes 1572872 | tf_op jit(solution)/shard_map/ppermute | solution.py:465
  76.5 26.3 %all-to-all-start = ((bf16[8,80,384]{2,1,0:T(8,128)(2,1)}), bf16[8,80,384]{2,1,0:T(8,128)(2,1)}, u32[]{:S(2)}, u32[]{:S(2)}) async-start(bf16[8,80,384]{2,1,0:T(8,128)(2,1)} %get-tuple-element.99), calls=%async_computation | async-start | bytes 983040 | tf_op jit(solution)/shard_map/all_to_all | solution.py:662
  82.0 12.8 %collective-permute-start.36 = (bf16[4,64,512]{2,1,0:T(8,128)(2,1)S(1)}, bf16[4,64,512]{2,1,0:T(8,128)(2,1)S(1)}, u32[]{:S(2)}, u32[]{:S(2)}) collective-permute-start(bf16[4,64,512]{2,1,0:T(8,128)(2,1)S(1)} %get-tuple-element.128), channel_id=1, source_target_pairs={{0,1},{1,0},{2,3},{3,2},{4,5},{5,4},{6,7},{7,6},{8,9},{9,8},{10,11... | collective-permute-start | bytes 786440 | tf_op jit(solution)/shard_map/ppermute | solution.py:465
  86.3 8.4 %collective-permute-start.25 = (bf16[256,512]{1,0:T(8,128)(2,1)S(1)}, bf16[256,512]{1,0:T(8,128)(2,1)S(1)}, u32[]{:S(2)}, u32[]{:S(2)}) collective-permute-start(bf16[256,512]{1,0:T(8,128)(2,1)S(1)} %fusion.2), channel_id=1, source_target_pairs={{0,16},{8,24},{16,0},{24,8},{1,17},{9,25},{17,1},{25,9},{2,18},{10... | collective-permute-start | bytes 786440 | tf_op jit(solution)/shard_map/ppermute | solution.py:465
  88.8 12.2 %collective-permute-start.26 = (bf16[2,64,1280]{2,1,0:T(8,128)(2,1)S(1)}, bf16[2,64,1280]{2,1,0:T(8,128)(2,1)S(1)}, u32[]{:S(2)}, u32[]{:S(2)}) collective-permute-start(bf16[2,64,1280]{2,1,0:T(8,128)(2,1)S(1)} %add_convert_fusion), channel_id=1, source_target_pairs={{0,2},{1,3},{2,0},{3,1},{4,6},{5,7},{6,4},{7,5},{8,10},{9,11},{10,... | collective-permute-start | bytes 983048 | tf_op jit(solution)/shard_map/ppermute | solution.py:465
  94.7 10.5 %collective-permute-start.37 = (bf16[2,64,512]{2,1,0:T(8,128)(2,1)S(1)}, bf16[2,64,512]{2,1,0:T(8,128)(2,1)}, u32[]{:S(2)}, u32[]{:S(2)}) collective-permute-start(bf16[2,64,512]{2,1,0:T(8,128)(2,1)S(1)} %add_convert_fusion.5), channel_id=1, source_target_pairs={{0,2},{1,3},{2,0},{3,1},{4,6},{5,7},{6,4},{7,5},{8,10},{9,11},{10,... | collective-permute-start | bytes 393224 | tf_op jit(solution)/shard_map/ppermute | solution.py:465
  102.0 9.2 %collective-permute-start.30 = (bf16[64,1280]{1,0:T(8,128)(2,1)S(1)}, bf16[64,1280]{1,0:T(8,128)(2,1)S(1)}, u32[]{:S(2)}, u32[]{:S(2)}) collective-permute-start(bf16[64,1280]{1,0:T(8,128)(2,1)S(1)} %fusion.3), channel_id=1, source_target_pairs={{0,4},{1,5},{2,6},{3,7},{4,0},{5,1},{6,2},{7,3},{8,12},{9,13},{10,... | collective-permute-start | bytes 491528 | tf_op jit(solution)/shard_map/ppermute | solution.py:465
  103.9 11.6 %collective-permute-start.28 = (bf16[80,384]{1,0:T(8,128)(2,1)S(1)}, bf16[80,384]{1,0:T(8,128)(2,1)S(1)}, u32[]{:S(2)}, u32[]{:S(2)}) collective-permute-start(bf16[80,384]{1,0:T(8,128)(2,1)S(1)} %reduce_sum.12.a), channel_id=1, source_target_pairs={{0,16},{8,24},{16,0},{24,8},{1,17},{9,25},{17,1},{25,9},{2,18},{10... | collective-permute-start | bytes 184328 | tf_op jit(solution)/shard_map/ppermute | solution.py:465
  106.1 7.7 %collective-permute-start.38 = (bf16[64,512]{1,0:T(8,128)(2,1)S(1)}, bf16[64,512]{1,0:T(8,128)(2,1)S(1)}, u32[]{:S(2)}, u32[]{:S(2)}) collective-permute-start(bf16[64,512]{1,0:T(8,128)(2,1)S(1)} %fusion.5), channel_id=1, source_target_pairs={{0,4},{1,5},{2,6},{3,7},{4,0},{5,1},{6,2},{7,3},{8,12},{9,13},{10,... | collective-permute-start | bytes 196616 | tf_op jit(solution)/shard_map/ppermute | solution.py:465
  112.2 6.2 %collective-permute-start.32 = (bf16[64,1280]{1,0:T(8,128)(2,1)S(1)}, bf16[64,1280]{1,0:T(8,128)(2,1)S(1)}, u32[]{:S(2)}, u32[]{:S(2)}) collective-permute-start(bf16[64,1280]{1,0:T(8,128)(2,1)S(1)} %fusion.1.a), channel_id=1, source_target_pairs={{0,16},{8,24},{16,0},{24,8},{1,17},{9,25},{17,1},{25,9},{2,18},{10... | collective-permute-start | bytes 491528 | tf_op jit(solution)/shard_map/ppermute | solution.py:465
  114.7 4.5 %collective-permute-start.40 = (bf16[64,512]{1,0:T(8,128)(2,1)S(1)}, bf16[64,512]{1,0:T(8,128)(2,1)S(1)}, u32[]{:S(2)}, u32[]{:S(2)}) collective-permute-start(bf16[64,512]{1,0:T(8,128)(2,1)S(1)} %fusion.4.refs_0_), channel_id=1, source_target_pairs={{0,16},{8,24},{16,0},{24,8},{1,17},{9,25},{17,1},{25,9},{2,18},{10... | collective-permute-start | bytes 196616 | tf_op jit(solution)/shard_map/ppermute | solution.py:465
  115.5 3.6 %collective-permute-start.29 = (bf16[80,384]{1,0:T(8,128)(2,1)S(1)}, bf16[80,384]{1,0:T(8,128)(2,1)S(1)}, u32[]{:S(2)}, u32[]{:S(2)}) collective-permute-start(bf16[80,384]{1,0:T(8,128)(2,1)S(1)} %collective-permute-done.28.c), channel_id=1, source_target_pairs={{0,8},{8,0},{16,24},{24,16},{1,9},{9,1},{17,25},{25,17},{2,10},{10... | collective-permute-start | bytes 184328 | tf_op jit(solution)/shard_map/ppermute | solution.py:465
  116.0 4.5 %collective-permute-start.31 = (bf16[64,1280]{1,0:T(8,128)(2,1)S(1)}, bf16[64,1280]{1,0:T(8,128)(2,1)S(1)}, u32[]{:S(2)}, u32[]{:S(2)}) collective-permute-start(bf16[64,1280]{1,0:T(8,128)(2,1)S(1)} %fusion.1.a), channel_id=1, source_target_pairs={{0,8},{8,0},{16,24},{24,16},{1,9},{9,1},{17,25},{25,17},{2,10},{10... | collective-permute-start | bytes 491528 | tf_op jit(solution)/shard_map/ppermute | solution.py:465
  (16 other events, 100.6 us)

commit v5 on v4

--- a/solution.py
+++ b/solution.py
@@ -447,11 +447,11 @@
 
 COSTS.update(
     {
-        attend_kernel: 0.5,
-        middle_kernel: 10.2,
+        attend_kernel: 0.1,
+        middle_kernel: 3.0,
         down_grad_kernel: 1.0,
         up_grad_kernel: 1.0,
-        attend_back_kernel: 9.3,
+        attend_back_kernel: 7.0,
     }
 )
 
@@ -639,6 +639,8 @@
     if direct:
         up_got = swap(up_odd_grad, "fsdp", 1)
         dx_keep, up_got = lax.optimization_barrier((dx_keep, up_got))
+        up_got = after(up_got, got)
+        up_here, up_gone = plus(up_even_grad[::2], up_got[::2]), plus(up_even_grad[1::2], up_got[1::2])
     far = swap(plus(dx_keep[1], got[1]), "seq", 2)
     input_grad = e1 + ((dx_keep[0].astype(F32) + got[0].astype(F32)) + far.astype(F32))
 
@@ -648,15 +650,14 @@
             across = swap(mine, "seq", 2)
             return mine, swap(mine, "seq", 1), across, swap(across, "seq", 1)
 
-        def near(stay, got):
-            came = swap(plus(stay[1::2], got[1::2]), "fsdp", 2)
-            return plus(stay[2], got[2], came[1]), (stay[0], got[0], came[0])
-
         down_far = swap(plus(down_odd, down_got[4:]), "fsdp", 1)
         down_stay = plus(down_even, down_got[:4])
-        up_away, up_here = near(up_even_grad, after(up_got, got))
+        up_came = swap(up_gone, "fsdp", 2)
+        up_away = plus(up_here[1], up_came[1])
         down_far = after(down_far, far)
-        down_away, down_here = near(down_stay, down_far)
+        down_here = plus(down_stay[::2], down_far[::2])
+        down_came = swap(plus(down_stay[1::2], down_far[1::2]), "fsdp", 2)
+        down_away = plus(down_here[1], down_came[1])
         up_far = swap(up_away, "fsdp", 4)
         down_far = swap(down_away, "fsdp", 4)
         w_made = after(lax.all_to_all(w_grad, "fsdp", 0, 0, tiled=True), up_away)
@@ -681,8 +682,8 @@
             index,
             w_all,
         )
-        up_all = spread_out(plus(*up_here, after(up_far, input_grad, w_made)))
-        down_all = spread_out(plus(*down_here, down_far))
+        up_all = spread_out(plus(up_here[0], up_came[0], after(up_far, input_grad, w_made)))
+        down_all = spread_out(plus(down_here[0], down_came[0], after(down_far, up_all[0])))
         out_grad, up_grad, down_grad = run(
             end_wide_kernel,
             [((64, 512), F32), ((64, 2048), F32), ((256, 512), F32)],

time: 123 us -> 121 us (0.984)
  other arithmetic: 11.7 us -> 8.29 us
    convert_element_type x8, other arithmetic: 6.99 us -> 3.62 us  [plus(): return functools.reduce(jnp.add, [t.astype(F32) for t in terms]).astype(BF)]
  transfers between devices with their start and end apart: 43 -> 43, of which waited for: 14 -> 14; matrix products, arithmetic and copies ran while one was open for 8% -> 6% of each run, Pallas kernels for 14% -> 15%
where the time goes in v5:
time: 121 us; the launch traced here: 120 us
  waiting for transfers between devices  43.1 us (36%)
  starting transfers between devices  41.1 us (34%)
  Pallas kernels  27 us (22%)
  other arithmetic  8.29 us (7%)
    ppermute x42, waiting for transfers between devices, swap(): return lax.ppermute(values, axis, [(i, i ^ step) for i in range(size)])  43.1 us
    ppermute x42, starting transfers between devices, swap(): return lax.ppermute(values, axis, [(i, i ^ step) for i in range(size)])  36.9 us
    pallas_call x8, Pallas kernels, run(): pl.pallas_call(kernel, out_shape=outs, in_specs=[SMEM] + [VMEM] * len(arg...  27 us
    all_to_all x1, starting transfers between devices, body(): w_made = after(lax.all_to_all(w_grad, 'fsdp', 0, 0, tiled=True), up_away)  4.12 us
    convert_element_type x8, other arithmetic, plus(): return functools.reduce(jnp.add, [t.astype(F32) for t in terms]).astype(BF)  3.62 us
  transfers between devices with their start and end apart: 43, of which 14 were waited for; matrix products, arithmetic and copies ran while one was open for 6% of the time, Pallas kernels for 15%

profile of v5, /device:TPU:0, one launch (start us, length us, event | category | flops | bytes accessed | tf_op | source)
XLA Modules:
  0.0 120.5 jit_solution(7596227717397841095)
XLA Ops:
  1.2 2.0 %shard_map.305 = (bf16[80,896]{1,0:T(8,128)(2,1)}, bf16[128,512]{1,0:T(8,128)(2,1)}) custom-call(s32[4]{0:T(128)} %pad_add_fusion.idx, bf16[64,512]{1,0:T(8,128)(2,1)} %wq.1, bf16[64,512]{1,0:T(8,128)(2,1)} %wk.1, bf16[64,512]{1,0:T(8,128)(2,1)} %wv.1, bf16[64,512]{1,0:T(8,128)(2,1)} %wo.1, bf16[64,2048]{1,0:T(8,128)(2,1)} %up.1, bf16[256,512]{1,0:T(8,128)(2,1)} %down.1, ...), custom_call_target="tpu_custom_call" | custom-call | flops 1700000000 | bytes 5100000 | tf_op jit(solution)/shard_map/pallas_call | solution.py:40
  3.3 5.1 %collective-permute-start.2 = (bf16[80,896]{1,0:T(8,128)(2,1)}, bf16[80,896]{1,0:T(8,128)(2,1)S(1)}, u32[]{:S(2)}, u32[]{:S(2)}) collective-permute-start(bf16[80,896]{1,0:T(8,128)(2,1)} %get-tuple-element.73), channel_id=1, source_target_pairs={{0,6},{1,7},{2,4},{3,5},{4,2},{5,3},{6,0},{7,1},{8,14},{9,15},{10,... | collective-permute-start | bytes 430088 | tf_op jit(solution)/shard_map/ppermute | solution.py:465
  9.0 4.3 %collective-permute-done.2 = bf16[80,896]{1,0:T(8,128)(2,1)S(1)} collective-permute-done((bf16[80,896]{1,0:T(8,128)(2,1)}, bf16[80,896]{1,0:T(8,128)(2,1)S(1)}, u32[]{:S(2)}, u32[]{:S(2)}) %collective-permute-start.2) | collective-permute-done | bytes 143392 | tf_op jit(solution)/shard_map/ppermute | solution.py:465
  13.3 7.4 %collective-permute-done.1 = bf16[80,896]{1,0:T(8,128)(2,1)S(1)} collective-permute-done((bf16[80,896]{1,0:T(8,128)(2,1)}, bf16[80,896]{1,0:T(8,128)(2,1)S(1)}, u32[]{:S(2)}, u32[]{:S(2)}) %collective-permute-start.1) | collective-permute-done | bytes 143392 | tf_op jit(solution)/shard_map/ppermute | solution.py:465
  21.8 1.6 %collective-permute-start.4 = (bf16[576,512]{1,0:T(8,128)(2,1)S(1)}, bf16[576,512]{1,0:T(8,128)(2,1)S(1)}, u32[]{:S(2)}, u32[]{:S(2)}) collective-permute-start(bf16[576,512]{1,0:T(8,128)(2,1)S(1)} %pad_maximum_fusion), channel_id=1, source_target_pairs={{0,16},{8,24},{16,0},{24,8},{1,17},{9,25},{17,1},{25,9},{2,18},{10... | collective-permute-start | bytes 1769480 | tf_op jit(solution)/shard_map/ppermute | solution.py:465
  23.4 1.5 %collective-permute-start.5 = (bf16[4,80,896]{2,1,0:T(8,128)(2,1)S(1)}, bf16[4,80,896]{2,1,0:T(8,128)(2,1)S(1)}, u32[]{:S(2)}, u32[]{:S(2)}) collective-permute-start(bf16[4,80,896]{2,1,0:T(8,128)(2,1)S(1)} %pad_maximum_fusion.1.refs_4_.refs_6_.refs_13_), channel_id=1, source_target_pairs={{0,1},{1,0},{2,3},{3,2},{4,5},{5,4},{6,7},{7,6},{8,9},{9,8},{10,11... | collective-permute-start | bytes 1720328 | tf_op jit(solution)/shard_map/ppermute | solution.py:465
  24.9 2.5 %collective-permute-start.15 = (bf16[128,512]{1,0:T(8,128)(2,1)S(1)}, bf16[128,512]{1,0:T(8,128)(2,1)S(1)}, u32[]{:S(2)}, u32[]{:S(2)}) collective-permute-start(bf16[128,512]{1,0:T(8,128)(2,1)S(1)} %copy-done.4), channel_id=1, source_target_pairs={{0,6},{1,7},{2,4},{3,5},{4,2},{5,3},{6,0},{7,1},{8,14},{9,15},{10,... | collective-permute-start | bytes 393224 | tf_op jit(solution)/shard_map/ppermute | solution.py:465
  27.4 1.9 %collective-permute-start.13 = (bf16[128,512]{1,0:T(8,128)(2,1)S(1)}, bf16[128,512]{1,0:T(8,128)(2,1)S(1)}, u32[]{:S(2)}, u32[]{:S(2)}) collective-permute-start(bf16[128,512]{1,0:T(8,128)(2,1)S(1)} %copy-done.4), channel_id=1, source_target_pairs={{0,2},{1,3},{2,0},{3,1},{4,6},{5,7},{6,4},{7,5},{8,10},{9,11},{10,... | collective-permute-start | bytes 393224 | tf_op jit(solution)/shard_map/ppermute | solution.py:465
  29.3 7.8 %collective-permute-done.5.refs_5_.refs_7_.refs_14_ = bf16[4,80,896]{2,1,0:T(8,128)(2,1)S(1)} collective-permute-done((bf16[4,80,896]{2,1,0:T(8,128)(2,1)S(1)}, bf16[4,80,896]{2,1,0:T(8,128)(2,1)S(1)}, u32[]{:S(2)}, u32[]{:S(2)}) %collective-permute-start.5) | collective-permute-done | bytes 573472 | tf_op jit(solution)/shard_map/ppermute | solution.py:465
  37.7 1.6 %collective-permute-start.16 = (bf16[4,128,512]{2,1,0:T(8,128)(2,1)S(1)}, bf16[4,128,512]{2,1,0:T(8,128)(2,1)S(1)}, u32[]{:S(2)}, u32[]{:S(2)}) collective-permute-start(bf16[4,128,512]{2,1,0:T(8,128)(2,1)S(1)} %pad_maximum_fusion.2.refs_14_), channel_id=1, source_target_pairs={{0,1},{1,0},{2,3},{3,2},{4,5},{5,4},{6,7},{7,6},{8,9},{9,8},{10,11... | collective-permute-start | bytes 1572872 | tf_op jit(solution)/shard_map/ppermute | solution.py:465
  40.0 5.3 %shard_map.306 = (bf16[256,128]{1,0:T(8,128)(2,1)S(1)}, bf16[256,128]{1,0:T(8,128)(2,1)S(1)}, bf16[256,128]{1,0:T(8,128)(2,1)S(1)}, bf16[256,128]{1,0:T(8,128)(2...) custom-call(s32[4]{0:T(128)S(1)} %copy-done.2, ...), custom_call_target="tpu_custom_call" | custom-call | flops 100000000 | bytes 300000 | tf_op jit(solution)/shard_map/pallas_call | solution.py:40
  45.3 1.6 %collective-permute-start.8 = (bf16[256,128]{1,0:T(8,128)(2,1)S(1)}, bf16[256,128]{1,0:T(8,128)(2,1)S(1)}, u32[]{:S(2)}, u32[]{:S(2)}) collective-permute-start(bf16[256,128]{1,0:T(8,128)(2,1)S(1)} %get-tuple-element.77), channel_id=1, source_target_pairs={{0,16},{8,24},{16,0},{24,8},{1,17},{9,25},{17,1},{25,9},{2,18},{10... | collective-permute-start | bytes 196616 | tf_op jit(solution)/shard_map/ppermute | solution.py:465
  47.5 4.1 %collective-permute-done.16.refs_15_ = bf16[4,128,512]{2,1,0:T(8,128)(2,1)S(1)} collective-permute-done((bf16[4,128,512]{2,1,0:T(8,128)(2,1)S(1)}, bf16[4,128,512]{2,1,0:T(8,128)(2,1)S(1)}, u32[]{:S(2)}, u32[]{:S(2)}) %collective-permute-start.16) | collective-permute-done | bytes 524320 | tf_op jit(solution)/shard_map/ppermute | solution.py:465
  54.6 5.9 %shard_map.307 = (bf16[256,512]{1,0:T(8,128)(2,1)}, bf16[256,128]{1,0:T(8,128)(2,1)S(1)}, bf16[256,128]{1,0:T(8,128)(2,1)S(1)}, bf16[256,128]{1,0:T(8,128)(2,1)S...) custom-call(s32[4]{0:T(128)S(1)} %copy-done.2, ...), custom_call_target="tpu_custom_call" | custom-call | flops 3000000000 | bytes 9000000 | tf_op jit(solution)/shard_map/pallas_call | solution.py:40
  63.4 1.8 %shard_map.309 = (bf16[4,64,1280]{2,1,0:T(8,128)(2,1)S(1)}, bf16[4,64,1280]{2,1,0:T(8,128)(2,1)S(1)}) custom-call(s32[4]{0:T(128)S(1)} %copy-done.2, bf16[256,2304]{1,0:T(8,128)(2,1)S(1)} %get-tuple-element.95.mine, bf16[256,2304]{1,0:T(8,128)(2,1)S(1)} %collective-permute-done.22.other), custom_call_target="tpu_custom_call" | custom-call | flops 1000000000 | bytes 3000000 | tf_op jit(solution)/shard_map/pallas_call | solution.py:40
  65.2 1.4 %shard_map.311 = (bf16[4,64,512]{2,1,0:T(8,128)(2,1)S(1)}, bf16[4,64,512]{2,1,0:T(8,128)(2,1)S(1)}, bf16[8,64,512]{2,1,0:T(8,128)(2,1)S(1)}) custom-call(s32[4]{0:T(128)S(1)} %copy-done.2, bf16[256,1536]{1,0:T(8,128)(2,1)S(1)} %get-tuple-element.112.mine, bf16[256,1536]{1,0:T(8,128)(2,1)S(1)} %collective-permute-done.34.other), custom_call_target="tpu_custom_call" | custom-call | flops 1000000000 | bytes 3000000 | tf_op jit(solution)/shard_map/pallas_call | solution.py:40
  67.3 1.5 %collective-permute-start.23 = (bf16[4,64,1280]{2,1,0:T(8,128)(2,1)S(1)}, bf16[4,64,1280]{2,1,0:T(8,128)(2,1)}, u32[]{:S(2)}, u32[]{:S(2)}) collective-permute-start(bf16[4,64,1280]{2,1,0:T(8,128)(2,1)S(1)} %get-tuple-element.97), channel_id=1, source_target_pairs={{0,1},{1,0},{2,3},{3,2},{4,5},{5,4},{6,7},{7,6},{8,9},{9,8},{10,11... | collective-permute-start | bytes 1966088 | tf_op jit(solution)/shard_map/ppermute | solution.py:465
  68.9 7.6 %shard_map.308 = (bf16[2,256,512]{2,1,0:T(8,128)(2,1)S(1)}, bf16[2,256,512]{2,1,0:T(8,128)(2,1)}, bf16[8,80,384]{2,1,0:T(8,128)(2,1)}) custom-call(s32[4]{0:T(128)S(1)} %copy-done.2, bf16[256,128]{1,0:T(8,128)(2,1)S(1)} %get-tuple-element.84.refs_0_, bf16[256,128]{1,0:T(8,128)(2,1)S(1)} %collective-permute-done.19.refs_1_, ...), custom_call_target="tpu_custom_call" | custom-call | flops 7000000000 | bytes 21000000 | tf_op jit(solution)/shard_map/pallas_call | solution.py:40
  76.5 4.1 %all-to-all-start = ((bf16[8,80,384]{2,1,0:T(8,128)(2,1)}), bf16[8,80,384]{2,1,0:T(8,128)(2,1)}, u32[]{:S(2)}, u32[]{:S(2)}) async-start(bf16[8,80,384]{2,1,0:T(8,128)(2,1)} %get-tuple-element.100), calls=%async_computation | async-start | bytes 983040 | tf_op jit(solution)/shard_map/all_to_all | solution.py:663
  82.0 1.8 %collective-permute-start.36 = (bf16[4,64,512]{2,1,0:T(8,128)(2,1)S(1)}, bf16[4,64,512]{2,1,0:T(8,128)(2,1)S(1)}, u32[]{:S(2)}, u32[]{:S(2)}) collective-permute-start(bf16[4,64,512]{2,1,0:T(8,128)(2,1)S(1)} %get-tuple-element.134), channel_id=1, source_target_pairs={{0,1},{1,0},{2,3},{3,2},{4,5},{5,4},{6,7},{7,6},{8,9},{9,8},{10,11... | collective-permute-start | bytes 786440 | tf_op jit(solution)/shard_map/ppermute | solution.py:465
  83.7 1.6 %collective-permute-done.23 = bf16[4,64,1280]{2,1,0:T(8,128)(2,1)} collective-permute-done((bf16[4,64,1280]{2,1,0:T(8,128)(2,1)S(1)}, bf16[4,64,1280]{2,1,0:T(8,128)(2,1)}, u32[]{:S(2)}, u32[]{:S(2)}) %collective-permute-start.23) | collective-permute-done | bytes 655392 | tf_op jit(solution)/shard_map/ppermute | solution.py:465
  86.3 1.5 %collective-permute-start.25 = (bf16[256,512]{1,0:T(8,128)(2,1)S(1)}, bf16[256,512]{1,0:T(8,128)(2,1)S(1)}, u32[]{:S(2)}, u32[]{:S(2)}) collective-permute-start(bf16[256,512]{1,0:T(8,128)(2,1)S(1)} %fusion.2), channel_id=1, source_target_pairs={{0,16},{8,24},{16,0},{24,8},{1,17},{9,25},{17,1},{25,9},{2,18},{10... | collective-permute-start | bytes 786440 | tf_op jit(solution)/shard_map/ppermute | solution.py:465
  89.1 5.6 %collective-permute-done.36 = bf16[4,64,512]{2,1,0:T(8,128)(2,1)S(1)} collective-permute-done((bf16[4,64,512]{2,1,0:T(8,128)(2,1)S(1)}, bf16[4,64,512]{2,1,0:T(8,128)(2,1)S(1)}, u32[]{:S(2)}, u32[]{:S(2)}) %collective-permute-start.36) | collective-permute-done | bytes 262176 | tf_op jit(solution)/shard_map/ppermute | solution.py:465
  94.8 1.5 %collective-permute-start.37 = (bf16[2,64,512]{2,1,0:T(8,128)(2,1)S(1)}, bf16[2,64,512]{2,1,0:T(8,128)(2,1)S(1)}, u32[]{:S(2)}, u32[]{:S(2)}) collective-permute-start(bf16[2,64,512]{2,1,0:T(8,128)(2,1)S(1)} %get-tuple-element.132), channel_id=1, source_target_pairs={{0,2},{1,3},{2,0},{3,1},{4,6},{5,7},{6,4},{7,5},{8,10},{9,11},{10,... | collective-permute-start | bytes 393224 | tf_op jit(solution)/shard_map/ppermute | solution.py:465
  96.3 1.9 %fusion = f32[256,512]{1,0:T(8,128)} fusion(f32[256,512]{1,0:T(8,128)S(1)} %get-tuple-element.83, bf16[256,512]{1,0:T(8,128)(2,1)S(1)} %collective-permute-done.25, bf16[2,256,512]{2,1,0:T(8,128)(2,1)} %collective-permute-done.24, bf16[2,256,512]{2,1,0:T(8,128)(2,1)S(1)} %get-tuple-element.98), kind=kLoop, calls=%fused_computation.6 | loop fusion | flops 786432 | bytes 1835008 | tf_op jit(solution)/shard_map/add | solution.py:645
  98.1 2.9 %collective-permute-done.26 = bf16[2,64,1280]{2,1,0:T(8,128)(2,1)S(1)} collective-permute-done((bf16[2,64,1280]{2,1,0:T(8,128)(2,1)S(1)}, bf16[2,64,1280]{2,1,0:T(8,128)(2,1)S(1)}, u32[]{:S(2)}, u32[]{:S(2)}) %collective-permute-start.26) | collective-permute-done | bytes 327712 | tf_op jit(solution)/shard_map/ppermute | solution.py:465
  104.3 2.0 %collective-permute-start.38 = (bf16[64,512]{1,0:T(8,128)(2,1)S(1)}, bf16[64,512]{1,0:T(8,128)(2,1)S(1)}, u32[]{:S(2)}, u32[]{:S(2)}) collective-permute-start(bf16[64,512]{1,0:T(8,128)(2,1)S(1)} %fusion.5), channel_id=1, source_target_pairs={{0,4},{1,5},{2,6},{3,7},{4,0},{5,1},{6,2},{7,3},{8,12},{9,13},{10,... | collective-permute-start | bytes 196616 | tf_op jit(solution)/shard_map/ppermute | solution.py:465
  106.3 4.1 %collective-permute-done.30 = bf16[64,1280]{1,0:T(8,128)(2,1)S(1)} collective-permute-done((bf16[64,1280]{1,0:T(8,128)(2,1)S(1)}, bf16[64,1280]{1,0:T(8,128)(2,1)S(1)}, u32[]{:S(2)}, u32[]{:S(2)}) %collective-permute-start.30) | collective-permute-done | bytes 163872 | tf_op jit(solution)/shard_map/ppermute | solution.py:465
  110.4 2.6 %collective-permute-start.32 = (bf16[64,1280]{1,0:T(8,128)(2,1)S(1)}, bf16[64,1280]{1,0:T(8,128)(2,1)S(1)}, u32[]{:S(2)}, u32[]{:S(2)}) collective-permute-start(bf16[64,1280]{1,0:T(8,128)(2,1)S(1)} %fusion.1.a), channel_id=1, source_target_pairs={{0,16},{8,24},{16,0},{24,8},{1,17},{9,25},{17,1},{25,9},{2,18},{10... | collective-permute-start | bytes 491528 | tf_op jit(solution)/shard_map/ppermute | solution.py:465
  114.2 2.1 %collective-permute-done.32.c = bf16[64,1280]{1,0:T(8,128)(2,1)S(1)} collective-permute-done((bf16[64,1280]{1,0:T(8,128)(2,1)S(1)}, bf16[64,1280]{1,0:T(8,128)(2,1)S(1)}, u32[]{:S(2)}, u32[]{:S(2)}) %collective-permute-start.32) | collective-permute-done | bytes 163872 | tf_op jit(solution)/shard_map/ppermute | solution.py:465
  117.4 1.4 %shard_map.310 = (f32[64,512]{1,0:T(8,128)}, f32[64,512]{1,0:T(8,128)}, f32[64,512]{1,0:T(8,128)}, f32[64]{0:T(128)}, f32[64]{0:T(128)}, /*index=5*/f32[64]{0:T(...) custom-call(s32[4]{0:T(128)S(1)} %copy-done.2, ...), custom_call_target="tpu_custom_call" | custom-call | flops 1700000000 | bytes 5100000 | tf_op jit(solution)/shard_map/pallas_call | solution.py:40
  118.8 1.6 %shard_map.312 = (f32[64,512]{1,0:T(8,128)}, f32[64,2048]{1,0:T(8,128)}, f32[256,512]{1,0:T(8,128)}) custom-call(s32[4]{0:T(128)S(1)} %copy-done.2, bf16[64,1280]{1,0:T(8,128)(2,1)S(1)} %fusion.1.a, bf16[64,1280]{1,0:T(8,128)(2,1)S(1)} %collective-permute-done.31.b, bf16[64,1280]{1,0:T(8,128)(2,1)S(1)} %collective-permute-done.32.c, ...), custom_call_target="tpu_custom_call" | custom-call | flops 1700000000 | bytes 5100000 | tf_op jit(solution)/shard_map/pallas_call | solution.py:40
  (88 shorter events, 20.0 us)
Async XLA Ops:
  3.3 10.0 %collective-permute-start.2 = (bf16[80,896]{1,0:T(8,128)(2,1)}, bf16[80,896]{1,0:T(8,128)(2,1)S(1)}, u32[]{:S(2)}, u32[]{:S(2)}) collective-permute-start(bf16[80,896]{1,0:T(8,128)(2,1)} %get-tuple-element.73), channel_id=1, source_target_pairs={{0,6},{1,7},{2,4},{3,5},{4,2},{5,3},{6,0},{7,1},{8,14},{9,15},{10,... | collective-permute-start | bytes 430088 | tf_op jit(solution)/shard_map/ppermute | solution.py:465
  8.4 12.3 %collective-permute-start.1 = (bf16[80,896]{1,0:T(8,128)(2,1)}, bf16[80,896]{1,0:T(8,128)(2,1)S(1)}, u32[]{:S(2)}, u32[]{:S(2)}) collective-permute-start(bf16[80,896]{1,0:T(8,128)(2,1)} %get-tuple-element.73), channel_id=1, source_target_pairs={{0,4},{1,5},{2,6},{3,7},{4,0},{5,1},{6,2},{7,3},{8,12},{9,13},{10,... | collective-permute-start | bytes 430088 | tf_op jit(solution)/shard_map/ppermute | solution.py:465
  8.4 12.3 %collective-permute-start = (bf16[80,896]{1,0:T(8,128)(2,1)}, bf16[80,896]{1,0:T(8,128)(2,1)S(1)}, u32[]{:S(2)}, u32[]{:S(2)}) collective-permute-start(bf16[80,896]{1,0:T(8,128)(2,1)} %get-tuple-element.73), channel_id=1, source_target_pairs={{0,2},{1,3},{2,0},{3,1},{4,6},{5,7},{6,4},{7,5},{8,10},{9,11},{10,... | collective-permute-start | bytes 430088 | tf_op jit(solution)/shard_map/ppermute | solution.py:465
  21.8 15.3 %collective-permute-start.4 = (bf16[576,512]{1,0:T(8,128)(2,1)S(1)}, bf16[576,512]{1,0:T(8,128)(2,1)S(1)}, u32[]{:S(2)}, u32[]{:S(2)}) collective-permute-start(bf16[576,512]{1,0:T(8,128)(2,1)S(1)} %pad_maximum_fusion), channel_id=1, source_target_pairs={{0,16},{8,24},{16,0},{24,8},{1,17},{9,25},{17,1},{25,9},{2,18},{10... | collective-permute-start | bytes 1769480 | tf_op jit(solution)/shard_map/ppermute | solution.py:465
  23.4 13.8 %collective-permute-start.5 = (bf16[4,80,896]{2,1,0:T(8,128)(2,1)S(1)}, bf16[4,80,896]{2,1,0:T(8,128)(2,1)S(1)}, u32[]{:S(2)}, u32[]{:S(2)}) collective-permute-start(bf16[4,80,896]{2,1,0:T(8,128)(2,1)S(1)} %pad_maximum_fusion.1.refs_4_.refs_6_.refs_13_), channel_id=1, source_target_pairs={{0,1},{1,0},{2,3},{3,2},{4,5},{5,4},{6,7},{7,6},{8,9},{9,8},{10,11... | collective-permute-start | bytes 1720328 | tf_op jit(solution)/shard_map/ppermute | solution.py:465
  24.9 12.7 %collective-permute-start.15 = (bf16[128,512]{1,0:T(8,128)(2,1)S(1)}, bf16[128,512]{1,0:T(8,128)(2,1)S(1)}, u32[]{:S(2)}, u32[]{:S(2)}) collective-permute-start(bf16[128,512]{1,0:T(8,128)(2,1)S(1)} %copy-done.4), channel_id=1, source_target_pairs={{0,6},{1,7},{2,4},{3,5},{4,2},{5,3},{6,0},{7,1},{8,14},{9,15},{10,... | collective-permute-start | bytes 393224 | tf_op jit(solution)/shard_map/ppermute | solution.py:465
  27.4 10.2 %collective-permute-start.14 = (bf16[128,512]{1,0:T(8,128)(2,1)S(1)}, bf16[128,512]{1,0:T(8,128)(2,1)S(1)}, u32[]{:S(2)}, u32[]{:S(2)}) collective-permute-start(bf16[128,512]{1,0:T(8,128)(2,1)S(1)} %copy-done.4), channel_id=1, source_target_pairs={{0,4},{1,5},{2,6},{3,7},{4,0},{5,1},{6,2},{7,3},{8,12},{9,13},{10,... | collective-permute-start | bytes 393224 | tf_op jit(solution)/shard_map/ppermute | solution.py:465
  27.4 10.2 %collective-permute-start.13 = (bf16[128,512]{1,0:T(8,128)(2,1)S(1)}, bf16[128,512]{1,0:T(8,128)(2,1)S(1)}, u32[]{:S(2)}, u32[]{:S(2)}) collective-permute-start(bf16[128,512]{1,0:T(8,128)(2,1)S(1)} %copy-done.4), channel_id=1, source_target_pairs={{0,2},{1,3},{2,0},{3,1},{4,6},{5,7},{6,4},{7,5},{8,10},{9,11},{10,... | collective-permute-start | bytes 393224 | tf_op jit(solution)/shard_map/ppermute | solution.py:465
  37.7 13.9 %collective-permute-start.16 = (bf16[4,128,512]{2,1,0:T(8,128)(2,1)S(1)}, bf16[4,128,512]{2,1,0:T(8,128)(2,1)S(1)}, u32[]{:S(2)}, u32[]{:S(2)}) collective-permute-start(bf16[4,128,512]{2,1,0:T(8,128)(2,1)S(1)} %pad_maximum_fusion.2.refs_14_), channel_id=1, source_target_pairs={{0,1},{1,0},{2,3},{3,2},{4,5},{5,4},{6,7},{7,6},{8,9},{9,8},{10,11... | collective-permute-start | bytes 1572872 | tf_op jit(solution)/shard_map/ppermute | solution.py:465
  39.4 12.8 %collective-permute-start.11 = (bf16[4,80,512]{2,1,0:T(8,128)(2,1)S(1)}, bf16[4,80,512]{2,1,0:T(8,128)(2,1)S(1)}, u32[]{:S(2)}, u32[]{:S(2)}) collective-permute-start(bf16[4,80,512]{2,1,0:T(8,128)(2,1)S(1)} %slice.97), channel_id=1, source_target_pairs={{0,16},{8,24},{16,0},{24,8},{1,17},{9,25},{17,1},{25,9},{2,18},{10... | collective-permute-start | bytes 983048 | tf_op jit(solution)/shard_map/ppermute | solution.py:465
  45.3 6.3 %collective-permute-start.8 = (bf16[256,128]{1,0:T(8,128)(2,1)S(1)}, bf16[256,128]{1,0:T(8,128)(2,1)S(1)}, u32[]{:S(2)}, u32[]{:S(2)}) collective-permute-start(bf16[256,128]{1,0:T(8,128)(2,1)S(1)} %get-tuple-element.77), channel_id=1, source_target_pairs={{0,16},{8,24},{16,0},{24,8},{1,17},{9,25},{17,1},{25,9},{2,18},{10... | collective-permute-start | bytes 196616 | tf_op jit(solution)/shard_map/ppermute | solution.py:465
  46.9 4.8 %collective-permute-start.9 = (bf16[256,128]{1,0:T(8,128)(2,1)S(1)}, bf16[256,128]{1,0:T(8,128)(2,1)S(1)}, u32[]{:S(2)}, u32[]{:S(2)}) collective-permute-start(bf16[256,128]{1,0:T(8,128)(2,1)S(1)} %get-tuple-element.78), channel_id=1, source_target_pairs={{0,24},{8,16},{16,8},{24,0},{1,25},{9,17},{17,9},{25,1},{2,26},{10... | collective-permute-start | bytes 196616 | tf_op jit(solution)/shard_map/ppermute | solution.py:465
  46.9 5.8 %collective-permute-start.17 = (bf16[4,128,512]{2,1,0:T(8,128)(2,1)S(1)}, bf16[4,128,512]{2,1,0:T(8,128)(2,1)S(1)}, u32[]{:S(2)}, u32[]{:S(2)}) collective-permute-start(bf16[4,128,512]{2,1,0:T(8,128)(2,1)S(1)} %pad_maximum_fusion.2.refs_14_), channel_id=1, source_target_pairs={{0,8},{8,0},{16,24},{24,16},{1,9},{9,1},{17,25},{25,17},{2,10},{10... | collective-permute-start | bytes 1572872 | tf_op jit(solution)/shard_map/ppermute | solution.py:465
  60.7 4.5 %collective-permute-start.34 = (bf16[256,1536]{1,0:T(8,128)(2,1)S(1)}, bf16[256,1536]{1,0:T(8,128)(2,1)S(1)}, u32[]{:S(2)}, u32[]{:S(2)}) collective-permute-start(bf16[256,1536]{1,0:T(8,128)(2,1)S(1)} %get-tuple-element.113), channel_id=1, source_target_pairs={{0,8},{8,0},{16,24},{24,16},{1,9},{9,1},{17,25},{25,17},{2,10},{10... | collective-permute-start | bytes 2359304 | tf_op jit(solution)/shard_map/ppermute | solution.py:465
  61.1 7.8 %collective-permute-start.19 = (bf16[256,128]{1,0:T(8,128)(2,1)S(1)}, bf16[256,128]{1,0:T(8,128)(2,1)S(1)}, u32[]{:S(2)}, u32[]{:S(2)}) collective-permute-start(bf16[256,128]{1,0:T(8,128)(2,1)S(1)} %get-tuple-element.85), channel_id=1, source_target_pairs={{0,8},{8,0},{16,24},{24,16},{1,9},{9,1},{17,25},{25,17},{2,10},{10... | collective-permute-start | bytes 196616 | tf_op jit(solution)/shard_map/ppermute | solution.py:465
  61.2 7.6 %collective-permute-start.20 = (bf16[256,128]{1,0:T(8,128)(2,1)S(1)}, bf16[256,128]{1,0:T(8,128)(2,1)S(1)}, u32[]{:S(2)}, u32[]{:S(2)}) collective-permute-start(bf16[256,128]{1,0:T(8,128)(2,1)S(1)} %get-tuple-element.86), channel_id=1, source_target_pairs={{0,16},{8,24},{16,0},{24,8},{1,17},{9,25},{17,1},{25,9},{2,18},{10... | collective-permute-start | bytes 196616 | tf_op jit(solution)/shard_map/ppermute | solution.py:465
  61.8 7.0 %collective-permute-start.21 = (bf16[256,128]{1,0:T(8,128)(2,1)S(1)}, bf16[256,128]{1,0:T(8,128)(2,1)S(1)}, u32[]{:S(2)}, u32[]{:S(2)}) collective-permute-start(bf16[256,128]{1,0:T(8,128)(2,1)S(1)} %get-tuple-element.87), channel_id=1, source_target_pairs={{0,24},{8,16},{16,8},{24,0},{1,25},{9,17},{17,9},{25,1},{2,26},{10... | collective-permute-start | bytes 196616 | tf_op jit(solution)/shard_map/ppermute | solution.py:465
  66.6 14.1 %collective-permute-start.35 = (bf16[8,64,512]{2,1,0:T(8,128)(2,1)S(1)}, bf16[8,64,512]{2,1,0:T(8,128)(2,1)}, u32[]{:S(2)}, u32[]{:S(2)}) collective-permute-start(bf16[8,64,512]{2,1,0:T(8,128)(2,1)S(1)} %get-tuple-element.115), channel_id=1, source_target_pairs={{0,16},{8,24},{16,0},{24,8},{1,17},{9,25},{17,1},{25,9},{2,18},{10... | collective-permute-start | bytes 1572872 | tf_op jit(solution)/shard_map/ppermute | solution.py:465
  67.3 18.0 %collective-permute-start.23 = (bf16[4,64,1280]{2,1,0:T(8,128)(2,1)S(1)}, bf16[4,64,1280]{2,1,0:T(8,128)(2,1)}, u32[]{:S(2)}, u32[]{:S(2)}) collective-permute-start(bf16[4,64,1280]{2,1,0:T(8,128)(2,1)S(1)} %get-tuple-element.97), channel_id=1, source_target_pairs={{0,1},{1,0},{2,3},{3,2},{4,5},{5,4},{6,7},{7,6},{8,9},{9,8},{10,11... | collective-permute-start | bytes 1966088 | tf_op jit(solution)/shard_map/ppermute | solution.py:465
  76.5 8.8 %collective-permute-start.24 = (bf16[2,256,512]{2,1,0:T(8,128)(2,1)}, bf16[2,256,512]{2,1,0:T(8,128)(2,1)}, u32[]{:S(2)}, u32[]{:S(2)}) collective-permute-start(bf16[2,256,512]{2,1,0:T(8,128)(2,1)} %get-tuple-element.99), channel_id=1, source_target_pairs={{0,8},{8,0},{16,24},{24,16},{1,9},{9,1},{17,25},{25,17},{2,10},{10... | collective-permute-start | bytes 1572872 | tf_op jit(solution)/shard_map/ppermute | solution.py:465
  76.5 25.5 %all-to-all-start = ((bf16[8,80,384]{2,1,0:T(8,128)(2,1)}), bf16[8,80,384]{2,1,0:T(8,128)(2,1)}, u32[]{:S(2)}, u32[]{:S(2)}) async-start(bf16[8,80,384]{2,1,0:T(8,128)(2,1)} %get-tuple-element.100), calls=%async_computation | async-start | bytes 983040 | tf_op jit(solution)/shard_map/all_to_all | solution.py:663
  82.0 12.8 %collective-permute-start.36 = (bf16[4,64,512]{2,1,0:T(8,128)(2,1)S(1)}, bf16[4,64,512]{2,1,0:T(8,128)(2,1)S(1)}, u32[]{:S(2)}, u32[]{:S(2)}) collective-permute-start(bf16[4,64,512]{2,1,0:T(8,128)(2,1)S(1)} %get-tuple-element.134), channel_id=1, source_target_pairs={{0,1},{1,0},{2,3},{3,2},{4,5},{5,4},{6,7},{7,6},{8,9},{9,8},{10,11... | collective-permute-start | bytes 786440 | tf_op jit(solution)/shard_map/ppermute | solution.py:465
  86.3 8.4 %collective-permute-start.25 = (bf16[256,512]{1,0:T(8,128)(2,1)S(1)}, bf16[256,512]{1,0:T(8,128)(2,1)S(1)}, u32[]{:S(2)}, u32[]{:S(2)}) collective-permute-start(bf16[256,512]{1,0:T(8,128)(2,1)S(1)} %fusion.2), channel_id=1, source_target_pairs={{0,16},{8,24},{16,0},{24,8},{1,17},{9,25},{17,1},{25,9},{2,18},{10... | collective-permute-start | bytes 786440 | tf_op jit(solution)/shard_map/ppermute | solution.py:465
  89.0 12.0 %collective-permute-start.26 = (bf16[2,64,1280]{2,1,0:T(8,128)(2,1)S(1)}, bf16[2,64,1280]{2,1,0:T(8,128)(2,1)S(1)}, u32[]{:S(2)}, u32[]{:S(2)}) collective-permute-start(bf16[2,64,1280]{2,1,0:T(8,128)(2,1)S(1)} %get-tuple-element.130), channel_id=1, source_target_pairs={{0,2},{1,3},{2,0},{3,1},{4,6},{5,7},{6,4},{7,5},{8,10},{9,11},{10,... | collective-permute-start | bytes 983048 | tf_op jit(solution)/shard_map/ppermute | solution.py:465
  94.8 9.5 %collective-permute-start.37 = (bf16[2,64,512]{2,1,0:T(8,128)(2,1)S(1)}, bf16[2,64,512]{2,1,0:T(8,128)(2,1)S(1)}, u32[]{:S(2)}, u32[]{:S(2)}) collective-permute-start(bf16[2,64,512]{2,1,0:T(8,128)(2,1)S(1)} %get-tuple-element.132), channel_id=1, source_target_pairs={{0,2},{1,3},{2,0},{3,1},{4,6},{5,7},{6,4},{7,5},{8,10},{9,11},{10,... | collective-permute-start | bytes 393224 | tf_op jit(solution)/shard_map/ppermute | solution.py:465
  101.1 9.3 %collective-permute-start.30 = (bf16[64,1280]{1,0:T(8,128)(2,1)S(1)}, bf16[64,1280]{1,0:T(8,128)(2,1)S(1)}, u32[]{:S(2)}, u32[]{:S(2)}) collective-permute-start(bf16[64,1280]{1,0:T(8,128)(2,1)S(1)} %fusion.3), channel_id=1, source_target_pairs={{0,4},{1,5},{2,6},{3,7},{4,0},{5,1},{6,2},{7,3},{8,12},{9,13},{10,... | collective-permute-start | bytes 491528 | tf_op jit(solution)/shard_map/ppermute | solution.py:465
  103.1 10.6 %collective-permute-start.28 = (bf16[80,384]{1,0:T(8,128)(2,1)S(1)}, bf16[80,384]{1,0:T(8,128)(2,1)S(1)}, u32[]{:S(2)}, u32[]{:S(2)}) collective-permute-start(bf16[80,384]{1,0:T(8,128)(2,1)S(1)} %reduce_sum.12.a), channel_id=1, source_target_pairs={{0,16},{8,24},{16,0},{24,8},{1,17},{9,25},{17,1},{25,9},{2,18},{10... | collective-permute-start | bytes 184328 | tf_op jit(solution)/shard_map/ppermute | solution.py:465
  104.3 8.7 %collective-permute-start.38 = (bf16[64,512]{1,0:T(8,128)(2,1)S(1)}, bf16[64,512]{1,0:T(8,128)(2,1)S(1)}, u32[]{:S(2)}, u32[]{:S(2)}) collective-permute-start(bf16[64,512]{1,0:T(8,128)(2,1)S(1)} %fusion.5), channel_id=1, source_target_pairs={{0,4},{1,5},{2,6},{3,7},{4,0},{5,1},{6,2},{7,3},{8,12},{9,13},{10,... | collective-permute-start | bytes 196616 | tf_op jit(solution)/shard_map/ppermute | solution.py:465
  110.4 5.9 %collective-permute-start.32 = (bf16[64,1280]{1,0:T(8,128)(2,1)S(1)}, bf16[64,1280]{1,0:T(8,128)(2,1)S(1)}, u32[]{:S(2)}, u32[]{:S(2)}) collective-permute-start(bf16[64,1280]{1,0:T(8,128)(2,1)S(1)} %fusion.1.a), channel_id=1, source_target_pairs={{0,16},{8,24},{16,0},{24,8},{1,17},{9,25},{17,1},{25,9},{2,18},{10... | collective-permute-start | bytes 491528 | tf_op jit(solution)/shard_map/ppermute | solution.py:465
  113.1 4.3 %collective-permute-start.40 = (bf16[64,512]{1,0:T(8,128)(2,1)S(1)}, bf16[64,512]{1,0:T(8,128)(2,1)S(1)}, u32[]{:S(2)}, u32[]{:S(2)}) collective-permute-start(bf16[64,512]{1,0:T(8,128)(2,1)S(1)} %fusion.4.refs_0_), channel_id=1, source_target_pairs={{0,16},{8,24},{16,0},{24,8},{1,17},{9,25},{17,1},{25,9},{2,18},{10... | collective-permute-start | bytes 196616 | tf_op jit(solution)/shard_map/ppermute | solution.py:465
  113.7 3.7 %collective-permute-start.29 = (bf16[80,384]{1,0:T(8,128)(2,1)S(1)}, bf16[80,384]{1,0:T(8,128)(2,1)S(1)}, u32[]{:S(2)}, u32[]{:S(2)}) collective-permute-start(bf16[80,384]{1,0:T(8,128)(2,1)S(1)} %collective-permute-done.28.c), channel_id=1, source_target_pairs={{0,8},{8,0},{16,24},{24,16},{1,9},{9,1},{17,25},{25,17},{2,10},{10... | collective-permute-start | bytes 184328 | tf_op jit(solution)/shard_map/ppermute | solution.py:465
  114.2 4.6 %collective-permute-start.31 = (bf16[64,1280]{1,0:T(8,128)(2,1)S(1)}, bf16[64,1280]{1,0:T(8,128)(2,1)S(1)}, u32[]{:S(2)}, u32[]{:S(2)}) collective-permute-start(bf16[64,1280]{1,0:T(8,128)(2,1)S(1)} %fusion.1.a), channel_id=1, source_target_pairs={{0,8},{8,0},{16,24},{24,16},{1,9},{9,1},{17,25},{25,17},{2,10},{10... | collective-permute-start | bytes 491528 | tf_op jit(solution)/shard_map/ppermute | solution.py:465
  (16 other events, 101.0 us)
